TPU v7x, 128 devices: a whole 4x4x4 slice. The times are simulated.
128 devices in a mesh: gx: 8 (over x_hi, y), gy: 4 (over x_lo, core), gz: 4 (over z).
Axes of the slice: x: 4 (x_hi: 2, x_lo: 2; x = x_hi * 2 + x_lo), y: 4, z: 4, core: 2. Of those that a mesh axis runs over, the one named last changes fastest.
Arguments:
- state: float32 [2, 8, 16, 64, 9, 512], P(None, 'gx', 'gy', 'gz'), may hold values from -6 to 6
- deriv: bfloat16 [512, 1536], replicated, may hold values from -0.25 to 0.25
- lift: bfloat16 [384, 512], replicated, may hold values from -0.3125 to 0.3125
- material: float32 [3, 8, 16, 64], P(None, 'gx', 'gy', 'gz'), may hold values from 0.5 to 2
- stored: float32 [8, 16, 64, 9, 384], P('gx', 'gy', 'gz'), may hold values from -6 to 6
- orient: int32 [8, 16, 64, 6], P('gx', 'gy', 'gz'), may hold values from 0 to 7, as said below
- flags: int32 [8, 16, 64, 6], P('gx', 'gy', 'gz'), may hold values 0 or 1
Outputs:
- advanced: float32 [2, 8, 16, 64, 9, 512], P(None, 'gx', 'gy', 'gz')
- kernel: float32 [8, 16, 64, 9], P('gx', 'gy', 'gz')
Inputs may be any that keep to these rules, and one draw needn't show every extreme that they name: `orient`: codes of the lower face (even s) of an element are the inverse symmetry of the code on the matching upper face of the element before it along that direction, taken cyclically over the whole grid.
All inputs are finite; a program needn't handle non-finite values. No bound on the sum of `flags` on one device may be relied on, other than what follows from the above.
Results may differ from a plain program's by a relative error of at most 0.0013.
Values sent between devices are 32-bit elements; how exact they have to be, the bound alone decides.
No kernel may reach another device: no remote copies, remote signals or barrier semaphores. Data moves between devices by JAX's collectives and lax.ppermute only.
A program may use at most 192 MiB of HBM per device.

v0:
```python
import jax
import jax.numpy as jnp
import numpy as np
from functools import partial
from jax import lax
from jax.experimental import pallas as pl
from jax.experimental.pallas import tpu as pltpu
from jax.sharding import PartitionSpec as P

NP = 8
FACE = NP * NP
LANES = 128
step_size = 0.15
stress_slot = ((3, 8, 7), (8, 4, 6), (7, 6, 5))
shear_pairs = ((6, 1, 2), (7, 0, 2), (8, 0, 1))
LIMIT = 56 * 1024 * 1024


def trace_table():
    table = np.zeros((NP**3, 4 * FACE), np.float32)
    for first in range(NP):
        for second in range(NP):
            m = first * NP + second
            table[first * 64 + second, m] = 1.0
            table[first * 64 + 56 + second, FACE + m] = 1.0
            table[first * 64 + second * 8, 2 * FACE + m] = 1.0
            table[first * 64 + second * 8 + 7, 3 * FACE + m] = 1.0
    return table


def lane_index(shape):
    return lax.broadcasted_iota(jnp.int32, shape, len(shape) - 1)


def merged(forward, adjoint, upper):
    rows = forward.shape[:-1]
    flat = (-1, LANES)
    turned = pltpu.roll(adjoint.reshape(flat), FACE, 1)
    own = (lane_index(turned.shape) >= FACE) == upper
    return jnp.where(own, forward.reshape(flat), turned).reshape(rows + (LANES,))


def pack_kernel(parity_ref, low_ref, high_ref, far_ref, near_ref):
    low = merged(low_ref[0, 0], low_ref[1, 0], False)
    high = merged(high_ref[0, 0], high_ref[1, 0], True)
    odd = parity_ref[0] == 1
    far_ref[0] = jnp.where(odd, high, low)
    near_ref[0] = jnp.where(odd, low, high)


def pack_faces(parity, state):
    _, count_y, fields, count_z, nodes = state.shape
    tiles = nodes // LANES
    block = (2, 1, fields, count_z, LANES)
    message = jax.ShapeDtypeStruct((count_y, fields, count_z, LANES), jnp.float32)
    out_spec = pl.BlockSpec((1, fields, count_z, LANES), lambda y, p: (y, 0, 0, 0))
    return pl.pallas_call(
        pack_kernel,
        out_shape=(message, message),
        grid_spec=pltpu.PrefetchScalarGridSpec(
            num_scalar_prefetch=1,
            grid=(count_y,),
            in_specs=[
                pl.BlockSpec(block, lambda y, p: (0, y, 0, 0, 0)),
                pl.BlockSpec(block, lambda y, p: (0, y, 0, 0, tiles - 1)),
            ],
            out_specs=(out_spec, out_spec),
        ),
        cost_estimate=pl.CostEstimate(flops=10**6, bytes_accessed=2 * 10**6, transcendentals=0),
        name="pack_faces",
    )(parity, state, state)


def trace_kernel(parity_ref, state_ref, table_ref, trace_ref, y_two, y_one, z_two, z_one):
    y = pl.program_id(0)
    _, _, fields, count_z, nodes = state_ref.shape
    table = table_ref[...]
    for s in range(2):
        values = state_ref[s, 0].reshape(fields * count_z, nodes)
        high = values.astype(jnp.bfloat16)
        low = (values - high.astype(jnp.float32)).astype(jnp.bfloat16)
        picked = jnp.dot(high, table, preferred_element_type=jnp.float32)
        picked = picked + jnp.dot(low, table, preferred_element_type=jnp.float32)
        trace_ref[s, 0] = picked.reshape(fields, count_z, 2 * LANES)
    odd_y = parity_ref[1] == 1
    odd_z = parity_ref[2] == 1

    @pl.when(y == 0)
    def _():
        down = merged(trace_ref[0, 0, :, :, :LANES], trace_ref[1, 0, :, :, :LANES], False)

        @pl.when(odd_y)
        def _():
            y_one[...] = down

        @pl.when(jnp.logical_not(odd_y))
        def _():
            y_two[...] = down

    @pl.when(y == pl.num_programs(0) - 1)
    def _():
        up = merged(trace_ref[0, 0, :, :, :LANES], trace_ref[1, 0, :, :, :LANES], True)

        @pl.when(odd_y)
        def _():
            y_two[...] = up

        @pl.when(jnp.logical_not(odd_y))
        def _():
            y_one[...] = up

    first = merged(trace_ref[0, 0, :, 0, LANES:], trace_ref[1, 0, :, 0, LANES:], False)
    last = merged(
        trace_ref[0, 0, :, count_z - 1, LANES:], trace_ref[1, 0, :, count_z - 1, LANES:], True
    )
    z_two[y] = jnp.where(odd_z, last, first)
    z_one[y] = jnp.where(odd_z, first, last)


def extract_traces(parity, state, table):
    _, count_y, fields, count_z, nodes = state.shape
    f32 = jnp.float32
    y_message = jax.ShapeDtypeStruct((fields, count_z, LANES), f32)
    z_message = jax.ShapeDtypeStruct((count_y, fields, LANES), f32)
    y_spec = pl.BlockSpec(y_message.shape, lambda y, p: (0, 0, 0))
    z_spec = pl.BlockSpec(z_message.shape, lambda y, p: (0, 0, 0))
    return pl.pallas_call(
        trace_kernel,
        out_shape=(
            jax.ShapeDtypeStruct((2, count_y, fields, count_z, 2 * LANES), f32),
            y_message,
            y_message,
            z_message,
            z_message,
        ),
        grid_spec=pltpu.PrefetchScalarGridSpec(
            num_scalar_prefetch=1,
            grid=(count_y,),
            in_specs=[
                pl.BlockSpec((2, 1, fields, count_z, nodes), lambda y, p: (0, y, 0, 0, 0)),
                pl.BlockSpec(table.shape, lambda y, p: (0, 0)),
            ],
            out_specs=(
                pl.BlockSpec((2, 1, fields, count_z, 2 * LANES), lambda y, p: (0, y, 0, 0, 0)),
                y_spec,
                y_spec,
                z_spec,
                z_spec,
            ),
        ),
        cost_estimate=pl.CostEstimate(flops=6 * 10**8, bytes_accessed=4 * 10**6, transcendentals=0),
        name="extract_traces",
    )(parity, state, table)


def spread(columns, rows, pick):
    return lax.dot_general(
        columns,
        pick,
        (((0,), (0,)), ((), ())),
        precision=lax.Precision.HIGHEST,
        preferred_element_type=jnp.float32,
    )


def volume_kernel(
    ends_ref, state_ref, d0_ref, d1_ref, d2_ref, material_ref, orient_ref, flags_ref,
    partial_ref, coef_ref, source_ref, edge_ref,
    low_ref, grad_ref, div_ref, wide_ref,
):
    step = pl.program_id(0)
    _, count_y, fields, count_z, _ = state_ref.shape
    rows = 2 * count_y * count_z
    width = partial_ref.shape[-1]

    @pl.when(step == 0)
    def _():
        for f in range(fields):
            low_ref[f] = state_ref[:, :, f].reshape(rows, -1).astype(jnp.bfloat16)
        lanes = lane_index((3 * count_y, 3 * count_y * LANES))
        row = lax.broadcasted_iota(jnp.int32, lanes.shape, 0)
        pick = (lanes // LANES == row).astype(jnp.float32)
        medium = spread(material_ref[...].reshape(3 * count_y, count_z), 3 * count_y, pick)
        lanes = lane_index((6 * count_y, 3 * count_y * LANES))
        row = lax.broadcasted_iota(jnp.int32, lanes.shape, 0)
        block = lanes // LANES
        face = 2 * (block // count_y) + (lanes % LANES) // FACE
        pick = (face * count_y + block % count_y == row).astype(jnp.float32)
        codes = spread(
            orient_ref[...].reshape(6 * count_y, count_z).astype(jnp.float32), 6 * count_y, pick
        )
        kinds = spread(
            flags_ref[...].reshape(6 * count_y, count_z).astype(jnp.float32), 6 * count_y, pick
        )
        lane = lane_index((count_z, LANES))
        upper = lane >= FACE
        half_sign = jnp.where(upper, 0.5, -0.5)
        node = lane % FACE
        near, far = (node // NP, node % NP)
        z_pos = lax.broadcasted_iota(jnp.int32, lane.shape, 0)
        for y in range(count_y):
            lam = medium[:, y * LANES : (y + 1) * LANES]
            mu = medium[:, (count_y + y) * LANES : (count_y + y + 1) * LANES]
            rho = medium[:, (2 * count_y + y) * LANES : (2 * count_y + y + 1) * LANES]
            inv = 1.0 / rho
            wide_ref[0, y] = lam
            wide_ref[1, y] = mu
            wide_ref[2, y] = inv
            coef_ref[0, y] = half_sign * lam
            coef_ref[1, y] = half_sign * mu
            coef_ref[2, y] = half_sign * inv
            coef_ref[3, y] = 0.5 * jnp.sqrt((lam + 2.0 * mu) * inv)
            for d in range(3):
                at = (d * count_y + y) * LANES
                code = jnp.round(codes[:, at : at + LANES]).astype(jnp.int32)
                swap = code >= 4
                lead = jnp.where(swap, far, near)
                trail = jnp.where(swap, near, far)
                lead = jnp.where(code % 2 == 1, NP - 1 - lead, lead)
                trail = jnp.where((code // 2) % 2 == 1, NP - 1 - trail, trail)
                source_ref[d, y] = lead * NP + trail + jnp.where(upper, 0, FACE)
                if d > 0:
                    free = jnp.where(jnp.round(kinds[:, at : at + LANES]) == 1.0, 1.0, 0.0)
                    if d == 1:
                        low_end = (ends_ref[0] == 1) if y == 0 else False
                        high_end = (ends_ref[1] == 1) if y == count_y - 1 else False
                        rim = jnp.where(
                            upper,
                            jnp.where(high_end, 1.0, 0.0),
                            jnp.where(low_end, 1.0, 0.0),
                        )
                    else:
                        low_rim = jnp.where(z_pos == 0, jnp.where(ends_ref[2] == 1, 1.0, 0.0), 0.0)
                        high_rim = jnp.where(
                            z_pos == count_z - 1, jnp.where(ends_ref[3] == 1, 1.0, 0.0), 0.0
                        )
                        rim = jnp.where(upper, high_rim, low_rim)
                    edge_ref[d - 1, 0, y] = rim
                    edge_ref[d - 1, 1, y] = free

    derivs = (d0_ref, d1_ref, d2_ref)
    velocity = jnp.concatenate([low_ref[i] for i in range(3)], axis=0)
    for d in range(3):
        grad_ref[d] = jnp.dot(
            velocity, derivs[d][...], preferred_element_type=jnp.float32
        )
    total = None
    for d in range(3):
        stress = jnp.concatenate([low_ref[stress_slot[i][d]] for i in range(3)], axis=0)
        part = jnp.dot(stress, derivs[d][...], preferred_element_type=jnp.float32)
        total = part if total is None else total + part
    div_ref[...] = total
    base = pl.multiple_of(step * width, LANES)
    for s in range(2):
        scale = step_size if s == 0 else -step_size
        for y in range(count_y):
            at = (s * count_y + y) * count_z
            for tile in range(width // LANES):
                columns = slice(tile * LANES, (tile + 1) * LANES)
                lam = scale * wide_ref[0, y]
                mu = scale * wide_ref[1, y]
                inv = scale * wide_ref[2, y]

                def g(d, i):
                    return grad_ref[d, i * rows + at : i * rows + at + count_z, columns]

                def put(f, term):
                    old = state_ref[s, y, f, :, pl.ds(base + tile * LANES, LANES)]
                    partial_ref[s, y, f, :, columns] = old + term

                for i in range(3):
                    put(i, inv * div_ref[i * rows + at : i * rows + at + count_z, columns])
                diag = [g(i, i) for i in range(3)]
                common = lam * (diag[0] + diag[1] + diag[2])
                for i in range(3):
                    put(3 + i, common + (mu + mu) * diag[i])
                for f, i, j in shear_pairs:
                    put(f, mu * (g(j, i) + g(i, j)))


def volume(ends, state, deriv, material, orient, flags):
    _, count_y, fields, count_z, nodes = state.shape
    f32 = jnp.float32
    width = 256
    parts = nodes // width
    rows = 2 * count_y * count_z
    whole = lambda shape: pl.BlockSpec(shape, lambda n, e: (0,) * len(shape))
    deriv_spec = lambda d: pl.BlockSpec((nodes, width), lambda n, e: (0, d * parts + n))
    outs = (
        jax.ShapeDtypeStruct(state.shape, f32),
        jax.ShapeDtypeStruct((4, count_y, count_z, LANES), f32),
        jax.ShapeDtypeStruct((3, count_y, count_z, LANES), jnp.int32),
        jax.ShapeDtypeStruct((2, 2, count_y, count_z, LANES), f32),
    )
    return pl.pallas_call(
        volume_kernel,
        out_shape=outs,
        grid_spec=pltpu.PrefetchScalarGridSpec(
            num_scalar_prefetch=1,
            grid=(parts,),
            in_specs=[
                whole(state.shape),
                deriv_spec(0),
                deriv_spec(1),
                deriv_spec(2),
                whole(material.shape),
                whole(orient.shape),
                whole(flags.shape),
            ],
            out_specs=(
                pl.BlockSpec(
                    (2, count_y, fields, count_z, width), lambda n, e: (0, 0, 0, 0, n)
                ),
                whole(outs[1].shape),
                whole(outs[2].shape),
                whole(outs[3].shape),
            ),
            scratch_shapes=[
                pltpu.VMEM((fields, rows, nodes), jnp.bfloat16),
                pltpu.VMEM((3, 3 * rows, width), f32),
                pltpu.VMEM((3 * rows, width), f32),
                pltpu.VMEM((3, count_y, count_z, LANES), f32),
            ],
        ),
        compiler_params=pltpu.CompilerParams(vmem_limit_bytes=LIMIT),
        cost_estimate=pl.CostEstimate(
            flops=12 * 10**8 * 3, bytes_accessed=8 * 10**6, transcendentals=0
        ),
        name="volume",
    )(ends, state, deriv, deriv, deriv, material, orient, flags)


def final_kernel(
    parity_ref, low_x_ref, high_x_ref, trace_ref, far_ref, near_ref, y_two, y_one, z_two, z_one,
    coef_ref, source_ref, edge_ref, partial_ref, stored_ref, lift_ref,
    advanced_ref, kernel_ref,
    flux_ref, sum_ref,
):
    y = pl.program_id(0)
    last_y = pl.num_programs(0) - 1
    fields, count_z = (partial_ref.shape[2], partial_ref.shape[3])
    odd_x = parity_ref[0] == 1
    odd_y = parity_ref[1] == 1
    odd_z = parity_ref[2] == 1
    lane = lane_index((count_z, LANES))
    upper = lane >= FACE
    z_pos = lax.broadcasted_iota(jnp.int32, lane.shape, 0)
    lam, mu, inv, speed = [coef_ref[k, 0] for k in range(4)]
    below = jnp.maximum(y - 1, 0)
    above = jnp.minimum(y + 1, last_y)
    take_near = upper == odd_x
    for s in range(2):
        for d in range(3):
            source = source_ref[d, 0]
            if d == 0 and s == 1:
                source = (source + FACE) % LANES
            if d > 0:
                rim = edge_ref[d - 1, 0, 0] > 0.0
                free = edge_ref[d - 1, 1, 0]
                keep_velocity = free - 1.0
                keep_stress = -free - 1.0
            jumps = []
            for f in range(fields):
                if d == 0:
                    inside = jnp.where(upper, high_x_ref[s, 0, f], low_x_ref[s, 0, f])
                    near, far = (near_ref[0, f], far_ref[0, f])
                    mixed = jnp.where(take_near, near, far) if s == 0 else jnp.where(take_near, far, near)
                elif d == 1:
                    inside = trace_ref[s, y, f, :, :LANES]
                    two, one = (y_two[f], y_one[f])
                    from_below = jnp.where(odd_y, one, two)
                    from_above = jnp.where(odd_y, two, one)
                    if s == 1:
                        from_below = pltpu.roll(from_below, FACE, 1)
                        from_above = pltpu.roll(from_above, FACE, 1)
                    lower = jnp.where(y == 0, from_below, trace_ref[s, below, f, :, :LANES])
                    higher = jnp.where(y == last_y, from_above, trace_ref[s, above, f, :, :LANES])
                    mixed = jnp.where(upper, lower, higher)
                else:
                    inside = trace_ref[s, y, f, :, LANES:]
                    two = jnp.broadcast_to(z_two[0, f : f + 1, :], lane.shape)
                    one = jnp.broadcast_to(z_one[0, f : f + 1, :], lane.shape)
                    from_below = jnp.where(odd_z, one, two)
                    from_above = jnp.where(odd_z, two, one)
                    if s == 1:
                        from_below = pltpu.roll(from_below, FACE, 1)
                        from_above = pltpu.roll(from_above, FACE, 1)
                    lower = jnp.where(z_pos == 0, from_below, pltpu.roll(inside, 1, 0))
                    higher = jnp.where(
                        z_pos == count_z - 1, from_above, pltpu.roll(inside, count_z - 1, 0)
                    )
                    mixed = jnp.where(upper, lower, higher)
                turned = jnp.take_along_axis(mixed, source, axis=1)
                jump = turned - inside
                if d > 0:
                    keep = keep_velocity if f < 3 else keep_stress
                    jump = jnp.where(rim, inside * keep, jump)
                jumps.append(jump)
                if s == 1:
                    term = stored_ref[0, f, :, d * LANES : (d + 1) * LANES] * jump
                    if d == 0:
                        sum_ref[f] = term
                    else:
                        sum_ref[f] += term
            flux = [speed * jump for jump in jumps]
            for i in range(3):
                flux[i] = flux[i] + inv * jumps[stress_slot[i][d]]
            common = lam * jumps[d]
            for i in range(3):
                flux[3 + i] = flux[3 + i] + common
            for i, j, f in ((0, 0, 3), (1, 1, 4), (2, 2, 5), (1, 2, 6), (0, 2, 7), (0, 1, 8)):
                if j == d:
                    flux[f] = flux[f] + mu * jumps[i]
                if i == d:
                    flux[f] = flux[f] + mu * jumps[j]
            for f in range(fields):
                flux_ref[s, f, :, d * LANES : (d + 1) * LANES] = flux[f].astype(jnp.bfloat16)
        lifted = jnp.dot(
            flux_ref[s].reshape(fields * count_z, 3 * LANES),
            lift_ref[...],
            preferred_element_type=jnp.float32,
        ).reshape(fields, count_z, -1)
        scale = step_size if s == 0 else -step_size
        advanced_ref[s, 0] = partial_ref[s, 0] + scale * lifted
    row = lax.broadcasted_iota(jnp.int32, (8, LANES), 0)
    ones = jnp.where(row == y, 1.0 / FACE, 0.0)
    for f in range(fields):
        sums = lax.dot_general(
            ones,
            sum_ref[f],
            (((1,), (1,)), ((), ())),
            precision=lax.Precision.HIGHEST,
            preferred_element_type=jnp.float32,
        )[: kernel_ref.shape[1]]

        @pl.when(y == 0)
        def _():
            kernel_ref[f] = sums

        @pl.when(y > 0)
        def _():
            kernel_ref[f] += sums


def finish(
    parity, state, traces, far, near, y_two, y_one, z_two, z_one, coef, source, edge, part, stored, lift
):
    _, count_y, fields, count_z, nodes = state.shape
    tiles = nodes // LANES
    f32 = jnp.float32
    whole = lambda a: pl.BlockSpec(a.shape, lambda y, p: (0,) * a.ndim)
    outs = (
        jax.ShapeDtypeStruct(state.shape, f32),
        jax.ShapeDtypeStruct((fields, count_y, count_z), f32),
    )
    by_y = lambda lead, rest: pl.BlockSpec(
        lead + (1,) + rest, lambda y, p: (0,) * len(lead) + (y,) + (0,) * len(rest)
    )
    return pl.pallas_call(
        final_kernel,
        out_shape=outs,
        grid_spec=pltpu.PrefetchScalarGridSpec(
            num_scalar_prefetch=1,
            grid=(count_y,),
            in_specs=[
                pl.BlockSpec((2, 1, fields, count_z, LANES), lambda y, p: (0, y, 0, 0, 0)),
                pl.BlockSpec((2, 1, fields, count_z, LANES), lambda y, p: (0, y, 0, 0, tiles - 1)),
                whole(traces),
                by_y((), (fields, count_z, LANES)),
                by_y((), (fields, count_z, LANES)),
                whole(y_two),
                whole(y_one),
                by_y((), (fields, LANES)),
                by_y((), (fields, LANES)),
                by_y((4,), (count_z, LANES)),
                by_y((3,), (count_z, LANES)),
                by_y((2, 2), (count_z, LANES)),
                by_y((2,), (fields, count_z, nodes)),
                by_y((), (fields, count_z, 3 * LANES)),
                whole(lift),
            ],
            out_specs=(
                by_y((2,), (fields, count_z, nodes)),
                pl.BlockSpec(outs[1].shape, lambda y, p: (0, 0, 0)),
            ),
            scratch_shapes=[
                pltpu.VMEM((2, fields, count_z, 3 * LANES), jnp.bfloat16),
                pltpu.VMEM((fields, count_z, LANES), f32),
            ],
        ),
        compiler_params=pltpu.CompilerParams(vmem_limit_bytes=LIMIT),
        cost_estimate=pl.CostEstimate(flops=9 * 10**8, bytes_accessed=10**7, transcendentals=0),
        name="finish",
    )(parity, state, state, traces, far, near, y_two, y_one, z_two, z_one, coef, source, edge, part, stored, lift)


def swaps(count, start, wrap):
    pairs = []
    for i in range(start, count if wrap else count - 1, 2):
        j = (i + 1) % count
        pairs += [(i, j), (j, i)]
    return pairs


def local(state, deriv, lift, material, stored, orient, flags):
    view = jnp.transpose(state[:, 0], (0, 1, 3, 2, 4))
    stored_view = jnp.transpose(stored[0], (0, 2, 1, 3))
    orient_view = jnp.transpose(orient[0], (2, 0, 1))
    flags_view = jnp.transpose(flags[0], (2, 0, 1))
    ix, iy, iz = (lax.axis_index(a) for a in ("gx", "gy", "gz"))
    nx, ny, nz = (lax.axis_size(a) for a in ("gx", "gy", "gz"))
    parity = jnp.stack([ix % 2, iy % 2, iz % 2]).astype(jnp.int32)
    ends = jnp.stack([iy == 0, iy == ny - 1, iz == 0, iz == nz - 1]).astype(jnp.int32)
    far, near = pack_faces(parity, view)
    far_in = lax.ppermute(far, "gx", swaps(nx, 1, True))
    near_in = lax.ppermute(near, "gx", swaps(nx, 0, True))
    table = jnp.asarray(trace_table(), jnp.bfloat16)
    traces, y_two, y_one, z_two, z_one = extract_traces(parity, view, table)
    y_two = lax.ppermute(y_two, "gy", swaps(ny, 1, False))
    y_one = lax.ppermute(y_one, "gy", swaps(ny, 0, False))
    z_two = lax.ppermute(z_two, "gz", swaps(nz, 1, False))
    z_one = lax.ppermute(z_one, "gz", swaps(nz, 0, False))
    part, coef, source, edge = volume(ends, view, deriv, material[:, 0], orient_view, flags_view)
    advanced, kernel = finish(
        parity, view, traces, far_in, near_in, y_two, y_one, z_two, z_one, coef, source, edge, part,
        stored_view, lift,
    )
    return (
        jnp.transpose(advanced, (0, 1, 3, 2, 4))[:, None],
        jnp.transpose(kernel, (1, 2, 0))[None],
    )


def solution(mesh):
    placed = (
        P(None, "gx", "gy", "gz", None, None),
        P(),
        P(),
        P(None, "gx", "gy", "gz"),
        P("gx", "gy", "gz", None, None),
        P("gx", "gy", "gz", None),
        P("gx", "gy", "gz", None),
    )
    return jax.shard_map(
        local,
        mesh=mesh,
        in_specs=placed,
        out_specs=(P(None, "gx", "gy", "gz", None, None), P("gx", "gy", "gz", None)),
        check_vma=False,
    )
```

profile of v0, /device:TPU:1, one launch (start us, length us, event | category | flops | bytes accessed | tf_op | source)
XLA Modules:
  0.0 44.2 jit_solution(5464702827246962946)
XLA Ops:
  0.7 0.6 %pad_add_fusion.parity_ref = s32[3]{0:T(128)} fusion(s32[1]{0:T(128)} %bitcast.2, s32[1]{0:T(128)} %bitcast.1, s32[1]{0:T(128)} %bitcast), kind=kLoop, calls=%fused_computation.1 | loop fusion | flops 6 | bytes 24 | tf_op jit(solution)/shard_map/stack | solution.py:512
  1.2 4.2 %pack_faces.1 = (f32[4,9,16,128]{3,2,1,0:T(8,128)}, f32[4,9,16,128]{3,2,1,0:T(8,128)}) custom-call(s32[3]{0:T(128)} %pad_add_fusion.parity_ref, f32[2,4,9,16,512]{4,3,2,1,0:T(8,128)} %bitcast.28, f32[2,4,9,16,512]{4,3,2,1,0:T(8,128)} %bitcast.29), custom_call_target="tpu_custom_call" | custom-call | flops 1000000 | bytes 2000000 | tf_op jit(solution)/shard_map/pack_faces/pallas_call | solution.py:57
  5.5 6.0 %collective-permute-start = (f32[4,9,16,128]{3,2,1,0:T(8,128)}, f32[4,9,16,128]{3,2,1,0:T(8,128)S(1)}, u32[]{:S(2)}, u32[]{:S(2)}) collective-permute-start(f32[4,9,16,128]{3,2,1,0:T(8,128)} %get-tuple-element.16), channel_id=1, source_target_pairs={{16,32},{32,16},{48,64},{64,48},{80,96},{96,80},{112,0},{0,112},{1... | collective-permute-start | bytes 884744 | tf_op jit(solution)/shard_map/ppermute | solution.py:515
  11.5 0.0 collective-permute-start.1
  11.5 5.4 %extract_traces.1 = (f32[2,4,9,16,256]{4,3,2,1,0:T(8,128)}, f32[9,16,128]{2,1,0:T(8,128)}, f32[9,16,128]{2,1,0:T(8,128)}, f32[4,9,128]{2,1,0:T(8,128)}, f32[4,9,128]{2,1,0:T(8,128)}) custom-call(s32[3]{0:T(128)} %pad_add_fusion.parity_ref, f32[2,4,9,16,512]{4,3,2,1,0:T(8,128)} %bitcast.30, bf16[512,256]{1,0:T(8,128)(2,1)} %constant.39.clone.table_ref), custom_call_target="tpu_custom_call" | custom-call | flops 600000000 | bytes 4000000 | tf_op jit(solution)/shard_map/extract_traces/pallas_call | solution.py:127
  16.9 0.7 %collective-permute-start.4 = (f32[4,9,128]{2,1,0:T(8,128)}, f32[4,9,128]{2,1,0:T(8,128)S(1)}, u32[]{:S(2)}, u32[]{:S(2)}) collective-permute-start(f32[4,9,128]{2,1,0:T(8,128)} %get-tuple-element.20), channel_id=1, source_target_pairs={{1,2},{2,1},{5,6},{6,5},{9,10},{10,9},{13,14},{14,13},{17,18},{18,... | collective-permute-start | bytes 55304 | tf_op jit(solution)/shard_map/ppermute | solution.py:521
  17.6 4.6 %collective-permute-start.5 = (f32[4,9,128]{2,1,0:T(8,128)}, f32[4,9,128]{2,1,0:T(8,128)S(1)}, u32[]{:S(2)}, u32[]{:S(2)}) collective-permute-start(f32[4,9,128]{2,1,0:T(8,128)} %get-tuple-element.21), channel_id=1, source_target_pairs={{0,1},{1,0},{2,3},{3,2},{4,5},{5,4},{6,7},{7,6},{8,9},{9,8},{10,11... | collective-permute-start | bytes 55304 | tf_op jit(solution)/shard_map/ppermute | solution.py:522
  22.2 3.6 %collective-permute-start.2 = (f32[9,16,128]{2,1,0:T(8,128)}, f32[9,16,128]{2,1,0:T(8,128)S(1)}, u32[]{:S(2)}, u32[]{:S(2)}) collective-permute-start(f32[9,16,128]{2,1,0:T(8,128)} %get-tuple-element.18), channel_id=1, source_target_pairs={{4,8},{8,4},{5,9},{9,5},{6,10},{10,6},{7,11},{11,7},{20,24},{24,20... | collective-permute-start | bytes 221192 | tf_op jit(solution)/shard_map/ppermute | solution.py:519
  25.8 0.6 %add_convert_fusion.ends_ref = s32[4]{0:T(128)} fusion(pred[1]{0:T(512)(128)(4,1)} %bitcast.9, pred[1]{0:T(512)(128)(4,1)} %bitcast.8, pred[1]{0:T(512)(128)(4,1)} %bitcast.7, pred[1]{0:T(512)(128)(4,1)} %bitcast.6), kind=kLoop, calls=%fused_computation | loop fusion | flops 16 | bytes 20 | tf_op jit(solution)/shard_map/convert_element_type | solution.py:513
  26.4 0.0 collective-permute-done.4.z_two
  26.4 0.0 copy-start.4
  26.4 0.0 collective-permute-start.3
  26.4 6.2 %volume.1 = (f32[2,4,9,16,512]{4,3,2,1,0:T(8,128)}, f32[4,4,16,128]{3,2,1,0:T(8,128)}, s32[3,4,16,128]{3,2,1,0:T(8,128)}, f32[2,2,4,16,128]{4,3,2,1,0:T(8,128)}) custom-call(s32[4]{0:T(128)} %add_convert_fusion.ends_ref, f32[2,4,9,16,512]{4,3,2,1,0:T(8,128)} %bitcast.31, bf16[512,1536]{1,0:T(8,128)(2,1)} %d2_ref.1, bf16[512,1536]{1,0:T(8,128)(2,1)} %d2_ref.1, ...), custom_call_target="tpu_custom_call" | custom-call | flops 3600000000 | bytes 8000000 | tf_op jit(solution)/shard_map/volume/pallas_call | solution.py:295
  32.7 0.0 copy-done.4
  32.7 0.0 collective-permute-done.5.z_one
  32.7 0.0 copy-start.5
  32.7 0.0 collective-permute-done.2.y_two
  32.7 0.0 copy-start.2
  32.7 0.0 collective-permute-done.3.y_one
  32.7 0.0 copy-start.3
  32.7 0.0 collective-permute-done.far_ref
  32.7 0.0 copy-start
  32.8 0.0 collective-permute-done.1.near_ref
  32.8 0.0 copy-start.1
  32.8 0.5 %copy-done.5 = f32[4,9,128]{2,1,0:T(8,128)} copy-done((f32[4,9,128]{2,1,0:T(8,128)}, f32[4,9,128]{2,1,0:T(8,128)S(1)}, u32[]{:S(2)}) %copy-start.5) | copy-done | bytes 18456
  33.3 0.0 copy-done.2
  33.3 0.0 copy-done.3
  33.4 0.1 copy-done
  33.5 0.1 copy-done.1
  33.6 10.7 %finish.1 = (f32[2,4,9,16,512]{4,3,2,1,0:T(8,128)}, f32[9,4,16]{2,1,0:T(4,128)}) custom-call(s32[3]{0:T(128)} %pad_add_fusion.parity_ref, f32[2,4,9,16,512]{4,3,2,1,0:T(8,128)} %bitcast.32, f32[2,4,9,16,512]{4,3,2,1,0:T(8,128)} %bitcast.33, f32[2,4,9,16,256]{4,3,2,1,0:T(8,128)} %get-tuple-element.15.trace_ref, f32[4,9,16,128]{3,2,1,0:T(8,128)} %copy-done, ...), custom_call_target="tpu_custom_call" | custom-call | flops 900000000 | bytes 10000000 | tf_op jit(solution)/shard_map/finish/pallas_call | solution.py:459
Async XLA Ops:
  5.5 27.3 %collective-permute-start = (f32[4,9,16,128]{3,2,1,0:T(8,128)}, f32[4,9,16,128]{3,2,1,0:T(8,128)S(1)}, u32[]{:S(2)}, u32[]{:S(2)}) collective-permute-start(f32[4,9,16,128]{3,2,1,0:T(8,128)} %get-tuple-element.16), channel_id=1, source_target_pairs={{16,32},{32,16},{48,64},{64,48},{80,96},{96,80},{112,0},{0,112},{1... | collective-permute-start | bytes 884744 | tf_op jit(solution)/shard_map/ppermute | solution.py:515
  11.5 21.3 %collective-permute-start.1 = (f32[4,9,16,128]{3,2,1,0:T(8,128)}, f32[4,9,16,128]{3,2,1,0:T(8,128)S(1)}, u32[]{:S(2)}, u32[]{:S(2)}) collective-permute-start(f32[4,9,16,128]{3,2,1,0:T(8,128)} %get-tuple-element.17), channel_id=1, source_target_pairs={{0,16},{16,0},{32,48},{48,32},{64,80},{80,64},{96,112},{112,96},{1... | collective-permute-start | bytes 884744 | tf_op jit(solution)/shard_map/ppermute | solution.py:516
  16.9 9.5 %collective-permute-start.4 = (f32[4,9,128]{2,1,0:T(8,128)}, f32[4,9,128]{2,1,0:T(8,128)S(1)}, u32[]{:S(2)}, u32[]{:S(2)}) collective-permute-start(f32[4,9,128]{2,1,0:T(8,128)} %get-tuple-element.20), channel_id=1, source_target_pairs={{1,2},{2,1},{5,6},{6,5},{9,10},{10,9},{13,14},{14,13},{17,18},{18,... | collective-permute-start | bytes 55304 | tf_op jit(solution)/shard_map/ppermute | solution.py:521
  17.6 15.1 %collective-permute-start.5 = (f32[4,9,128]{2,1,0:T(8,128)}, f32[4,9,128]{2,1,0:T(8,128)S(1)}, u32[]{:S(2)}, u32[]{:S(2)}) collective-permute-start(f32[4,9,128]{2,1,0:T(8,128)} %get-tuple-element.21), channel_id=1, source_target_pairs={{0,1},{1,0},{2,3},{3,2},{4,5},{5,4},{6,7},{7,6},{8,9},{9,8},{10,11... | collective-permute-start | bytes 55304 | tf_op jit(solution)/shard_map/ppermute | solution.py:522
  22.2 10.5 %collective-permute-start.2 = (f32[9,16,128]{2,1,0:T(8,128)}, f32[9,16,128]{2,1,0:T(8,128)S(1)}, u32[]{:S(2)}, u32[]{:S(2)}) collective-permute-start(f32[9,16,128]{2,1,0:T(8,128)} %get-tuple-element.18), channel_id=1, source_target_pairs={{4,8},{8,4},{5,9},{9,5},{6,10},{10,6},{7,11},{11,7},{20,24},{24,20... | collective-permute-start | bytes 221192 | tf_op jit(solution)/shard_map/ppermute | solution.py:519
  26.4 6.3 %copy-start.4 = (f32[4,9,128]{2,1,0:T(8,128)}, f32[4,9,128]{2,1,0:T(8,128)S(1)}, u32[]{:S(2)}) copy-start(f32[4,9,128]{2,1,0:T(8,128)S(1)} %collective-permute-done.4.z_two) | copy-start | bytes 55300
  26.4 6.3 %collective-permute-start.3 = (f32[9,16,128]{2,1,0:T(8,128)}, f32[9,16,128]{2,1,0:T(8,128)S(1)}, u32[]{:S(2)}, u32[]{:S(2)}) collective-permute-start(f32[9,16,128]{2,1,0:T(8,128)} %get-tuple-element.19), channel_id=1, source_target_pairs={{0,4},{4,0},{8,12},{12,8},{1,5},{5,1},{9,13},{13,9},{2,6},{6,2},{1... | collective-permute-start | bytes 221192 | tf_op jit(solution)/shard_map/ppermute | solution.py:520
  32.7 0.6 %copy-start.5 = (f32[4,9,128]{2,1,0:T(8,128)}, f32[4,9,128]{2,1,0:T(8,128)S(1)}, u32[]{:S(2)}) copy-start(f32[4,9,128]{2,1,0:T(8,128)S(1)} %collective-permute-done.5.z_one) | copy-start | bytes 55300
  32.7 0.6 %copy-start.2 = (f32[9,16,128]{2,1,0:T(8,128)}, f32[9,16,128]{2,1,0:T(8,128)S(1)}, u32[]{:S(2)}) copy-start(f32[9,16,128]{2,1,0:T(8,128)S(1)} %collective-permute-done.2.y_two) | copy-start | bytes 221188
  32.7 0.6 %copy-start.3 = (f32[9,16,128]{2,1,0:T(8,128)}, f32[9,16,128]{2,1,0:T(8,128)S(1)}, u32[]{:S(2)}) copy-start(f32[9,16,128]{2,1,0:T(8,128)S(1)} %collective-permute-done.3.y_one) | copy-start | bytes 221188
  32.7 0.7 %copy-start = (f32[4,9,16,128]{3,2,1,0:T(8,128)}, f32[4,9,16,128]{3,2,1,0:T(8,128)S(1)}, u32[]{:S(2)}) copy-start(f32[4,9,16,128]{3,2,1,0:T(8,128)S(1)} %collective-permute-done.far_ref) | copy-start | bytes 884740
  32.8 0.8 %copy-start.1 = (f32[4,9,16,128]{3,2,1,0:T(8,128)}, f32[4,9,16,128]{3,2,1,0:T(8,128)S(1)}, u32[]{:S(2)}) copy-start(f32[4,9,16,128]{3,2,1,0:T(8,128)S(1)} %collective-permute-done.1.near_ref) | copy-start | bytes 884740
where the time goes:
time: 44.6 us; the launch traced here: 44.2 us
  Pallas kernels  26.5 us (59%)
  starting transfers between devices  14.9 us (33%)
  other arithmetic  1.21 us (3%)
  local copies, waits for them, and re-layouts  0.81 us (2%)
  between operations  0.77 us (2%)
    pallas_call x1, Pallas kernels, finish(): pl.pallas_call(final_kernel, out_shape=outs, grid_spec=pltpu.PrefetchScal...  10.7 us
    pallas_call x1, Pallas kernels, volume(): pl.pallas_call(volume_kernel, out_shape=outs, grid_spec=pltpu.PrefetchSca...  6.24 us
    ppermute x1, starting transfers between devices, local(): far_in = lax.ppermute(far, 'gx', swaps(nx, 1, True))  6.02 us
    pallas_call x1, Pallas kernels, extract_traces(): pl.pallas_call(trace_kernel, out_shape=(jax.ShapeDtypeStruct((2, count_y,...  5.41 us
    ppermute x1, starting transfers between devices, local(): z_one = lax.ppermute(z_one, 'gz', swaps(nz, 0, False))  4.6 us
    pallas_call x1, Pallas kernels, pack_faces(): pl.pallas_call(pack_kernel, out_shape=(message, message), grid_spec=pltpu...  4.21 us
    ppermute x1, starting transfers between devices, local(): y_two = lax.ppermute(y_two, 'gy', swaps(ny, 1, False))  3.61 us
  transfers between devices with their start and end apart: 6, of which 0 were waited for; matrix products, arithmetic and copies ran while one was open for 1% of the time, Pallas kernels for 26%

commit v1 on v0

--- a/solution.py
+++ b/solution.py
@@ -13,7 +13,7 @@
 step_size = 0.15
 stress_slot = ((3, 8, 7), (8, 4, 6), (7, 6, 5))
 shear_pairs = ((6, 1, 2), (7, 0, 2), (8, 0, 1))
-LIMIT = 56 * 1024 * 1024
+LIMIT = 20 * 1024 * 1024
 
 
 def trace_table():
@@ -40,117 +40,39 @@
     return jnp.where(own, forward.reshape(flat), turned).reshape(rows + (LANES,))
 
 
-def pack_kernel(parity_ref, low_ref, high_ref, far_ref, near_ref):
-    low = merged(low_ref[0, 0], low_ref[1, 0], False)
-    high = merged(high_ref[0, 0], high_ref[1, 0], True)
-    odd = parity_ref[0] == 1
-    far_ref[0] = jnp.where(odd, high, low)
-    near_ref[0] = jnp.where(odd, low, high)
-
-
-def pack_faces(parity, state):
+def odd_position(axis):
+    return lax.axis_index(axis) % 2 == 1
+
+
+def pack_kernel(low_ref, high_ref, far_ref, near_ref):
+    odd = odd_position("gx")
+    for y in range(far_ref.shape[0]):
+        low = merged(low_ref[0, y], low_ref[1, y], False)
+        high = merged(high_ref[0, y], high_ref[1, y], True)
+        far_ref[y] = jnp.where(odd, high, low)
+        near_ref[y] = jnp.where(odd, low, high)
+
+
+def pack_faces(state):
     _, count_y, fields, count_z, nodes = state.shape
     tiles = nodes // LANES
-    block = (2, 1, fields, count_z, LANES)
+    part = count_y // 2
+    block = (2, part, fields, count_z, LANES)
     message = jax.ShapeDtypeStruct((count_y, fields, count_z, LANES), jnp.float32)
-    out_spec = pl.BlockSpec((1, fields, count_z, LANES), lambda y, p: (y, 0, 0, 0))
+    out_spec = pl.BlockSpec((part, fields, count_z, LANES), lambda y: (y, 0, 0, 0))
     return pl.pallas_call(
         pack_kernel,
         out_shape=(message, message),
-        grid_spec=pltpu.PrefetchScalarGridSpec(
-            num_scalar_prefetch=1,
-            grid=(count_y,),
-            in_specs=[
-                pl.BlockSpec(block, lambda y, p: (0, y, 0, 0, 0)),
-                pl.BlockSpec(block, lambda y, p: (0, y, 0, 0, tiles - 1)),
-            ],
-            out_specs=(out_spec, out_spec),
-        ),
+        grid=(2,),
+        in_specs=[
+            pl.BlockSpec(block, lambda y: (0, y, 0, 0, 0)),
+            pl.BlockSpec(block, lambda y: (0, y, 0, 0, tiles - 1)),
+        ],
+        out_specs=(out_spec, out_spec),
+        compiler_params=pltpu.CompilerParams(vmem_limit_bytes=LIMIT),
         cost_estimate=pl.CostEstimate(flops=10**6, bytes_accessed=2 * 10**6, transcendentals=0),
         name="pack_faces",
-    )(parity, state, state)
-
-
-def trace_kernel(parity_ref, state_ref, table_ref, trace_ref, y_two, y_one, z_two, z_one):
-    y = pl.program_id(0)
-    _, _, fields, count_z, nodes = state_ref.shape
-    table = table_ref[...]
-    for s in range(2):
-        values = state_ref[s, 0].reshape(fields * count_z, nodes)
-        high = values.astype(jnp.bfloat16)
-        low = (values - high.astype(jnp.float32)).astype(jnp.bfloat16)
-        picked = jnp.dot(high, table, preferred_element_type=jnp.float32)
-        picked = picked + jnp.dot(low, table, preferred_element_type=jnp.float32)
-        trace_ref[s, 0] = picked.reshape(fields, count_z, 2 * LANES)
-    odd_y = parity_ref[1] == 1
-    odd_z = parity_ref[2] == 1
-
-    @pl.when(y == 0)
-    def _():
-        down = merged(trace_ref[0, 0, :, :, :LANES], trace_ref[1, 0, :, :, :LANES], False)
-
-        @pl.when(odd_y)
-        def _():
-            y_one[...] = down
-
-        @pl.when(jnp.logical_not(odd_y))
-        def _():
-            y_two[...] = down
-
-    @pl.when(y == pl.num_programs(0) - 1)
-    def _():
-        up = merged(trace_ref[0, 0, :, :, :LANES], trace_ref[1, 0, :, :, :LANES], True)
-
-        @pl.when(odd_y)
-        def _():
-            y_two[...] = up
-
-        @pl.when(jnp.logical_not(odd_y))
-        def _():
-            y_one[...] = up
-
-    first = merged(trace_ref[0, 0, :, 0, LANES:], trace_ref[1, 0, :, 0, LANES:], False)
-    last = merged(
-        trace_ref[0, 0, :, count_z - 1, LANES:], trace_ref[1, 0, :, count_z - 1, LANES:], True
-    )
-    z_two[y] = jnp.where(odd_z, last, first)
-    z_one[y] = jnp.where(odd_z, first, last)
-
-
-def extract_traces(parity, state, table):
-    _, count_y, fields, count_z, nodes = state.shape
-    f32 = jnp.float32
-    y_message = jax.ShapeDtypeStruct((fields, count_z, LANES), f32)
-    z_message = jax.ShapeDtypeStruct((count_y, fields, LANES), f32)
-    y_spec = pl.BlockSpec(y_message.shape, lambda y, p: (0, 0, 0))
-    z_spec = pl.BlockSpec(z_message.shape, lambda y, p: (0, 0, 0))
-    return pl.pallas_call(
-        trace_kernel,
-        out_shape=(
-            jax.ShapeDtypeStruct((2, count_y, fields, count_z, 2 * LANES), f32),
-            y_message,
-            y_message,
-            z_message,
-            z_message,
-        ),
-        grid_spec=pltpu.PrefetchScalarGridSpec(
-            num_scalar_prefetch=1,
-            grid=(count_y,),
-            in_specs=[
-                pl.BlockSpec((2, 1, fields, count_z, nodes), lambda y, p: (0, y, 0, 0, 0)),
-                pl.BlockSpec(table.shape, lambda y, p: (0, 0)),
-            ],
-            out_specs=(
-                pl.BlockSpec((2, 1, fields, count_z, 2 * LANES), lambda y, p: (0, y, 0, 0, 0)),
-                y_spec,
-                y_spec,
-                z_spec,
-                z_spec,
-            ),
-        ),
-        cost_estimate=pl.CostEstimate(flops=6 * 10**8, bytes_accessed=4 * 10**6, transcendentals=0),
-        name="extract_traces",
-    )(parity, state, table)
+    )(state, state)
 
 
 def spread(columns, rows, pick):
@@ -164,14 +86,45 @@
 
 
 def volume_kernel(
-    ends_ref, state_ref, d0_ref, d1_ref, d2_ref, material_ref, orient_ref, flags_ref,
-    partial_ref, coef_ref, source_ref, edge_ref,
+    state_ref, d0_ref, d1_ref, d2_ref, material_ref, orient_ref, flags_ref, table_ref,
+    partial_ref, coef_ref, source_ref, edge_ref, trace_ref, y_two, y_one, z_two, z_one,
     low_ref, grad_ref, div_ref, wide_ref,
 ):
     step = pl.program_id(0)
     _, count_y, fields, count_z, _ = state_ref.shape
     rows = 2 * count_y * count_z
     width = partial_ref.shape[-1]
+    ends = [
+        lax.axis_index("gy") == 0,
+        lax.axis_index("gy") == lax.axis_size("gy") - 1,
+        lax.axis_index("gz") == 0,
+        lax.axis_index("gz") == lax.axis_size("gz") - 1,
+    ]
+
+    values = state_ref[step].reshape(count_y * fields * count_z, -1)
+    high = values.astype(jnp.bfloat16)
+    low = (values - high.astype(jnp.float32)).astype(jnp.bfloat16)
+    table = table_ref[...]
+    picked = jnp.dot(high, table, preferred_element_type=jnp.float32)
+    picked = picked + jnp.dot(low, table, preferred_element_type=jnp.float32)
+    trace_ref[step] = picked.reshape(count_y, fields, count_z, 2 * LANES)
+
+    @pl.when(step == 1)
+    def _():
+        odd_y = odd_position("gy")
+        odd_z = odd_position("gz")
+        end = count_y - 1
+        down = merged(trace_ref[0, 0, :, :, :LANES], trace_ref[1, 0, :, :, :LANES], False)
+        up = merged(trace_ref[0, end, :, :, :LANES], trace_ref[1, end, :, :, :LANES], True)
+        y_two[...] = jnp.where(odd_y, up, down)
+        y_one[...] = jnp.where(odd_y, down, up)
+        for y in range(count_y):
+            first = merged(trace_ref[0, y, :, 0, LANES:], trace_ref[1, y, :, 0, LANES:], False)
+            last = merged(
+                trace_ref[0, y, :, count_z - 1, LANES:], trace_ref[1, y, :, count_z - 1, LANES:], True
+            )
+            z_two[y] = jnp.where(odd_z, last, first)
+            z_one[y] = jnp.where(odd_z, first, last)
 
     @pl.when(step == 0)
     def _():
@@ -222,17 +175,17 @@
                 if d > 0:
                     free = jnp.where(jnp.round(kinds[:, at : at + LANES]) == 1.0, 1.0, 0.0)
                     if d == 1:
-                        low_end = (ends_ref[0] == 1) if y == 0 else False
-                        high_end = (ends_ref[1] == 1) if y == count_y - 1 else False
+                        low_end = (ends[0]) if y == 0 else False
+                        high_end = (ends[1]) if y == count_y - 1 else False
                         rim = jnp.where(
                             upper,
                             jnp.where(high_end, 1.0, 0.0),
                             jnp.where(low_end, 1.0, 0.0),
                         )
                     else:
-                        low_rim = jnp.where(z_pos == 0, jnp.where(ends_ref[2] == 1, 1.0, 0.0), 0.0)
+                        low_rim = jnp.where(z_pos == 0, jnp.where(ends[2], 1.0, 0.0), 0.0)
                         high_rim = jnp.where(
-                            z_pos == count_z - 1, jnp.where(ends_ref[3] == 1, 1.0, 0.0), 0.0
+                            z_pos == count_z - 1, jnp.where(ends[3], 1.0, 0.0), 0.0
                         )
                         rim = jnp.where(upper, high_rim, low_rim)
                     edge_ref[d - 1, 0, y] = rim
@@ -278,60 +231,61 @@
                     put(f, mu * (g(j, i) + g(i, j)))
 
 
-def volume(ends, state, deriv, material, orient, flags):
+def volume(state, deriv, material, orient, flags, table):
     _, count_y, fields, count_z, nodes = state.shape
     f32 = jnp.float32
-    width = 256
-    parts = nodes // width
+    parts = 2
+    width = nodes // parts
     rows = 2 * count_y * count_z
-    whole = lambda shape: pl.BlockSpec(shape, lambda n, e: (0,) * len(shape))
-    deriv_spec = lambda d: pl.BlockSpec((nodes, width), lambda n, e: (0, d * parts + n))
+    whole = lambda shape: pl.BlockSpec(shape, lambda n: (0,) * len(shape))
+    deriv_spec = lambda d: pl.BlockSpec((nodes, width), lambda n: (0, d * parts + n))
+    y_message = jax.ShapeDtypeStruct((fields, count_z, LANES), f32)
+    z_message = jax.ShapeDtypeStruct((count_y, fields, LANES), f32)
     outs = (
         jax.ShapeDtypeStruct(state.shape, f32),
         jax.ShapeDtypeStruct((4, count_y, count_z, LANES), f32),
         jax.ShapeDtypeStruct((3, count_y, count_z, LANES), jnp.int32),
         jax.ShapeDtypeStruct((2, 2, count_y, count_z, LANES), f32),
+        jax.ShapeDtypeStruct((2, count_y, fields, count_z, 2 * LANES), f32),
+        y_message,
+        y_message,
+        z_message,
+        z_message,
     )
     return pl.pallas_call(
         volume_kernel,
         out_shape=outs,
-        grid_spec=pltpu.PrefetchScalarGridSpec(
-            num_scalar_prefetch=1,
-            grid=(parts,),
-            in_specs=[
-                whole(state.shape),
-                deriv_spec(0),
-                deriv_spec(1),
-                deriv_spec(2),
-                whole(material.shape),
-                whole(orient.shape),
-                whole(flags.shape),
-            ],
-            out_specs=(
-                pl.BlockSpec(
-                    (2, count_y, fields, count_z, width), lambda n, e: (0, 0, 0, 0, n)
-                ),
-                whole(outs[1].shape),
-                whole(outs[2].shape),
-                whole(outs[3].shape),
-            ),
-            scratch_shapes=[
-                pltpu.VMEM((fields, rows, nodes), jnp.bfloat16),
-                pltpu.VMEM((3, 3 * rows, width), f32),
-                pltpu.VMEM((3 * rows, width), f32),
-                pltpu.VMEM((3, count_y, count_z, LANES), f32),
-            ],
-        ),
+        grid=(parts,),
+        in_specs=[
+            whole(state.shape),
+            deriv_spec(0),
+            deriv_spec(1),
+            deriv_spec(2),
+            whole(material.shape),
+            whole(orient.shape),
+            whole(flags.shape),
+            whole(table.shape),
+        ],
+        out_specs=(
+            pl.BlockSpec((2, count_y, fields, count_z, width), lambda n: (0, 0, 0, 0, n)),
+        )
+        + tuple(whole(out.shape) for out in outs[1:]),
+        scratch_shapes=[
+            pltpu.VMEM((fields, rows, nodes), jnp.bfloat16),
+            pltpu.VMEM((3, 3 * rows, width), f32),
+            pltpu.VMEM((3 * rows, width), f32),
+            pltpu.VMEM((3, count_y, count_z, LANES), f32),
+        ],
         compiler_params=pltpu.CompilerParams(vmem_limit_bytes=LIMIT),
         cost_estimate=pl.CostEstimate(
-            flops=12 * 10**8 * 3, bytes_accessed=8 * 10**6, transcendentals=0
+            flops=42 * 10**8, bytes_accessed=12 * 10**6, transcendentals=0
         ),
         name="volume",
-    )(ends, state, deriv, deriv, deriv, material, orient, flags)
+    )(state, deriv, deriv, deriv, material, orient, flags, table)
 
 
 def final_kernel(
-    parity_ref, low_x_ref, high_x_ref, trace_ref, far_ref, near_ref, y_two, y_one, z_two, z_one,
+    low_x_ref, high_x_ref, trace_ref, far_ref, near_ref, y_two, y_one, z_two, z_one,
     coef_ref, source_ref, edge_ref, partial_ref, stored_ref, lift_ref,
     advanced_ref, kernel_ref,
     flux_ref, sum_ref,
@@ -339,9 +293,9 @@
     y = pl.program_id(0)
     last_y = pl.num_programs(0) - 1
     fields, count_z = (partial_ref.shape[2], partial_ref.shape[3])
-    odd_x = parity_ref[0] == 1
-    odd_y = parity_ref[1] == 1
-    odd_z = parity_ref[2] == 1
+    odd_x = odd_position("gx")
+    odd_y = odd_position("gy")
+    odd_z = odd_position("gz")
     lane = lane_index((count_z, LANES))
     upper = lane >= FACE
     z_pos = lax.broadcasted_iota(jnp.int32, lane.shape, 0)
@@ -422,76 +376,59 @@
         ).reshape(fields, count_z, -1)
         scale = step_size if s == 0 else -step_size
         advanced_ref[s, 0] = partial_ref[s, 0] + scale * lifted
-    row = lax.broadcasted_iota(jnp.int32, (8, LANES), 0)
-    ones = jnp.where(row == y, 1.0 / FACE, 0.0)
     for f in range(fields):
-        sums = lax.dot_general(
-            ones,
-            sum_ref[f],
-            (((1,), (1,)), ((), ())),
-            precision=lax.Precision.HIGHEST,
-            preferred_element_type=jnp.float32,
-        )[: kernel_ref.shape[1]]
-
-        @pl.when(y == 0)
-        def _():
-            kernel_ref[f] = sums
-
-        @pl.when(y > 0)
-        def _():
-            kernel_ref[f] += sums
+        sums = jnp.sum(sum_ref[f], axis=1, keepdims=True) * (1.0 / FACE)
+        across = jnp.sum(jnp.where(z_pos == lane, sums, 0.0), axis=0, keepdims=True)
+        kernel_ref[f, pl.ds(y, 1), :] = across[:, :count_z]
 
 
 def finish(
-    parity, state, traces, far, near, y_two, y_one, z_two, z_one, coef, source, edge, part, stored, lift
+    state, traces, far, near, y_two, y_one, z_two, z_one, coef, source, edge, part, stored, lift
 ):
     _, count_y, fields, count_z, nodes = state.shape
     tiles = nodes // LANES
     f32 = jnp.float32
-    whole = lambda a: pl.BlockSpec(a.shape, lambda y, p: (0,) * a.ndim)
+    whole = lambda a: pl.BlockSpec(a.shape, lambda y: (0,) * a.ndim)
     outs = (
         jax.ShapeDtypeStruct(state.shape, f32),
         jax.ShapeDtypeStruct((fields, count_y, count_z), f32),
     )
     by_y = lambda lead, rest: pl.BlockSpec(
-        lead + (1,) + rest, lambda y, p: (0,) * len(lead) + (y,) + (0,) * len(rest)
+        lead + (1,) + rest, lambda y: (0,) * len(lead) + (y,) + (0,) * len(rest)
     )
     return pl.pallas_call(
         final_kernel,
         out_shape=outs,
-        grid_spec=pltpu.PrefetchScalarGridSpec(
-            num_scalar_prefetch=1,
-            grid=(count_y,),
-            in_specs=[
-                pl.BlockSpec((2, 1, fields, count_z, LANES), lambda y, p: (0, y, 0, 0, 0)),
-                pl.BlockSpec((2, 1, fields, count_z, LANES), lambda y, p: (0, y, 0, 0, tiles - 1)),
-                whole(traces),
-                by_y((), (fields, count_z, LANES)),
-                by_y((), (fields, count_z, LANES)),
-                whole(y_two),
-                whole(y_one),
-                by_y((), (fields, LANES)),
-                by_y((), (fields, LANES)),
-                by_y((4,), (count_z, LANES)),
-                by_y((3,), (count_z, LANES)),
-                by_y((2, 2), (count_z, LANES)),
-                by_y((2,), (fields, count_z, nodes)),
-                by_y((), (fields, count_z, 3 * LANES)),
-                whole(lift),
-            ],
-            out_specs=(
-                by_y((2,), (fields, count_z, nodes)),
-                pl.BlockSpec(outs[1].shape, lambda y, p: (0, 0, 0)),
-            ),
-            scratch_shapes=[
-                pltpu.VMEM((2, fields, count_z, 3 * LANES), jnp.bfloat16),
-                pltpu.VMEM((fields, count_z, LANES), f32),
-            ],
+        grid=(count_y,),
+        in_specs=[
+            pl.BlockSpec((2, 1, fields, count_z, LANES), lambda y: (0, y, 0, 0, 0)),
+            pl.BlockSpec((2, 1, fields, count_z, LANES), lambda y: (0, y, 0, 0, tiles - 1)),
+            whole(traces),
+            by_y((), (fields, count_z, LANES)),
+            by_y((), (fields, count_z, LANES)),
+            whole(y_two),
+            whole(y_one),
+            by_y((), (fields, LANES)),
+            by_y((), (fields, LANES)),
+            by_y((4,), (count_z, LANES)),
+            by_y((3,), (count_z, LANES)),
+            by_y((2, 2), (count_z, LANES)),
+            by_y((2,), (fields, count_z, nodes)),
+            by_y((), (fields, count_z, 3 * LANES)),
+            whole(lift),
+        ],
+        out_specs=(
+            by_y((2,), (fields, count_z, nodes)),
+            pl.BlockSpec(outs[1].shape, lambda y: (0, 0, 0)),
         ),
+        scratch_shapes=[
+            pltpu.VMEM((2, fields, count_z, 3 * LANES), jnp.bfloat16),
+            pltpu.VMEM((fields, count_z, LANES), f32),
+        ],
         compiler_params=pltpu.CompilerParams(vmem_limit_bytes=LIMIT),
         cost_estimate=pl.CostEstimate(flops=9 * 10**8, bytes_accessed=10**7, transcendentals=0),
         name="finish",
-    )(parity, state, state, traces, far, near, y_two, y_one, z_two, z_one, coef, source, edge, part, stored, lift)
+    )(state, state, traces, far, near, y_two, y_one, z_two, z_one, coef, source, edge, part, stored, lift)
 
 
 def swaps(count, start, wrap):
@@ -507,22 +444,20 @@
     stored_view = jnp.transpose(stored[0], (0, 2, 1, 3))
     orient_view = jnp.transpose(orient[0], (2, 0, 1))
     flags_view = jnp.transpose(flags[0], (2, 0, 1))
-    ix, iy, iz = (lax.axis_index(a) for a in ("gx", "gy", "gz"))
     nx, ny, nz = (lax.axis_size(a) for a in ("gx", "gy", "gz"))
-    parity = jnp.stack([ix % 2, iy % 2, iz % 2]).astype(jnp.int32)
-    ends = jnp.stack([iy == 0, iy == ny - 1, iz == 0, iz == nz - 1]).astype(jnp.int32)
-    far, near = pack_faces(parity, view)
+    far, near = pack_faces(view)
     far_in = lax.ppermute(far, "gx", swaps(nx, 1, True))
     near_in = lax.ppermute(near, "gx", swaps(nx, 0, True))
     table = jnp.asarray(trace_table(), jnp.bfloat16)
-    traces, y_two, y_one, z_two, z_one = extract_traces(parity, view, table)
+    part, coef, source, edge, traces, y_two, y_one, z_two, z_one = volume(
+        view, deriv, material[:, 0], orient_view, flags_view, table
+    )
     y_two = lax.ppermute(y_two, "gy", swaps(ny, 1, False))
     y_one = lax.ppermute(y_one, "gy", swaps(ny, 0, False))
     z_two = lax.ppermute(z_two, "gz", swaps(nz, 1, False))
     z_one = lax.ppermute(z_one, "gz", swaps(nz, 0, False))
-    part, coef, source, edge = volume(ends, view, deriv, material[:, 0], orient_view, flags_view)
     advanced, kernel = finish(
-        parity, view, traces, far_in, near_in, y_two, y_one, z_two, z_one, coef, source, edge, part,
+        view, traces, far_in, near_in, y_two, y_one, z_two, z_one, coef, source, edge, part,
         stored_view, lift,
     )
     return (

time: 44.6 us -> 29.4 us (0.66)
  the two profiles are of different devices: /device:TPU:1 before, /device:TPU:72 now
where the time goes in v1:
time: 29.4 us; the launch traced here: 29.2 us
  starting transfers between devices  10.7 us (36%)
  Pallas kernels  8.33 us (28%)
  waiting for transfers between devices  7.71 us (26%)
  local copies, waits for them, and re-layouts  1.69 us (6%)
  between operations  0.74 us (3%)
    ppermute x1, starting transfers between devices, local(): near_in = lax.ppermute(near, 'gx', swaps(nx, 0, True))  4.35 us
    pallas_call x1, Pallas kernels, finish(): pl.pallas_call(final_kernel, out_shape=outs, grid=(count_y,), in_specs=[p...  4.03 us
    ppermute x1, waiting for transfers between devices, local(): z_one = lax.ppermute(z_one, 'gz', swaps(nz, 0, False))  3.91 us
    pallas_call x1, Pallas kernels, volume(): pl.pallas_call(volume_kernel, out_shape=outs, grid=(parts,), in_specs=[wh...  3.8 us
    ppermute x1, waiting for transfers between devices, local(): z_two = lax.ppermute(z_two, 'gz', swaps(nz, 1, False))  3.79 us
    ppermute x1, starting transfers between devices, local(): y_one = lax.ppermute(y_one, 'gy', swaps(ny, 0, False))  2.04 us
    ppermute x1, starting transfers between devices, local(): z_two = lax.ppermute(z_two, 'gz', swaps(nz, 1, False))  2 us
    unnamed x16, local copies, waits for them, and re-layouts  1.69 us
  transfers between devices with their start and end apart: 6, of which 2 were waited for; matrix products, arithmetic and copies ran while one was open for 0% of the time, Pallas kernels for 13%

profile of v1, /device:TPU:72, one launch (start us, length us, event | category | flops | bytes accessed | tf_op | source)
XLA Modules:
  0.0 29.2 jit_solution(14851272072184947254)
XLA Ops:
  0.6 0.0 copy-start
  0.6 1.7 %copy-done = f32[2,1,4,16,9,512]{5,3,4,2,1,0:T(8,128)S(1)} copy-done((f32[2,1,4,16,9,512]{5,3,4,2,1,0:T(8,128)S(1)}, f32[2,1,4,16,9,512]{5,3,4,2,1,0:T(8,128)}, u32[]{:S(2)}) %copy-start) | copy-done | bytes 2359320
  2.3 0.0 copy-start.3
  2.3 0.0 copy-start.4
  2.3 0.0 copy-start.5
  2.3 0.0 copy-start.6
  2.3 0.0 copy-start.7
  2.3 0.5 %pack_faces.1 = (f32[4,9,16,128]{3,2,1,0:T(8,128)S(1)}, f32[4,9,16,128]{3,2,1,0:T(8,128)S(1)}) custom-call(f32[2,4,9,16,512]{4,3,2,1,0:T(8,128)S(1)} %bitcast.21, f32[2,4,9,16,512]{4,3,2,1,0:T(8,128)S(1)} %bitcast.22), custom_call_target="tpu_custom_call" | custom-call | flops 1000000 | bytes 2000000 | tf_op jit(solution)/shard_map/pack_faces/pallas_call | solution.py:63
  2.8 1.7 %collective-permute-start = (f32[4,9,16,128]{3,2,1,0:T(8,128)S(1)}, f32[4,9,16,128]{3,2,1,0:T(8,128)S(1)}, u32[]{:S(2)}, u32[]{:S(2)}) collective-permute-start(f32[4,9,16,128]{3,2,1,0:T(8,128)S(1)} %get-tuple-element.16), channel_id=1, source_target_pairs={{16,32},{32,16},{48,64},{64,48},{80,96},{96,80},{112,0},{0,112},{1... | collective-permute-start | bytes 884744 | tf_op jit(solution)/shard_map/ppermute | solution.py:449
  4.5 4.3 %collective-permute-start.1 = (f32[4,9,16,128]{3,2,1,0:T(8,128)S(1)}, f32[4,9,16,128]{3,2,1,0:T(8,128)S(1)}, u32[]{:S(2)}, u32[]{:S(2)}) collective-permute-start(f32[4,9,16,128]{3,2,1,0:T(8,128)S(1)} %get-tuple-element.17), channel_id=1, source_target_pairs={{0,16},{16,0},{32,48},{48,32},{64,80},{80,64},{96,112},{112,96},{1... | collective-permute-start | bytes 884744 | tf_op jit(solution)/shard_map/ppermute | solution.py:450
  8.8 0.0 copy-done.3
  8.8 0.0 copy-done.4
  8.8 0.0 copy-done.5
  8.8 0.0 copy-done.6
  8.8 0.0 copy-done.7
  8.9 0.0 copy-start.1
  8.9 0.0 copy-start.2
  8.9 3.8 %volume.1 = (f32[2,4,9,16,512]{4,3,2,1,0:T(8,128)S(1)}, f32[4,4,16,128]{3,2,1,0:T(8,128)S(1)}, s32[3,4,16,128]{3,2,1,0:T(8,128)S(1)}, f32[2,2,4,16,128]{4,3,2,1,...) custom-call(f32[2,4,9,16,512]{4,3,2,1,0:T(8,128)S(1)} %bitcast.23, ...), custom_call_target="tpu_custom_call" | custom-call | flops 4200000000 | bytes 12000000 | tf_op jit(solution)/shard_map/volume/pallas_call | solution.py:255
  12.7 0.7 %collective-permute-start.2 = (f32[9,16,128]{2,1,0:T(8,128)S(1)}, f32[9,16,128]{2,1,0:T(8,128)S(1)}, u32[]{:S(2)}, u32[]{:S(2)}) collective-permute-start(f32[9,16,128]{2,1,0:T(8,128)S(1)} %get-tuple-element.18), channel_id=1, source_target_pairs={{4,8},{8,4},{5,9},{9,5},{6,10},{10,6},{7,11},{11,7},{20,24},{24,20... | collective-permute-start | bytes 221192 | tf_op jit(solution)/shard_map/ppermute | solution.py:455
  13.4 2.0 %collective-permute-start.3 = (f32[9,16,128]{2,1,0:T(8,128)S(1)}, f32[9,16,128]{2,1,0:T(8,128)S(1)}, u32[]{:S(2)}, u32[]{:S(2)}) collective-permute-start(f32[9,16,128]{2,1,0:T(8,128)S(1)} %get-tuple-element.19), channel_id=1, source_target_pairs={{0,4},{4,0},{8,12},{12,8},{1,5},{5,1},{9,13},{13,9},{2,6},{6,2},{1... | collective-permute-start | bytes 221192 | tf_op jit(solution)/shard_map/ppermute | solution.py:456
  15.4 2.0 %collective-permute-start.4 = (f32[4,9,128]{2,1,0:T(8,128)S(1)}, f32[4,9,128]{2,1,0:T(8,128)S(1)}, u32[]{:S(2)}, u32[]{:S(2)}) collective-permute-start(f32[4,9,128]{2,1,0:T(8,128)S(1)} %get-tuple-element.20), channel_id=1, source_target_pairs={{1,2},{2,1},{5,6},{6,5},{9,10},{10,9},{13,14},{14,13},{17,18},{18,... | collective-permute-start | bytes 55304 | tf_op jit(solution)/shard_map/ppermute | solution.py:457
  17.4 3.8 %collective-permute-done.4.z_two = f32[4,9,128]{2,1,0:T(8,128)S(1)} collective-permute-done((f32[4,9,128]{2,1,0:T(8,128)S(1)}, f32[4,9,128]{2,1,0:T(8,128)S(1)}, u32[]{:S(2)}, u32[]{:S(2)}) %collective-permute-start.4) | collective-permute-done | bytes 18464 | tf_op jit(solution)/shard_map/ppermute | solution.py:457
  21.2 0.0 collective-permute-start.5
  21.2 3.9 %collective-permute-done.5.z_one = f32[4,9,128]{2,1,0:T(8,128)S(1)} collective-permute-done((f32[4,9,128]{2,1,0:T(8,128)S(1)}, f32[4,9,128]{2,1,0:T(8,128)S(1)}, u32[]{:S(2)}, u32[]{:S(2)}) %collective-permute-start.5) | collective-permute-done | bytes 18464 | tf_op jit(solution)/shard_map/ppermute | solution.py:458
  25.1 0.0 collective-permute-done.2.y_two
  25.1 0.0 collective-permute-done.3.y_one
  25.1 0.0 collective-permute-done.far_ref
  25.1 0.0 collective-permute-done.1.near_ref
  25.1 0.0 copy-done.1
  25.1 0.0 copy-done.2
  25.2 4.0 %finish.1 = (f32[2,4,9,16,512]{4,3,2,1,0:T(8,128)}, f32[9,4,16]{2,1,0:T(4,128)}) custom-call(f32[2,4,9,16,512]{4,3,2,1,0:T(8,128)S(1)} %bitcast.24, f32[2,4,9,16,512]{4,3,2,1,0:T(8,128)S(1)} %bitcast.25, f32[2,4,9,16,256]{4,3,2,1,0:T(8,128)S(1)} %get-tuple-element.15.trace_ref, f32[4,9,16,128]{3,2,1,0:T(8,128)S(1)} %collective-permute-done.far_ref, ...), custom_call_target="tpu_custom_call" | custom-call | flops 900000000 | bytes 10000000 | tf_op jit(solution)/shard_map/finish/pallas_call | solution.py:399
Async XLA Ops:
  0.6 1.7 %copy-start = (f32[2,1,4,16,9,512]{5,3,4,2,1,0:T(8,128)S(1)}, f32[2,1,4,16,9,512]{5,3,4,2,1,0:T(8,128)}, u32[]{:S(2)}) copy-start(f32[2,1,4,16,9,512]{5,3,4,2,1,0:T(8,128)} %param.8) | copy-start | bytes 7077892
  2.3 6.5 %copy-start.3 = (bf16[512,1536]{1,0:T(8,128)(2,1)S(1)}, bf16[512,1536]{1,0:T(8,128)(2,1)}, u32[]{:S(2)}) copy-start(bf16[512,1536]{1,0:T(8,128)(2,1)} %d2_ref.1) | copy-start | bytes 4718596
  2.3 6.5 %copy-start.4 = (s32[1,4,16,6]{2,1,3,0:T(4,128)S(1)}, s32[1,4,16,6]{2,1,3,0:T(4,128)}, u32[]{:S(2)}) copy-start(s32[1,4,16,6]{2,1,3,0:T(4,128)} %param.13) | copy-start | bytes 4612
  2.3 6.5 %copy-start.5 = (s32[1,4,16,6]{2,1,3,0:T(4,128)S(1)}, s32[1,4,16,6]{2,1,3,0:T(4,128)}, u32[]{:S(2)}) copy-start(s32[1,4,16,6]{2,1,3,0:T(4,128)} %param.14) | copy-start | bytes 4612
  2.3 6.5 %copy-start.6 = (f32[3,1,4,16]{3,2,1,0:T(4,128)S(1)}, f32[3,1,4,16]{3,2,1,0:T(4,128)}, u32[]{:S(2)}) copy-start(f32[3,1,4,16]{3,2,1,0:T(4,128)} %param.11) | copy-start | bytes 2308
  2.3 6.5 %copy-start.7 = (bf16[512,256]{1,0:T(8,128)(2,1)S(1)}, bf16[512,256]{1,0:T(8,128)(2,1)}, u32[]{:S(2)}) copy-start(bf16[512,256]{1,0:T(8,128)(2,1)} %constant.2.clone.table_ref) | copy-start | bytes 786436
  2.8 22.3 %collective-permute-start = (f32[4,9,16,128]{3,2,1,0:T(8,128)S(1)}, f32[4,9,16,128]{3,2,1,0:T(8,128)S(1)}, u32[]{:S(2)}, u32[]{:S(2)}) collective-permute-start(f32[4,9,16,128]{3,2,1,0:T(8,128)S(1)} %get-tuple-element.16), channel_id=1, source_target_pairs={{16,32},{32,16},{48,64},{64,48},{80,96},{96,80},{112,0},{0,112},{1... | collective-permute-start | bytes 884744 | tf_op jit(solution)/shard_map/ppermute | solution.py:449
  4.5 20.6 %collective-permute-start.1 = (f32[4,9,16,128]{3,2,1,0:T(8,128)S(1)}, f32[4,9,16,128]{3,2,1,0:T(8,128)S(1)}, u32[]{:S(2)}, u32[]{:S(2)}) collective-permute-start(f32[4,9,16,128]{3,2,1,0:T(8,128)S(1)} %get-tuple-element.17), channel_id=1, source_target_pairs={{0,16},{16,0},{32,48},{48,32},{64,80},{80,64},{96,112},{112,96},{1... | collective-permute-start | bytes 884744 | tf_op jit(solution)/shard_map/ppermute | solution.py:450
  8.9 16.3 %copy-start.1 = (f32[1,4,16,9,384]{4,2,3,1,0:T(8,128)S(1)}, f32[1,4,16,9,384]{4,2,3,1,0:T(8,128)}, u32[]{:S(2)}) copy-start(f32[1,4,16,9,384]{4,2,3,1,0:T(8,128)} %param.12) | copy-start | bytes 2654212
  8.9 16.3 %copy-start.2 = (bf16[384,512]{1,0:T(8,128)(2,1)S(1)}, bf16[384,512]{1,0:T(8,128)(2,1)}, u32[]{:S(2)}) copy-start(bf16[384,512]{1,0:T(8,128)(2,1)} %lift_ref.1) | copy-start | bytes 1179652
  12.7 12.4 %collective-permute-start.2 = (f32[9,16,128]{2,1,0:T(8,128)S(1)}, f32[9,16,128]{2,1,0:T(8,128)S(1)}, u32[]{:S(2)}, u32[]{:S(2)}) collective-permute-start(f32[9,16,128]{2,1,0:T(8,128)S(1)} %get-tuple-element.18), channel_id=1, source_target_pairs={{4,8},{8,4},{5,9},{9,5},{6,10},{10,6},{7,11},{11,7},{20,24},{24,20... | collective-permute-start | bytes 221192 | tf_op jit(solution)/shard_map/ppermute | solution.py:455
  13.4 11.8 %collective-permute-start.3 = (f32[9,16,128]{2,1,0:T(8,128)S(1)}, f32[9,16,128]{2,1,0:T(8,128)S(1)}, u32[]{:S(2)}, u32[]{:S(2)}) collective-permute-start(f32[9,16,128]{2,1,0:T(8,128)S(1)} %get-tuple-element.19), channel_id=1, source_target_pairs={{0,4},{4,0},{8,12},{12,8},{1,5},{5,1},{9,13},{13,9},{2,6},{6,2},{1... | collective-permute-start | bytes 221192 | tf_op jit(solution)/shard_map/ppermute | solution.py:456
  15.4 5.8 %collective-permute-start.4 = (f32[4,9,128]{2,1,0:T(8,128)S(1)}, f32[4,9,128]{2,1,0:T(8,128)S(1)}, u32[]{:S(2)}, u32[]{:S(2)}) collective-permute-start(f32[4,9,128]{2,1,0:T(8,128)S(1)} %get-tuple-element.20), channel_id=1, source_target_pairs={{1,2},{2,1},{5,6},{6,5},{9,10},{10,9},{13,14},{14,13},{17,18},{18,... | collective-permute-start | bytes 55304 | tf_op jit(solution)/shard_map/ppermute | solution.py:457
  21.2 3.9 %collective-permute-start.5 = (f32[4,9,128]{2,1,0:T(8,128)S(1)}, f32[4,9,128]{2,1,0:T(8,128)S(1)}, u32[]{:S(2)}, u32[]{:S(2)}) collective-permute-start(f32[4,9,128]{2,1,0:T(8,128)S(1)} %get-tuple-element.21), channel_id=1, source_target_pairs={{0,1},{1,0},{2,3},{3,2},{4,5},{5,4},{6,7},{7,6},{8,9},{9,8},{10,11... | collective-permute-start | bytes 55304 | tf_op jit(solution)/shard_map/ppermute | solution.py:458

commit v2 on v1

--- a/solution.py
+++ b/solution.py
@@ -285,150 +285,142 @@
 
 
 def final_kernel(
-    low_x_ref, high_x_ref, trace_ref, far_ref, near_ref, y_two, y_one, z_two, z_one,
+    state_ref, trace_ref, far_ref, near_ref, y_two, y_one, z_two, z_one,
     coef_ref, source_ref, edge_ref, partial_ref, stored_ref, lift_ref,
     advanced_ref, kernel_ref,
-    flux_ref, sum_ref,
+    flux_ref, sum_ref, out_ref, out_sem,
 ):
-    y = pl.program_id(0)
-    last_y = pl.num_programs(0) - 1
-    fields, count_z = (partial_ref.shape[2], partial_ref.shape[3])
+    count_y, fields, count_z, nodes = state_ref.shape[1:]
+    last_y = count_y - 1
     odd_x = odd_position("gx")
     odd_y = odd_position("gy")
     odd_z = odd_position("gz")
     lane = lane_index((count_z, LANES))
     upper = lane >= FACE
     z_pos = lax.broadcasted_iota(jnp.int32, lane.shape, 0)
-    lam, mu, inv, speed = [coef_ref[k, 0] for k in range(4)]
-    below = jnp.maximum(y - 1, 0)
-    above = jnp.minimum(y + 1, last_y)
     take_near = upper == odd_x
-    for s in range(2):
-        for d in range(3):
-            source = source_ref[d, 0]
-            if d == 0 and s == 1:
-                source = (source + FACE) % LANES
-            if d > 0:
-                rim = edge_ref[d - 1, 0, 0] > 0.0
-                free = edge_ref[d - 1, 1, 0]
-                keep_velocity = free - 1.0
-                keep_stress = -free - 1.0
-            jumps = []
-            for f in range(fields):
-                if d == 0:
-                    inside = jnp.where(upper, high_x_ref[s, 0, f], low_x_ref[s, 0, f])
-                    near, far = (near_ref[0, f], far_ref[0, f])
-                    mixed = jnp.where(take_near, near, far) if s == 0 else jnp.where(take_near, far, near)
-                elif d == 1:
-                    inside = trace_ref[s, y, f, :, :LANES]
-                    two, one = (y_two[f], y_one[f])
-                    from_below = jnp.where(odd_y, one, two)
-                    from_above = jnp.where(odd_y, two, one)
+
+    def write(y):
+        return pltpu.make_async_copy(out_ref.at[:, y], advanced_ref.at[:, y], out_sem.at[y])
+
+    def row(y, carry):
+        below = jnp.maximum(y - 1, 0)
+        above = jnp.minimum(y + 1, last_y)
+        lam, mu, inv, speed = [coef_ref[k, y] for k in range(4)]
+        for s in range(2):
+            for d in range(3):
+                source = source_ref[d, y]
+                if d == 0 and s == 1:
+                    source = (source + FACE) % LANES
+                if d > 0:
+                    rim = edge_ref[d - 1, 0, y] > 0.0
+                    free = edge_ref[d - 1, 1, y]
+                    keep_velocity = free - 1.0
+                    keep_stress = -free - 1.0
+                jumps = []
+                for f in range(fields):
+                    if d == 0:
+                        inside = jnp.where(
+                            upper, state_ref[s, y, f, :, nodes - LANES :], state_ref[s, y, f, :, :LANES]
+                        )
+                        near, far = (near_ref[y, f], far_ref[y, f])
+                        if s == 1:
+                            near, far = (far, near)
+                        mixed = jnp.where(take_near, near, far)
+                    elif d == 1:
+                        inside = trace_ref[s, y, f, :, :LANES]
+                        two, one = (y_two[f], y_one[f])
+                        from_below = jnp.where(odd_y, one, two)
+                        from_above = jnp.where(odd_y, two, one)
+                        if s == 1:
+                            from_below = pltpu.roll(from_below, FACE, 1)
+                            from_above = pltpu.roll(from_above, FACE, 1)
+                        lower = jnp.where(y == 0, from_below, trace_ref[s, below, f, :, :LANES])
+                        higher = jnp.where(y == last_y, from_above, trace_ref[s, above, f, :, :LANES])
+                        mixed = jnp.where(upper, lower, higher)
+                    else:
+                        inside = trace_ref[s, y, f, :, LANES:]
+                        two = jnp.broadcast_to(z_two[y, f : f + 1, :], lane.shape)
+                        one = jnp.broadcast_to(z_one[y, f : f + 1, :], lane.shape)
+                        from_below = jnp.where(odd_z, one, two)
+                        from_above = jnp.where(odd_z, two, one)
+                        if s == 1:
+                            from_below = pltpu.roll(from_below, FACE, 1)
+                            from_above = pltpu.roll(from_above, FACE, 1)
+                        lower = jnp.where(z_pos == 0, from_below, pltpu.roll(inside, 1, 0))
+                        higher = jnp.where(
+                            z_pos == count_z - 1, from_above, pltpu.roll(inside, count_z - 1, 0)
+                        )
+                        mixed = jnp.where(upper, lower, higher)
+                    turned = jnp.take_along_axis(mixed, source, axis=1)
+                    jump = turned - inside
+                    if d > 0:
+                        keep = keep_velocity if f < 3 else keep_stress
+                        jump = jnp.where(rim, inside * keep, jump)
+                    jumps.append(jump)
                     if s == 1:
-                        from_below = pltpu.roll(from_below, FACE, 1)
-                        from_above = pltpu.roll(from_above, FACE, 1)
-                    lower = jnp.where(y == 0, from_below, trace_ref[s, below, f, :, :LANES])
-                    higher = jnp.where(y == last_y, from_above, trace_ref[s, above, f, :, :LANES])
-                    mixed = jnp.where(upper, lower, higher)
-                else:
-                    inside = trace_ref[s, y, f, :, LANES:]
-                    two = jnp.broadcast_to(z_two[0, f : f + 1, :], lane.shape)
-                    one = jnp.broadcast_to(z_one[0, f : f + 1, :], lane.shape)
-                    from_below = jnp.where(odd_z, one, two)
-                    from_above = jnp.where(odd_z, two, one)
-                    if s == 1:
-                        from_below = pltpu.roll(from_below, FACE, 1)
-                        from_above = pltpu.roll(from_above, FACE, 1)
-                    lower = jnp.where(z_pos == 0, from_below, pltpu.roll(inside, 1, 0))
-                    higher = jnp.where(
-                        z_pos == count_z - 1, from_above, pltpu.roll(inside, count_z - 1, 0)
-                    )
-                    mixed = jnp.where(upper, lower, higher)
-                turned = jnp.take_along_axis(mixed, source, axis=1)
-                jump = turned - inside
-                if d > 0:
-                    keep = keep_velocity if f < 3 else keep_stress
-                    jump = jnp.where(rim, inside * keep, jump)
-                jumps.append(jump)
-                if s == 1:
-                    term = stored_ref[0, f, :, d * LANES : (d + 1) * LANES] * jump
-                    if d == 0:
-                        sum_ref[f] = term
-                    else:
-                        sum_ref[f] += term
-            flux = [speed * jump for jump in jumps]
-            for i in range(3):
-                flux[i] = flux[i] + inv * jumps[stress_slot[i][d]]
-            common = lam * jumps[d]
-            for i in range(3):
-                flux[3 + i] = flux[3 + i] + common
-            for i, j, f in ((0, 0, 3), (1, 1, 4), (2, 2, 5), (1, 2, 6), (0, 2, 7), (0, 1, 8)):
-                if j == d:
-                    flux[f] = flux[f] + mu * jumps[i]
-                if i == d:
-                    flux[f] = flux[f] + mu * jumps[j]
-            for f in range(fields):
-                flux_ref[s, f, :, d * LANES : (d + 1) * LANES] = flux[f].astype(jnp.bfloat16)
+                        term = stored_ref[y, f, :, d * LANES : (d + 1) * LANES] * jump
+                        if d == 0:
+                            sum_ref[f] = term
+                        else:
+                            sum_ref[f] += term
+                flux = [speed * jump for jump in jumps]
+                for i in range(3):
+                    flux[i] = flux[i] + inv * jumps[stress_slot[i][d]]
+                common = lam * jumps[d]
+                for i in range(3):
+                    flux[3 + i] = flux[3 + i] + common
+                for i, j, f in ((0, 0, 3), (1, 1, 4), (2, 2, 5), (1, 2, 6), (0, 2, 7), (0, 1, 8)):
+                    if j == d:
+                        flux[f] = flux[f] + mu * jumps[i]
+                    if i == d:
+                        flux[f] = flux[f] + mu * jumps[j]
+                for f in range(fields):
+                    flux_ref[s, f, :, d * LANES : (d + 1) * LANES] = flux[f].astype(jnp.bfloat16)
         lifted = jnp.dot(
-            flux_ref[s].reshape(fields * count_z, 3 * LANES),
+            flux_ref[...].reshape(2 * fields * count_z, 3 * LANES),
             lift_ref[...],
             preferred_element_type=jnp.float32,
-        ).reshape(fields, count_z, -1)
-        scale = step_size if s == 0 else -step_size
-        advanced_ref[s, 0] = partial_ref[s, 0] + scale * lifted
-    for f in range(fields):
-        sums = jnp.sum(sum_ref[f], axis=1, keepdims=True) * (1.0 / FACE)
-        across = jnp.sum(jnp.where(z_pos == lane, sums, 0.0), axis=0, keepdims=True)
-        kernel_ref[f, pl.ds(y, 1), :] = across[:, :count_z]
+        ).reshape(2, fields, count_z, nodes)
+        for s in range(2):
+            scale = step_size if s == 0 else -step_size
+            out_ref[s, y] = partial_ref[s, y] + scale * lifted[s]
+        write(y).start()
+        for f in range(fields):
+            sums = jnp.sum(sum_ref[f], axis=1, keepdims=True) * (1.0 / FACE)
+            across = jnp.sum(jnp.where(z_pos == lane, sums, 0.0), axis=0, keepdims=True)
+            kernel_ref[f, pl.ds(y, 1), :] = across[:, :count_z]
+        return carry
+
+    lax.fori_loop(0, count_y, row, 0)
+    for y in range(count_y):
+        write(y).wait()
 
 
 def finish(
     state, traces, far, near, y_two, y_one, z_two, z_one, coef, source, edge, part, stored, lift
 ):
     _, count_y, fields, count_z, nodes = state.shape
-    tiles = nodes // LANES
     f32 = jnp.float32
-    whole = lambda a: pl.BlockSpec(a.shape, lambda y: (0,) * a.ndim)
     outs = (
         jax.ShapeDtypeStruct(state.shape, f32),
         jax.ShapeDtypeStruct((fields, count_y, count_z), f32),
     )
-    by_y = lambda lead, rest: pl.BlockSpec(
-        lead + (1,) + rest, lambda y: (0,) * len(lead) + (y,) + (0,) * len(rest)
-    )
     return pl.pallas_call(
         final_kernel,
         out_shape=outs,
-        grid=(count_y,),
-        in_specs=[
-            pl.BlockSpec((2, 1, fields, count_z, LANES), lambda y: (0, y, 0, 0, 0)),
-            pl.BlockSpec((2, 1, fields, count_z, LANES), lambda y: (0, y, 0, 0, tiles - 1)),
-            whole(traces),
-            by_y((), (fields, count_z, LANES)),
-            by_y((), (fields, count_z, LANES)),
-            whole(y_two),
-            whole(y_one),
-            by_y((), (fields, LANES)),
-            by_y((), (fields, LANES)),
-            by_y((4,), (count_z, LANES)),
-            by_y((3,), (count_z, LANES)),
-            by_y((2, 2), (count_z, LANES)),
-            by_y((2,), (fields, count_z, nodes)),
-            by_y((), (fields, count_z, 3 * LANES)),
-            whole(lift),
-        ],
-        out_specs=(
-            by_y((2,), (fields, count_z, nodes)),
-            pl.BlockSpec(outs[1].shape, lambda y: (0, 0, 0)),
-        ),
+        in_specs=[pl.BlockSpec(memory_space=pltpu.VMEM)] * 14,
+        out_specs=(pl.BlockSpec(memory_space=pl.ANY), pl.BlockSpec(memory_space=pltpu.VMEM)),
         scratch_shapes=[
             pltpu.VMEM((2, fields, count_z, 3 * LANES), jnp.bfloat16),
             pltpu.VMEM((fields, count_z, LANES), f32),
+            pltpu.VMEM(state.shape, f32),
+            pltpu.SemaphoreType.DMA((count_y,)),
         ],
         compiler_params=pltpu.CompilerParams(vmem_limit_bytes=LIMIT),
         cost_estimate=pl.CostEstimate(flops=9 * 10**8, bytes_accessed=10**7, transcendentals=0),
         name="finish",
-    )(state, state, traces, far, near, y_two, y_one, z_two, z_one, coef, source, edge, part, stored, lift)
+    )(state, traces, far, near, y_two, y_one, z_two, z_one, coef, source, edge, part, stored, lift)
 
 
 def swaps(count, start, wrap):
@@ -455,6 +447,7 @@
     y_two = lax.ppermute(y_two, "gy", swaps(ny, 1, False))
     y_one = lax.ppermute(y_one, "gy", swaps(ny, 0, False))
     z_two = lax.ppermute(z_two, "gz", swaps(nz, 1, False))
+    z_one, y_one = lax.optimization_barrier((z_one, y_one))
     z_one = lax.ppermute(z_one, "gz", swaps(nz, 0, False))
     advanced, kernel = finish(
         view, traces, far_in, near_in, y_two, y_one, z_two, z_one, coef, source, edge, part,

time: 29.4 us -> 27.5 us (0.935)
  the two profiles are of different devices: /device:TPU:72 before, /device:TPU:42 now
where the time goes in v2:
time: 27.5 us; the launch traced here: 27.3 us
  starting transfers between devices  12.5 us (45%)
  Pallas kernels  8.42 us (31%)
  waiting for transfers between devices  3.91 us (14%)
  local copies, waits for them, and re-layouts  1.69 us (6%)
  between operations  0.75 us (3%)
    pallas_call x1, Pallas kernels, finish(): pl.pallas_call(final_kernel, out_shape=outs, in_specs=[pl.BlockSpec(memor...  4.11 us
    ppermute x1, starting transfers between devices, local(): z_two = lax.ppermute(z_two, 'gz', swaps(nz, 1, False))  3.83 us
    pallas_call x1, Pallas kernels, volume(): pl.pallas_call(volume_kernel, out_shape=outs, grid=(parts,), in_specs=[wh...  3.8 us
    ppermute x1, starting transfers between devices, local(): near_in = lax.ppermute(near, 'gx', swaps(nx, 0, True))  3.45 us
    ppermute x1, starting transfers between devices, local(): y_two = lax.ppermute(y_two, 'gy', swaps(ny, 1, False))  3.43 us
    ppermute x1, waiting for transfers between devices, local(): z_one = lax.ppermute(z_one, 'gz', swaps(nz, 0, False))  2.03 us
    ppermute x1, waiting for transfers between devices, local(): z_two = lax.ppermute(z_two, 'gz', swaps(nz, 1, False))  1.87 us
    unnamed x16, local copies, waits for them, and re-layouts  1.69 us
  transfers between devices with their start and end apart: 6, of which 2 were waited for; matrix products, arithmetic and copies ran while one was open for 0% of the time, Pallas kernels for 14%

profile of v2, /device:TPU:42, one launch (start us, length us, event | category | flops | bytes accessed | tf_op | source)
XLA Modules:
  0.0 27.3 jit_solution(960235086702059496)
XLA Ops:
  0.6 0.0 copy-start
  0.6 1.7 %copy-done = f32[2,1,4,16,9,512]{5,3,4,2,1,0:T(8,128)S(1)} copy-done((f32[2,1,4,16,9,512]{5,3,4,2,1,0:T(8,128)S(1)}, f32[2,1,4,16,9,512]{5,3,4,2,1,0:T(8,128)}, u32[]{:S(2)}) %copy-start) | copy-done | bytes 2359320
  2.3 0.0 copy-start.3
  2.3 0.0 copy-start.4
  2.3 0.0 copy-start.5
  2.3 0.0 copy-start.6
  2.3 0.0 copy-start.7
  2.3 0.5 %pack_faces.1 = (f32[4,9,16,128]{3,2,1,0:T(8,128)S(1)}, f32[4,9,16,128]{3,2,1,0:T(8,128)S(1)}) custom-call(f32[2,4,9,16,512]{4,3,2,1,0:T(8,128)S(1)} %bitcast.21, f32[2,4,9,16,512]{4,3,2,1,0:T(8,128)S(1)} %bitcast.22), custom_call_target="tpu_custom_call" | custom-call | flops 1000000 | bytes 2000000 | tf_op jit(solution)/shard_map/pack_faces/pallas_call | solution.py:63
  2.8 1.7 %collective-permute-start = (f32[4,9,16,128]{3,2,1,0:T(8,128)S(1)}, f32[4,9,16,128]{3,2,1,0:T(8,128)S(1)}, u32[]{:S(2)}, u32[]{:S(2)}) collective-permute-start(f32[4,9,16,128]{3,2,1,0:T(8,128)S(1)} %get-tuple-element.18), channel_id=1, source_target_pairs={{16,32},{32,16},{48,64},{64,48},{80,96},{96,80},{112,0},{0,112},{1... | collective-permute-start | bytes 884744 | tf_op jit(solution)/shard_map/ppermute | solution.py:441
  4.5 3.4 %collective-permute-start.1 = (f32[4,9,16,128]{3,2,1,0:T(8,128)S(1)}, f32[4,9,16,128]{3,2,1,0:T(8,128)S(1)}, u32[]{:S(2)}, u32[]{:S(2)}) collective-permute-start(f32[4,9,16,128]{3,2,1,0:T(8,128)S(1)} %get-tuple-element.19), channel_id=1, source_target_pairs={{0,16},{16,0},{32,48},{48,32},{64,80},{80,64},{96,112},{112,96},{1... | collective-permute-start | bytes 884744 | tf_op jit(solution)/shard_map/ppermute | solution.py:442
  7.9 0.0 copy-done.3
  7.9 0.0 copy-done.4
  7.9 0.0 copy-done.5
  7.9 0.0 copy-done.6
  8.0 0.0 copy-done.7
  8.0 0.0 copy-start.1
  8.0 0.0 copy-start.2
  8.0 3.8 %volume.1 = (f32[2,4,9,16,512]{4,3,2,1,0:T(8,128)S(1)}, f32[4,4,16,128]{3,2,1,0:T(8,128)S(1)}, s32[3,4,16,128]{3,2,1,0:T(8,128)S(1)}, f32[2,2,4,16,128]{4,3,2,1,...) custom-call(f32[2,4,9,16,512]{4,3,2,1,0:T(8,128)S(1)} %bitcast.23, ...), custom_call_target="tpu_custom_call" | custom-call | flops 4200000000 | bytes 12000000 | tf_op jit(solution)/shard_map/volume/pallas_call | solution.py:255
  11.8 0.1 collective-permute-start.3
  11.9 3.4 %collective-permute-start.2 = (f32[9,16,128]{2,1,0:T(8,128)S(1)}, f32[9,16,128]{2,1,0:T(8,128)S(1)}, u32[]{:S(2)}, u32[]{:S(2)}) collective-permute-start(f32[9,16,128]{2,1,0:T(8,128)S(1)} %get-tuple-element.20), channel_id=1, source_target_pairs={{4,8},{8,4},{5,9},{9,5},{6,10},{10,6},{7,11},{11,7},{20,24},{24,20... | collective-permute-start | bytes 221192 | tf_op jit(solution)/shard_map/ppermute | solution.py:447
  15.3 3.8 %collective-permute-start.4 = (f32[4,9,128]{2,1,0:T(8,128)S(1)}, f32[4,9,128]{2,1,0:T(8,128)S(1)}, u32[]{:S(2)}, u32[]{:S(2)}) collective-permute-start(f32[4,9,128]{2,1,0:T(8,128)S(1)} %get-tuple-element.24), channel_id=1, source_target_pairs={{1,2},{2,1},{5,6},{6,5},{9,10},{10,9},{13,14},{14,13},{17,18},{18,... | collective-permute-start | bytes 55304 | tf_op jit(solution)/shard_map/ppermute | solution.py:449
  19.2 0.0 collective-permute-done.3.y_one
  19.2 0.1 collective-permute-start.5
  19.3 1.9 %collective-permute-done.4.z_two = f32[4,9,128]{2,1,0:T(8,128)S(1)} collective-permute-done((f32[4,9,128]{2,1,0:T(8,128)S(1)}, f32[4,9,128]{2,1,0:T(8,128)S(1)}, u32[]{:S(2)}, u32[]{:S(2)}) %collective-permute-start.4) | collective-permute-done | bytes 18464 | tf_op jit(solution)/shard_map/ppermute | solution.py:449
  21.1 0.0 collective-permute-done.2.y_two
  21.1 2.0 %collective-permute-done.5.z_one = f32[4,9,128]{2,1,0:T(8,128)S(1)} collective-permute-done((f32[4,9,128]{2,1,0:T(8,128)S(1)}, f32[4,9,128]{2,1,0:T(8,128)S(1)}, u32[]{:S(2)}, u32[]{:S(2)}) %collective-permute-start.5) | collective-permute-done | bytes 18464 | tf_op jit(solution)/shard_map/ppermute | solution.py:451
  23.2 0.0 collective-permute-done.far_ref
  23.2 0.0 collective-permute-done.1.near_ref
  23.2 0.0 copy-done.1
  23.2 0.0 copy-done.2
  23.2 4.1 %finish.1 = (f32[2,4,9,16,512]{4,3,2,1,0:T(8,128)}, f32[9,4,16]{2,1,0:T(4,128)}) custom-call(f32[2,4,9,16,512]{4,3,2,1,0:T(8,128)S(1)} %bitcast.24, f32[2,4,9,16,256]{4,3,2,1,0:T(8,128)S(1)} %get-tuple-element.17.trace_ref, f32[4,9,16,128]{3,2,1,0:T(8,128)S(1)} %collective-permute-done.far_ref, f32[4,9,16,128]{3,2,1,0:T(8,128)S(1)} %collective-permute-done.1.near_ref, ...), custom_call_target="tpu_custom_call" | custom-call | flops 900000000 | bytes 10000000 | tf_op jit(solution)/shard_map/finish/pallas_call | solution.py:409
Async XLA Ops:
  0.6 1.7 %copy-start = (f32[2,1,4,16,9,512]{5,3,4,2,1,0:T(8,128)S(1)}, f32[2,1,4,16,9,512]{5,3,4,2,1,0:T(8,128)}, u32[]{:S(2)}) copy-start(f32[2,1,4,16,9,512]{5,3,4,2,1,0:T(8,128)} %param.8) | copy-start | bytes 7077892
  2.3 5.6 %copy-start.3 = (bf16[512,1536]{1,0:T(8,128)(2,1)S(1)}, bf16[512,1536]{1,0:T(8,128)(2,1)}, u32[]{:S(2)}) copy-start(bf16[512,1536]{1,0:T(8,128)(2,1)} %d2_ref.1) | copy-start | bytes 4718596
  2.3 5.6 %copy-start.4 = (s32[1,4,16,6]{2,1,3,0:T(4,128)S(1)}, s32[1,4,16,6]{2,1,3,0:T(4,128)}, u32[]{:S(2)}) copy-start(s32[1,4,16,6]{2,1,3,0:T(4,128)} %param.13) | copy-start | bytes 4612
  2.3 5.6 %copy-start.5 = (s32[1,4,16,6]{2,1,3,0:T(4,128)S(1)}, s32[1,4,16,6]{2,1,3,0:T(4,128)}, u32[]{:S(2)}) copy-start(s32[1,4,16,6]{2,1,3,0:T(4,128)} %param.14) | copy-start | bytes 4612
  2.3 5.6 %copy-start.6 = (f32[3,1,4,16]{3,2,1,0:T(4,128)S(1)}, f32[3,1,4,16]{3,2,1,0:T(4,128)}, u32[]{:S(2)}) copy-start(f32[3,1,4,16]{3,2,1,0:T(4,128)} %param.11) | copy-start | bytes 2308
  2.3 5.6 %copy-start.7 = (bf16[512,256]{1,0:T(8,128)(2,1)S(1)}, bf16[512,256]{1,0:T(8,128)(2,1)}, u32[]{:S(2)}) copy-start(bf16[512,256]{1,0:T(8,128)(2,1)} %constant.2.clone.table_ref) | copy-start | bytes 786436
  2.8 20.3 %collective-permute-start = (f32[4,9,16,128]{3,2,1,0:T(8,128)S(1)}, f32[4,9,16,128]{3,2,1,0:T(8,128)S(1)}, u32[]{:S(2)}, u32[]{:S(2)}) collective-permute-start(f32[4,9,16,128]{3,2,1,0:T(8,128)S(1)} %get-tuple-element.18), channel_id=1, source_target_pairs={{16,32},{32,16},{48,64},{64,48},{80,96},{96,80},{112,0},{0,112},{1... | collective-permute-start | bytes 884744 | tf_op jit(solution)/shard_map/ppermute | solution.py:441
  4.5 18.7 %collective-permute-start.1 = (f32[4,9,16,128]{3,2,1,0:T(8,128)S(1)}, f32[4,9,16,128]{3,2,1,0:T(8,128)S(1)}, u32[]{:S(2)}, u32[]{:S(2)}) collective-permute-start(f32[4,9,16,128]{3,2,1,0:T(8,128)S(1)} %get-tuple-element.19), channel_id=1, source_target_pairs={{0,16},{16,0},{32,48},{48,32},{64,80},{80,64},{96,112},{112,96},{1... | collective-permute-start | bytes 884744 | tf_op jit(solution)/shard_map/ppermute | solution.py:442
  8.0 15.2 %copy-start.1 = (f32[1,4,16,9,384]{4,2,3,1,0:T(8,128)S(1)}, f32[1,4,16,9,384]{4,2,3,1,0:T(8,128)}, u32[]{:S(2)}) copy-start(f32[1,4,16,9,384]{4,2,3,1,0:T(8,128)} %param.12) | copy-start | bytes 2654212
  8.0 15.2 %copy-start.2 = (bf16[384,512]{1,0:T(8,128)(2,1)S(1)}, bf16[384,512]{1,0:T(8,128)(2,1)}, u32[]{:S(2)}) copy-start(bf16[384,512]{1,0:T(8,128)(2,1)} %lift_ref.1) | copy-start | bytes 1179652
  11.8 7.4 %collective-permute-start.3 = (f32[9,16,128]{2,1,0:T(8,128)S(1)}, f32[9,16,128]{2,1,0:T(8,128)S(1)}, u32[]{:S(2)}, u32[]{:S(2)}) collective-permute-start(f32[9,16,128]{2,1,0:T(8,128)S(1)} %get-tuple-element.22), channel_id=1, source_target_pairs={{0,4},{4,0},{8,12},{12,8},{1,5},{5,1},{9,13},{13,9},{2,6},{6,2},{1... | collective-permute-start | bytes 221192 | tf_op jit(solution)/shard_map/ppermute | solution.py:448
  11.9 9.2 %collective-permute-start.2 = (f32[9,16,128]{2,1,0:T(8,128)S(1)}, f32[9,16,128]{2,1,0:T(8,128)S(1)}, u32[]{:S(2)}, u32[]{:S(2)}) collective-permute-start(f32[9,16,128]{2,1,0:T(8,128)S(1)} %get-tuple-element.20), channel_id=1, source_target_pairs={{4,8},{8,4},{5,9},{9,5},{6,10},{10,6},{7,11},{11,7},{20,24},{24,20... | collective-permute-start | bytes 221192 | tf_op jit(solution)/shard_map/ppermute | solution.py:447
  15.3 5.8 %collective-permute-start.4 = (f32[4,9,128]{2,1,0:T(8,128)S(1)}, f32[4,9,128]{2,1,0:T(8,128)S(1)}, u32[]{:S(2)}, u32[]{:S(2)}) collective-permute-start(f32[4,9,128]{2,1,0:T(8,128)S(1)} %get-tuple-element.24), channel_id=1, source_target_pairs={{1,2},{2,1},{5,6},{6,5},{9,10},{10,9},{13,14},{14,13},{17,18},{18,... | collective-permute-start | bytes 55304 | tf_op jit(solution)/shard_map/ppermute | solution.py:449
  19.2 4.0 %collective-permute-start.5 = (f32[4,9,128]{2,1,0:T(8,128)S(1)}, f32[4,9,128]{2,1,0:T(8,128)S(1)}, u32[]{:S(2)}, u32[]{:S(2)}) collective-permute-start(f32[4,9,128]{2,1,0:T(8,128)S(1)} %get-tuple-element.25), channel_id=1, source_target_pairs={{0,1},{1,0},{2,3},{3,2},{4,5},{5,4},{6,7},{7,6},{8,9},{9,8},{10,11... | collective-permute-start | bytes 55304 | tf_op jit(solution)/shard_map/ppermute | solution.py:451

commit v3 on v2

v3 whole, which is shorter than its diff:
```python
import jax
import jax.numpy as jnp
import numpy as np
from functools import partial
from jax import lax
from jax.experimental import pallas as pl
from jax.experimental.pallas import tpu as pltpu
from jax.sharding import PartitionSpec as P

NP = 8
FACE = NP * NP
LANES = 128
step_size = 0.15
stress_slot = ((3, 8, 7), (8, 4, 6), (7, 6, 5))
shear_pairs = ((6, 1, 2), (7, 0, 2), (8, 0, 1))
LIMIT = 20 * 1024 * 1024
PACK_LIMIT = 56 * 1024 * 1024


def trace_table():
    table = np.zeros((NP**3, 4 * FACE), np.float32)
    for first in range(NP):
        for second in range(NP):
            m = first * NP + second
            table[first * 64 + second, m] = 1.0
            table[first * 64 + 56 + second, FACE + m] = 1.0
            table[first * 64 + second * 8, 2 * FACE + m] = 1.0
            table[first * 64 + second * 8 + 7, 3 * FACE + m] = 1.0
    return table


def lane_index(shape):
    return lax.broadcasted_iota(jnp.int32, shape, len(shape) - 1)


def merged(forward, adjoint, upper):
    rows = forward.shape[:-1]
    flat = (-1, LANES)
    turned = pltpu.roll(adjoint.reshape(flat), FACE, 1)
    own = (lane_index(turned.shape) >= FACE) == upper
    return jnp.where(own, forward.reshape(flat), turned).reshape(rows + (LANES,))


def odd_position(axis):
    return lax.axis_index(axis) % 2 == 1


def pack_kernel(state_ref, far_ref, near_ref, held_ref, ready_ref, sem, out_sem):
    odd = odd_position("gx")
    last = state_ref.shape[-1] - LANES
    part = held_ref.shape[3]
    chunks = [(h, c) for h in range(2) for c in range(2)]

    def fetch(h, c):
        first_tile = odd if h == 1 else jnp.logical_not(odd)
        at = pl.multiple_of(jnp.where(first_tile, 0, last), LANES)
        return pltpu.make_async_copy(
            state_ref.at[:, pl.ds(c * part, part), :, :, pl.ds(at, LANES)],
            held_ref.at[h, c],
            sem.at[h, c],
        )

    def deliver(h, c):
        target = (far_ref, near_ref)[h]
        return pltpu.make_async_copy(
            ready_ref.at[h, c], target.at[pl.ds(c * part, part)], out_sem.at[h, c]
        )

    for h, c in chunks:
        fetch(h, c).start()
    for h, c in chunks:
        fetch(h, c).wait()
        upper = jnp.logical_not(odd) if h == 1 else odd
        ready_ref[h, c] = merged(held_ref[h, c, 0], held_ref[h, c, 1], upper)
        deliver(h, c).start()
    for h, c in chunks:
        deliver(h, c).wait()


def pack_faces(state):
    _, count_y, fields, count_z, nodes = state.shape
    message = jax.ShapeDtypeStruct((count_y, fields, count_z, LANES), jnp.float32)
    return pl.pallas_call(
        pack_kernel,
        out_shape=(message, message),
        in_specs=[pl.BlockSpec(memory_space=pl.ANY)],
        out_specs=(pl.BlockSpec(memory_space=pl.ANY),) * 2,
        scratch_shapes=[
            pltpu.VMEM((2, 2, 2, count_y // 2, fields, count_z, LANES), jnp.float32),
            pltpu.VMEM((2, 2, count_y // 2, fields, count_z, LANES), jnp.float32),
            pltpu.SemaphoreType.DMA((2, 2)),
            pltpu.SemaphoreType.DMA((2, 2)),
        ],
        compiler_params=pltpu.CompilerParams(vmem_limit_bytes=PACK_LIMIT),
        cost_estimate=pl.CostEstimate(flops=10**6, bytes_accessed=2 * 10**6, transcendentals=0),
        name="pack_faces",
    )(state)


def trace_kernel(state_ref, table_ref, trace_ref, y_two, y_one, z_two, z_one):
    _, count_y, fields, count_z, _ = state_ref.shape

    def one_state(s, carry):
        values = state_ref[s].reshape(count_y * fields * count_z, -1)
        high = values.astype(jnp.bfloat16)
        low = (values - high.astype(jnp.float32)).astype(jnp.bfloat16)
        table = table_ref[...]
        picked = jnp.dot(high, table, preferred_element_type=jnp.float32)
        picked = picked + jnp.dot(low, table, preferred_element_type=jnp.float32)
        trace_ref[s] = picked.reshape(count_y, fields, count_z, 2 * LANES)
        return carry

    lax.fori_loop(0, 2, one_state, 0)
    odd_y = odd_position("gy")
    odd_z = odd_position("gz")
    end = count_y - 1
    down = merged(trace_ref[0, 0, :, :, :LANES], trace_ref[1, 0, :, :, :LANES], False)
    up = merged(trace_ref[0, end, :, :, :LANES], trace_ref[1, end, :, :, :LANES], True)
    y_two[...] = jnp.where(odd_y, up, down)
    y_one[...] = jnp.where(odd_y, down, up)
    for y in range(count_y):
        first = merged(trace_ref[0, y, :, 0, LANES:], trace_ref[1, y, :, 0, LANES:], False)
        last = merged(
            trace_ref[0, y, :, count_z - 1, LANES:], trace_ref[1, y, :, count_z - 1, LANES:], True
        )
        z_two[y] = jnp.where(odd_z, last, first)
        z_one[y] = jnp.where(odd_z, first, last)


def extract_traces(state, table):
    _, count_y, fields, count_z, nodes = state.shape
    f32 = jnp.float32
    y_message = jax.ShapeDtypeStruct((fields, count_z, LANES), f32)
    z_message = jax.ShapeDtypeStruct((count_y, fields, LANES), f32)
    return pl.pallas_call(
        trace_kernel,
        out_shape=(
            jax.ShapeDtypeStruct((2, count_y, fields, count_z, 2 * LANES), f32),
            y_message,
            y_message,
            z_message,
            z_message,
        ),
        in_specs=[pl.BlockSpec(memory_space=pltpu.VMEM)] * 2,
        out_specs=(pl.BlockSpec(memory_space=pltpu.VMEM),) * 5,
        compiler_params=pltpu.CompilerParams(vmem_limit_bytes=LIMIT),
        cost_estimate=pl.CostEstimate(flops=6 * 10**8, bytes_accessed=4 * 10**6, transcendentals=0),
        name="extract_traces",
    )(state, table)


def spread(columns, rows, pick):
    return lax.dot_general(
        columns,
        pick,
        (((0,), (0,)), ((), ())),
        precision=lax.Precision.HIGHEST,
        preferred_element_type=jnp.float32,
    )


def volume_kernel(
    state_ref, deriv_ref, material_ref, orient_ref, flags_ref,
    partial_ref, coef_ref, source_ref, edge_ref,
    low_ref, grad_ref, div_ref, wide_ref,
):
    _, count_y, fields, count_z, _ = state_ref.shape
    rows = 2 * count_y * count_z
    nodes = partial_ref.shape[-1]
    width = grad_ref.shape[-1]
    ends = [
        lax.axis_index("gy") == 0,
        lax.axis_index("gy") == lax.axis_size("gy") - 1,
        lax.axis_index("gz") == 0,
        lax.axis_index("gz") == lax.axis_size("gz") - 1,
    ]

    for f in range(fields):
        low_ref[f] = state_ref[:, :, f].reshape(rows, -1).astype(jnp.bfloat16)
    lanes = lane_index((3 * count_y, 3 * count_y * LANES))
    row = lax.broadcasted_iota(jnp.int32, lanes.shape, 0)
    pick = (lanes // LANES == row).astype(jnp.float32)
    medium = spread(material_ref[...].reshape(3 * count_y, count_z), 3 * count_y, pick)
    lanes = lane_index((6 * count_y, 3 * count_y * LANES))
    row = lax.broadcasted_iota(jnp.int32, lanes.shape, 0)
    block = lanes // LANES
    face = 2 * (block // count_y) + (lanes % LANES) // FACE
    pick = (face * count_y + block % count_y == row).astype(jnp.float32)
    codes = spread(
        orient_ref[...].reshape(6 * count_y, count_z).astype(jnp.float32), 6 * count_y, pick
    )
    kinds = spread(
        flags_ref[...].reshape(6 * count_y, count_z).astype(jnp.float32), 6 * count_y, pick
    )
    lane = lane_index((count_z, LANES))
    upper = lane >= FACE
    half_sign = jnp.where(upper, 0.5, -0.5)
    node = lane % FACE
    near, far = (node // NP, node % NP)
    z_pos = lax.broadcasted_iota(jnp.int32, lane.shape, 0)
    for y in range(count_y):
        lam = medium[:, y * LANES : (y + 1) * LANES]
        mu = medium[:, (count_y + y) * LANES : (count_y + y + 1) * LANES]
        rho = medium[:, (2 * count_y + y) * LANES : (2 * count_y + y + 1) * LANES]
        inv = 1.0 / rho
        wide_ref[0, y] = lam
        wide_ref[1, y] = mu
        wide_ref[2, y] = inv
        coef_ref[0, y] = half_sign * lam
        coef_ref[1, y] = half_sign * mu
        coef_ref[2, y] = half_sign * inv
        coef_ref[3, y] = 0.5 * jnp.sqrt((lam + 2.0 * mu) * inv)
        for d in range(3):
            at = (d * count_y + y) * LANES
            code = jnp.round(codes[:, at : at + LANES]).astype(jnp.int32)
            swap = code >= 4
            lead = jnp.where(swap, far, near)
            trail = jnp.where(swap, near, far)
            lead = jnp.where(code % 2 == 1, NP - 1 - lead, lead)
            trail = jnp.where((code // 2) % 2 == 1, NP - 1 - trail, trail)
            source_ref[d, y] = lead * NP + trail + jnp.where(upper, 0, FACE)
            if d > 0:
                free = jnp.where(jnp.round(kinds[:, at : at + LANES]) == 1.0, 1.0, 0.0)
                if d == 1:
                    low_end = (ends[0]) if y == 0 else False
                    high_end = (ends[1]) if y == count_y - 1 else False
                    rim = jnp.where(
                        upper,
                        jnp.where(high_end, 1.0, 0.0),
                        jnp.where(low_end, 1.0, 0.0),
                    )
                else:
                    low_rim = jnp.where(z_pos == 0, jnp.where(ends[2], 1.0, 0.0), 0.0)
                    high_rim = jnp.where(
                        z_pos == count_z - 1, jnp.where(ends[3], 1.0, 0.0), 0.0
                    )
                    rim = jnp.where(upper, high_rim, low_rim)
                edge_ref[d - 1, 0, y] = rim
                edge_ref[d - 1, 1, y] = free

    def columns_part(n, carry):
        base = n * width

        def operator(d):
            return deriv_ref[:, pl.ds(pl.multiple_of(d * nodes + base, LANES), width)]

        velocity = low_ref[0:3].reshape(3 * rows, nodes)
        for d in range(3):
            grad_ref[d] = jnp.dot(velocity, operator(d), preferred_element_type=jnp.float32)
        total = None
        for d in range(3):
            stress = jnp.concatenate([low_ref[stress_slot[i][d]] for i in range(3)], axis=0)
            part = jnp.dot(stress, operator(d), preferred_element_type=jnp.float32)
            total = part if total is None else total + part
        div_ref[...] = total
        for s in range(2):
            scale = step_size if s == 0 else -step_size
            for y in range(count_y):
                at = (s * count_y + y) * count_z
                lam = scale * wide_ref[0, y]
                mu = scale * wide_ref[1, y]
                inv = scale * wide_ref[2, y]
                for tile in range(width // LANES):
                    columns = slice(tile * LANES, (tile + 1) * LANES)
                    where = pl.ds(pl.multiple_of(base + tile * LANES, LANES), LANES)

                    def g(d, i):
                        return grad_ref[d, i * rows + at : i * rows + at + count_z, columns]

                    def put(f, term):
                        partial_ref[s, y, f, :, where] = state_ref[s, y, f, :, where] + term

                    for i in range(3):
                        put(i, inv * div_ref[i * rows + at : i * rows + at + count_z, columns])
                    diag = [g(i, i) for i in range(3)]
                    common = lam * (diag[0] + diag[1] + diag[2])
                    for i in range(3):
                        put(3 + i, common + (mu + mu) * diag[i])
                    for f, i, j in shear_pairs:
                        put(f, mu * (g(j, i) + g(i, j)))
        return carry

    lax.fori_loop(0, nodes // width, columns_part, 0)


def volume(state, deriv, material, orient, flags):
    _, count_y, fields, count_z, nodes = state.shape
    f32 = jnp.float32
    width = 256
    rows = 2 * count_y * count_z
    outs = (
        jax.ShapeDtypeStruct(state.shape, f32),
        jax.ShapeDtypeStruct((4, count_y, count_z, LANES), f32),
        jax.ShapeDtypeStruct((3, count_y, count_z, LANES), jnp.int32),
        jax.ShapeDtypeStruct((2, 2, count_y, count_z, LANES), f32),
    )
    return pl.pallas_call(
        volume_kernel,
        out_shape=outs,
        in_specs=[pl.BlockSpec(memory_space=pltpu.VMEM)] * 5,
        out_specs=(pl.BlockSpec(memory_space=pltpu.VMEM),) * 4,
        scratch_shapes=[
            pltpu.VMEM((fields, rows, nodes), jnp.bfloat16),
            pltpu.VMEM((3, 3 * rows, width), f32),
            pltpu.VMEM((3 * rows, width), f32),
            pltpu.VMEM((3, count_y, count_z, LANES), f32),
        ],
        compiler_params=pltpu.CompilerParams(vmem_limit_bytes=LIMIT),
        cost_estimate=pl.CostEstimate(
            flops=10**6, bytes_accessed=10**5, transcendentals=0
        ),
        name="volume",
    )(state, deriv, material, orient, flags)


def final_kernel(
    state_ref, trace_ref, far_ref, near_ref, y_two, y_one, z_two, z_one,
    coef_ref, source_ref, edge_ref, partial_ref, stored_ref, lift_ref,
    advanced_ref, kernel_ref,
    flux_ref, sum_ref, out_ref, out_sem,
):
    count_y, fields, count_z, nodes = state_ref.shape[1:]
    last_y = count_y - 1
    odd_x = odd_position("gx")
    odd_y = odd_position("gy")
    odd_z = odd_position("gz")
    lane = lane_index((count_z, LANES))
    upper = lane >= FACE
    z_pos = lax.broadcasted_iota(jnp.int32, lane.shape, 0)
    take_near = upper == odd_x

    def write(y):
        return pltpu.make_async_copy(out_ref.at[:, y], advanced_ref.at[:, y], out_sem.at[y])

    def row(y, carry):
        below = jnp.maximum(y - 1, 0)
        above = jnp.minimum(y + 1, last_y)
        lam, mu, inv, speed = [coef_ref[k, y] for k in range(4)]
        for s in range(2):
            for d in range(3):
                source = source_ref[d, y]
                if d == 0 and s == 1:
                    source = (source + FACE) % LANES
                if d > 0:
                    rim = edge_ref[d - 1, 0, y] > 0.0
                    free = edge_ref[d - 1, 1, y]
                    keep_velocity = free - 1.0
                    keep_stress = -free - 1.0
                jumps = []
                for f in range(fields):
                    if d == 0:
                        inside = jnp.where(
                            upper, state_ref[s, y, f, :, nodes - LANES :], state_ref[s, y, f, :, :LANES]
                        )
                        near, far = (near_ref[y, f], far_ref[y, f])
                        if s == 1:
                            near, far = (far, near)
                        mixed = jnp.where(take_near, near, far)
                    elif d == 1:
                        inside = trace_ref[s, y, f, :, :LANES]
                        two, one = (y_two[f], y_one[f])
                        from_below = jnp.where(odd_y, one, two)
                        from_above = jnp.where(odd_y, two, one)
                        if s == 1:
                            from_below = pltpu.roll(from_below, FACE, 1)
                            from_above = pltpu.roll(from_above, FACE, 1)
                        lower = jnp.where(y == 0, from_below, trace_ref[s, below, f, :, :LANES])
                        higher = jnp.where(y == last_y, from_above, trace_ref[s, above, f, :, :LANES])
                        mixed = jnp.where(upper, lower, higher)
                    else:
                        inside = trace_ref[s, y, f, :, LANES:]
                        two = jnp.broadcast_to(z_two[y, f : f + 1, :], lane.shape)
                        one = jnp.broadcast_to(z_one[y, f : f + 1, :], lane.shape)
                        from_below = jnp.where(odd_z, one, two)
                        from_above = jnp.where(odd_z, two, one)
                        if s == 1:
                            from_below = pltpu.roll(from_below, FACE, 1)
                            from_above = pltpu.roll(from_above, FACE, 1)
                        lower = jnp.where(z_pos == 0, from_below, pltpu.roll(inside, 1, 0))
                        higher = jnp.where(
                            z_pos == count_z - 1, from_above, pltpu.roll(inside, count_z - 1, 0)
                        )
                        mixed = jnp.where(upper, lower, higher)
                    turned = jnp.take_along_axis(mixed, source, axis=1)
                    jump = turned - inside
                    if d > 0:
                        keep = keep_velocity if f < 3 else keep_stress
                        jump = jnp.where(rim, inside * keep, jump)
                    jumps.append(jump)
                    if s == 1:
                        term = stored_ref[y, f, :, d * LANES : (d + 1) * LANES] * jump
                        if d == 0:
                            sum_ref[f] = term
                        else:
                            sum_ref[f] += term
                flux = [speed * jump for jump in jumps]
                for i in range(3):
                    flux[i] = flux[i] + inv * jumps[stress_slot[i][d]]
                common = lam * jumps[d]
                for i in range(3):
                    flux[3 + i] = flux[3 + i] + common
                for i, j, f in ((0, 0, 3), (1, 1, 4), (2, 2, 5), (1, 2, 6), (0, 2, 7), (0, 1, 8)):
                    if j == d:
                        flux[f] = flux[f] + mu * jumps[i]
                    if i == d:
                        flux[f] = flux[f] + mu * jumps[j]
                for f in range(fields):
                    flux_ref[s, f, :, d * LANES : (d + 1) * LANES] = flux[f].astype(jnp.bfloat16)
        lifted = jnp.dot(
            flux_ref[...].reshape(2 * fields * count_z, 3 * LANES),
            lift_ref[...],
            preferred_element_type=jnp.float32,
        ).reshape(2, fields, count_z, nodes)
        for s in range(2):
            scale = step_size if s == 0 else -step_size
            out_ref[s, y] = partial_ref[s, y] + scale * lifted[s]
        write(y).start()
        for f in range(fields):
            sums = jnp.sum(sum_ref[f], axis=1, keepdims=True) * (1.0 / FACE)
            across = jnp.sum(jnp.where(z_pos == lane, sums, 0.0), axis=0, keepdims=True)
            kernel_ref[f, pl.ds(y, 1), :] = across[:, :count_z]
        return carry

    lax.fori_loop(0, count_y, row, 0)
    for y in range(count_y):
        write(y).wait()


def finish(
    state, traces, far, near, y_two, y_one, z_two, z_one, coef, source, edge, part, stored, lift
):
    _, count_y, fields, count_z, nodes = state.shape
    f32 = jnp.float32
    outs = (
        jax.ShapeDtypeStruct(state.shape, f32),
        jax.ShapeDtypeStruct((fields, count_y, count_z), f32),
    )
    return pl.pallas_call(
        final_kernel,
        out_shape=outs,
        in_specs=[pl.BlockSpec(memory_space=pltpu.VMEM)] * 14,
        out_specs=(pl.BlockSpec(memory_space=pl.ANY), pl.BlockSpec(memory_space=pltpu.VMEM)),
        scratch_shapes=[
            pltpu.VMEM((2, fields, count_z, 3 * LANES), jnp.bfloat16),
            pltpu.VMEM((fields, count_z, LANES), f32),
            pltpu.VMEM(state.shape, f32),
            pltpu.SemaphoreType.DMA((count_y,)),
        ],
        compiler_params=pltpu.CompilerParams(vmem_limit_bytes=LIMIT),
        cost_estimate=pl.CostEstimate(flops=9 * 10**8, bytes_accessed=10**7, transcendentals=0),
        name="finish",
    )(state, traces, far, near, y_two, y_one, z_two, z_one, coef, source, edge, part, stored, lift)


def swaps(count, start, wrap):
    pairs = []
    for i in range(start, count if wrap else count - 1, 2):
        j = (i + 1) % count
        pairs += [(i, j), (j, i)]
    return pairs


def local(state, deriv, lift, material, stored, orient, flags):
    view = jnp.transpose(state[:, 0], (0, 1, 3, 2, 4))
    stored_view = jnp.transpose(stored[0], (0, 2, 1, 3))
    orient_view = jnp.transpose(orient[0], (2, 0, 1))
    flags_view = jnp.transpose(flags[0], (2, 0, 1))
    nx, ny, nz = (lax.axis_size(a) for a in ("gx", "gy", "gz"))
    table = jnp.asarray(trace_table(), jnp.bfloat16)
    far, near = pack_faces(view)
    far, near, table, state = lax.optimization_barrier((far, near, table, state))
    view = jnp.transpose(state[:, 0], (0, 1, 3, 2, 4))
    far_in = lax.ppermute(far, "gx", swaps(nx, 1, True))
    near_in = lax.ppermute(near, "gx", swaps(nx, 0, True))
    traces, y_two, y_one, z_two, z_one = extract_traces(view, table)
    y_one = lax.ppermute(y_one, "gy", swaps(ny, 0, False))
    y_two = lax.ppermute(y_two, "gy", swaps(ny, 1, False))
    z_one = lax.ppermute(z_one, "gz", swaps(nz, 0, False))
    medium = material[:, 0]
    z_two, medium, y_one = lax.optimization_barrier((z_two, medium, y_one))
    z_two = lax.ppermute(z_two, "gz", swaps(nz, 1, False))
    part, coef, source, edge = volume(view, deriv, medium, orient_view, flags_view)
    advanced, kernel = finish(
        view, traces, far_in, near_in, y_two, y_one, z_two, z_one, coef, source, edge, part,
        stored_view, lift,
    )
    return (
        jnp.transpose(advanced, (0, 1, 3, 2, 4))[:, None],
        jnp.transpose(kernel, (1, 2, 0))[None],
    )


def solution(mesh):
    placed = (
        P(None, "gx", "gy", "gz", None, None),
        P(),
        P(),
        P(None, "gx", "gy", "gz"),
        P("gx", "gy", "gz", None, None),
        P("gx", "gy", "gz", None),
        P("gx", "gy", "gz", None),
    )
    return jax.shard_map(
        local,
        mesh=mesh,
        in_specs=placed,
        out_specs=(P(None, "gx", "gy", "gz", None, None), P("gx", "gy", "gz", None)),
        check_vma=False,
    )
```

time: 27.5 us -> 26.1 us (0.949)
  waiting for transfers between devices: 3.91 us -> 0.02 us
  starting transfers between devices: 12.5 us -> 14.1 us
  Pallas kernels: 8.42 us -> 9.98 us
  local copies, waits for them, and re-layouts: 1.69 us -> 0.98 us
    ppermute x1, waiting for transfers between devices: 2.03 us -> 0.01 us  [local(): z_one = lax.ppermute(z_one, 'gz', swaps(nz, 0, False))]
    ppermute x1, waiting for transfers between devices: 1.87 us -> 0.01 us  [local(): z_two = lax.ppermute(z_two, 'gz', swaps(nz, 1, False))]
    pallas_call x2 -> x3, Pallas kernels: 4.31 us -> 5.87 us  [the longest x1 2.51 us: volume(): pl.pallas_call(volume_kernel, out_shape=outs, in_specs=[pl.BlockSpec(memo...]
    ppermute x1, starting transfers between devices: 3.83 us -> 5.33 us  [local(): z_two = lax.ppermute(z_two, 'gz', swaps(nz, 1, False))]
    unnamed x16, local copies, waits for them, and re-layouts: 1.69 us -> 0.98 us
  transfers between devices with their start and end apart: 6 -> 6, of which waited for: 2 -> 0; matrix products, arithmetic and copies ran while one was open for 0% -> 0% of each run, Pallas kernels for 14% -> 14%
where the time goes in v3:
time: 26.1 us; the launch traced here: 25.9 us
  starting transfers between devices  14.1 us (54%)
  Pallas kernels  9.98 us (38%)
  local copies, waits for them, and re-layouts  0.98 us (4%)
  between operations  0.8 us (3%)
    ppermute x1, starting transfers between devices, local(): z_two = lax.ppermute(z_two, 'gz', swaps(nz, 1, False))  5.33 us
    pallas_call x1, Pallas kernels, finish(): pl.pallas_call(final_kernel, out_shape=outs, in_specs=[pl.BlockSpec(memor...  4.11 us
    ppermute x1, starting transfers between devices, local(): near_in = lax.ppermute(near, 'gx', swaps(nx, 0, True))  3.45 us
    ppermute x1, starting transfers between devices, local(): y_two = lax.ppermute(y_two, 'gy', swaps(ny, 1, False))  3.43 us
    pallas_call x1, Pallas kernels, volume(): pl.pallas_call(volume_kernel, out_shape=outs, in_specs=[pl.BlockSpec(memo...  2.51 us
    pallas_call x1, Pallas kernels, pack_faces(): pl.pallas_call(pack_kernel, out_shape=(message, message), in_specs=[pl.Bl...  2.28 us
    ppermute x1, starting transfers between devices, local(): far_in = lax.ppermute(far, 'gx', swaps(nx, 1, True))  1.66 us
    pallas_call x1, Pallas kernels, extract_traces(): pl.pallas_call(trace_kernel, out_shape=(jax.ShapeDtypeStruct((2, count_y,...  1.08 us
  transfers between devices with their start and end apart: 6, of which 0 were waited for; matrix products, arithmetic and copies ran while one was open for 0% of the time, Pallas kernels for 14%

profile of v3, /device:TPU:42, one launch (start us, length us, event | category | flops | bytes accessed | tf_op | source)
XLA Modules:
  0.0 25.9 jit_solution(4646688206695888230)
XLA Ops:
  0.6 0.0 copy-start
  0.6 0.0 copy-start.1
  0.6 2.3 %pack_faces.1 = (f32[4,9,16,128]{3,2,1,0:T(8,128)}, f32[4,9,16,128]{3,2,1,0:T(8,128)}) custom-call(f32[2,4,9,16,512]{4,3,2,1,0:T(8,128)} %bitcast.24), custom_call_target="tpu_custom_call" | custom-call | flops 1000000 | bytes 2000000 | tf_op jit(solution)/shard_map/pack_faces/pallas_call | solution.py:83
  2.9 1.7 %collective-permute-start = (f32[4,9,16,128]{3,2,1,0:T(8,128)}, f32[4,9,16,128]{3,2,1,0:T(8,128)S(1)}, u32[]{:S(2)}, u32[]{:S(2)}) collective-permute-start(f32[4,9,16,128]{3,2,1,0:T(8,128)} %get-tuple-element.27), channel_id=1, source_target_pairs={{16,32},{32,16},{48,64},{64,48},{80,96},{96,80},{112,0},{0,112},{1... | collective-permute-start | bytes 884744 | tf_op jit(solution)/shard_map/ppermute | solution.py:473
  4.6 3.4 %collective-permute-start.1 = (f32[4,9,16,128]{3,2,1,0:T(8,128)}, f32[4,9,16,128]{3,2,1,0:T(8,128)S(1)}, u32[]{:S(2)}, u32[]{:S(2)}) collective-permute-start(f32[4,9,16,128]{3,2,1,0:T(8,128)} %get-tuple-element.28), channel_id=1, source_target_pairs={{0,16},{16,0},{32,48},{48,32},{64,80},{80,64},{96,112},{112,96},{1... | collective-permute-start | bytes 884744 | tf_op jit(solution)/shard_map/ppermute | solution.py:474
  8.0 0.0 copy-done
  8.0 0.0 copy-start.4
  8.1 0.9 %copy-done.4 = bf16[512,256]{1,0:T(8,128)(2,1)S(1)} copy-done((bf16[512,256]{1,0:T(8,128)(2,1)S(1)}, bf16[512,256]{1,0:T(8,128)(2,1)}, u32[]{:S(2)}) %copy-start.4) | copy-done | bytes 262168
  9.0 0.0 copy-start.5
  9.0 0.0 copy-start.6
  9.0 0.0 copy-start.7
  9.0 1.1 %extract_traces.1 = (f32[2,4,9,16,256]{4,3,2,1,0:T(8,128)S(1)}, f32[9,16,128]{2,1,0:T(8,128)S(1)}, f32[9,16,128]{2,1,0:T(8,128)S(1)}, f32[4,9,128]{2,1,0:T(8,128)S(1)}, f32[4,9,128]{2,1,0:T(8,128)S(1)}) custom-call(f32[2,4,9,16,512]{4,3,2,1,0:T(8,128)S(1)} %bitcast.25, bf16[512,256]{1,0:T(8,128)(2,1)S(1)} %copy-done.4), custom_call_target="tpu_custom_call" | custom-call | flops 600000000 | bytes 4000000 | tf_op jit(solution)/shard_map/extract_traces/pallas_call | solution.py:135
  10.1 0.0 copy-start.2
  10.1 0.0 copy-start.3
  10.1 0.1 collective-permute-start.3
  10.2 3.4 %collective-permute-start.2 = (f32[9,16,128]{2,1,0:T(8,128)S(1)}, f32[9,16,128]{2,1,0:T(8,128)S(1)}, u32[]{:S(2)}, u32[]{:S(2)}) collective-permute-start(f32[9,16,128]{2,1,0:T(8,128)S(1)} %get-tuple-element.29), channel_id=1, source_target_pairs={{4,8},{8,4},{5,9},{9,5},{6,10},{10,6},{7,11},{11,7},{20,24},{24,20... | collective-permute-start | bytes 221192 | tf_op jit(solution)/shard_map/ppermute | solution.py:477
  13.6 0.2 collective-permute-start.5
  13.8 0.0 collective-permute-done.3.y_one
  13.8 5.3 %collective-permute-start.4 = (f32[4,9,128]{2,1,0:T(8,128)S(1)}, f32[4,9,128]{2,1,0:T(8,128)S(1)}, u32[]{:S(2)}, u32[]{:S(2)}) collective-permute-start(f32[4,9,128]{2,1,0:T(8,128)S(1)} %get-tuple-element.33), channel_id=1, source_target_pairs={{1,2},{2,1},{5,6},{6,5},{9,10},{10,9},{13,14},{14,13},{17,18},{18,... | collective-permute-start | bytes 55304 | tf_op jit(solution)/shard_map/ppermute | solution.py:481
  19.2 0.0 copy-done.1
  19.2 0.0 copy-done.5
  19.2 0.0 copy-done.6
  19.2 0.0 copy-done.7
  19.2 2.5 %volume.1 = (f32[2,4,9,16,512]{4,3,2,1,0:T(8,128)S(1)}, f32[4,4,16,128]{3,2,1,0:T(8,128)S(1)}, s32[3,4,16,128]{3,2,1,0:T(8,128)S(1)}, f32[2,2,4,16,128]{4,3,2,1,0:T(8,128)S(1)}) custom-call(f32[2,4,9,16,512]{4,3,2,1,0:T(8,128)S(1)} %bitcast.26, bf16[512,1536]{1,0:T(8,128)(2,1)S(1)} %copy-done.1, f32[3,4,16]{2,1,0:T(4,128)S(1)} %bitcast.31, ...), custom_call_target="tpu_custom_call" | custom-call | flops 1000000 | bytes 100000 | tf_op jit(solution)/shard_map/volume/pallas_call | solution.py:297
  21.7 0.0 collective-permute-done.5.z_one
  21.7 0.0 collective-permute-done.2.y_two
  21.8 0.0 collective-permute-done.4.z_two
  21.8 0.0 collective-permute-done.far_ref
  21.8 0.0 collective-permute-done.1.near_ref
  21.8 0.0 copy-done.2
  21.8 0.0 copy-done.3
  21.8 4.1 %finish.1 = (f32[2,4,9,16,512]{4,3,2,1,0:T(8,128)}, f32[9,4,16]{2,1,0:T(4,128)}) custom-call(f32[2,4,9,16,512]{4,3,2,1,0:T(8,128)S(1)} %bitcast.27, f32[2,4,9,16,256]{4,3,2,1,0:T(8,128)S(1)} %get-tuple-element.26.trace_ref, f32[4,9,16,128]{3,2,1,0:T(8,128)S(1)} %collective-permute-done.far_ref, f32[4,9,16,128]{3,2,1,0:T(8,128)S(1)} %collective-permute-done.1.near_ref, ...), custom_call_target="tpu_custom_call" | custom-call | flops 900000000 | bytes 10000000 | tf_op jit(solution)/shard_map/finish/pallas_call | solution.py:438
Async XLA Ops:
  0.6 7.4 %copy-start = (f32[2,1,4,16,9,512]{5,3,4,2,1,0:T(8,128)S(1)}, f32[2,1,4,16,9,512]{5,3,4,2,1,0:T(8,128)}, u32[]{:S(2)}) copy-start(f32[2,1,4,16,9,512]{5,3,4,2,1,0:T(8,128)} %param.8) | copy-start | bytes 7077892
  0.6 18.5 %copy-start.1 = (bf16[512,1536]{1,0:T(8,128)(2,1)S(1)}, bf16[512,1536]{1,0:T(8,128)(2,1)}, u32[]{:S(2)}) copy-start(bf16[512,1536]{1,0:T(8,128)(2,1)} %deriv_ref.1) | copy-start | bytes 4718596
  2.9 18.8 %collective-permute-start = (f32[4,9,16,128]{3,2,1,0:T(8,128)}, f32[4,9,16,128]{3,2,1,0:T(8,128)S(1)}, u32[]{:S(2)}, u32[]{:S(2)}) collective-permute-start(f32[4,9,16,128]{3,2,1,0:T(8,128)} %get-tuple-element.27), channel_id=1, source_target_pairs={{16,32},{32,16},{48,64},{64,48},{80,96},{96,80},{112,0},{0,112},{1... | collective-permute-start | bytes 884744 | tf_op jit(solution)/shard_map/ppermute | solution.py:473
  4.6 17.2 %collective-permute-start.1 = (f32[4,9,16,128]{3,2,1,0:T(8,128)}, f32[4,9,16,128]{3,2,1,0:T(8,128)S(1)}, u32[]{:S(2)}, u32[]{:S(2)}) collective-permute-start(f32[4,9,16,128]{3,2,1,0:T(8,128)} %get-tuple-element.28), channel_id=1, source_target_pairs={{0,16},{16,0},{32,48},{48,32},{64,80},{80,64},{96,112},{112,96},{1... | collective-permute-start | bytes 884744 | tf_op jit(solution)/shard_map/ppermute | solution.py:474
  8.0 1.0 %copy-start.4 = (bf16[512,256]{1,0:T(8,128)(2,1)S(1)}, bf16[512,256]{1,0:T(8,128)(2,1)}, u32[]{:S(2)}) copy-start(bf16[512,256]{1,0:T(8,128)(2,1)} %constant.2.clone.table_ref) | copy-start | bytes 786436
  9.0 10.2 %copy-start.5 = (s32[1,4,16,6]{2,1,3,0:T(4,128)S(1)}, s32[1,4,16,6]{2,1,3,0:T(4,128)}, u32[]{:S(2)}) copy-start(s32[1,4,16,6]{2,1,3,0:T(4,128)} %param.13) | copy-start | bytes 4612
  9.0 10.2 %copy-start.6 = (s32[1,4,16,6]{2,1,3,0:T(4,128)S(1)}, s32[1,4,16,6]{2,1,3,0:T(4,128)}, u32[]{:S(2)}) copy-start(s32[1,4,16,6]{2,1,3,0:T(4,128)} %param.14) | copy-start | bytes 4612
  9.0 10.2 %copy-start.7 = (f32[3,1,4,16]{3,2,1,0:T(4,128)S(1)}, f32[3,1,4,16]{3,2,1,0:T(4,128)}, u32[]{:S(2)}) copy-start(f32[3,1,4,16]{3,2,1,0:T(4,128)} %param.11) | copy-start | bytes 2308
  10.1 11.7 %copy-start.2 = (f32[1,4,16,9,384]{4,2,3,1,0:T(8,128)S(1)}, f32[1,4,16,9,384]{4,2,3,1,0:T(8,128)}, u32[]{:S(2)}) copy-start(f32[1,4,16,9,384]{4,2,3,1,0:T(8,128)} %param.12) | copy-start | bytes 2654212
  10.1 11.7 %copy-start.3 = (bf16[384,512]{1,0:T(8,128)(2,1)S(1)}, bf16[384,512]{1,0:T(8,128)(2,1)}, u32[]{:S(2)}) copy-start(bf16[384,512]{1,0:T(8,128)(2,1)} %lift_ref.1) | copy-start | bytes 1179652
  10.1 3.7 %collective-permute-start.3 = (f32[9,16,128]{2,1,0:T(8,128)S(1)}, f32[9,16,128]{2,1,0:T(8,128)S(1)}, u32[]{:S(2)}, u32[]{:S(2)}) collective-permute-start(f32[9,16,128]{2,1,0:T(8,128)S(1)} %get-tuple-element.31), channel_id=1, source_target_pairs={{0,4},{4,0},{8,12},{12,8},{1,5},{5,1},{9,13},{13,9},{2,6},{6,2},{1... | collective-permute-start | bytes 221192 | tf_op jit(solution)/shard_map/ppermute | solution.py:476
  10.2 11.5 %collective-permute-start.2 = (f32[9,16,128]{2,1,0:T(8,128)S(1)}, f32[9,16,128]{2,1,0:T(8,128)S(1)}, u32[]{:S(2)}, u32[]{:S(2)}) collective-permute-start(f32[9,16,128]{2,1,0:T(8,128)S(1)} %get-tuple-element.29), channel_id=1, source_target_pairs={{4,8},{8,4},{5,9},{9,5},{6,10},{10,6},{7,11},{11,7},{20,24},{24,20... | collective-permute-start | bytes 221192 | tf_op jit(solution)/shard_map/ppermute | solution.py:477
  13.6 8.1 %collective-permute-start.5 = (f32[4,9,128]{2,1,0:T(8,128)S(1)}, f32[4,9,128]{2,1,0:T(8,128)S(1)}, u32[]{:S(2)}, u32[]{:S(2)}) collective-permute-start(f32[4,9,128]{2,1,0:T(8,128)S(1)} %get-tuple-element.34), channel_id=1, source_target_pairs={{0,1},{1,0},{2,3},{3,2},{4,5},{5,4},{6,7},{7,6},{8,9},{9,8},{10,11... | collective-permute-start | bytes 55304 | tf_op jit(solution)/shard_map/ppermute | solution.py:478
  13.8 7.9 %collective-permute-start.4 = (f32[4,9,128]{2,1,0:T(8,128)S(1)}, f32[4,9,128]{2,1,0:T(8,128)S(1)}, u32[]{:S(2)}, u32[]{:S(2)}) collective-permute-start(f32[4,9,128]{2,1,0:T(8,128)S(1)} %get-tuple-element.33), channel_id=1, source_target_pairs={{1,2},{2,1},{5,6},{6,5},{9,10},{10,9},{13,14},{14,13},{17,18},{18,... | collective-permute-start | bytes 55304 | tf_op jit(solution)/shard_map/ppermute | solution.py:481

commit v4 on v3

--- a/solution.py
+++ b/solution.py
@@ -14,7 +14,7 @@
 stress_slot = ((3, 8, 7), (8, 4, 6), (7, 6, 5))
 shear_pairs = ((6, 1, 2), (7, 0, 2), (8, 0, 1))
 LIMIT = 20 * 1024 * 1024
-PACK_LIMIT = 56 * 1024 * 1024
+PACK_LIMIT = 50 * 1024 * 1024
 
 
 def trace_table():
@@ -45,36 +45,29 @@
     return lax.axis_index(axis) % 2 == 1
 
 
-def pack_kernel(state_ref, far_ref, near_ref, held_ref, ready_ref, sem, out_sem):
+def pack_kernel(state_ref, held_ref, far_ref, near_ref, sem):
     odd = odd_position("gx")
-    last = state_ref.shape[-1] - LANES
-    part = held_ref.shape[3]
-    chunks = [(h, c) for h in range(2) for c in range(2)]
-
-    def fetch(h, c):
-        first_tile = odd if h == 1 else jnp.logical_not(odd)
-        at = pl.multiple_of(jnp.where(first_tile, 0, last), LANES)
+    tiles = state_ref.shape[-1] // LANES
+    order = [0, tiles - 1] + list(range(1, tiles - 1))
+
+    def fetch(t):
+        columns = pl.ds(t * LANES, LANES)
         return pltpu.make_async_copy(
-            state_ref.at[:, pl.ds(c * part, part), :, :, pl.ds(at, LANES)],
-            held_ref.at[h, c],
-            sem.at[h, c],
+            state_ref.at[:, :, :, :, columns], held_ref.at[:, :, :, :, columns], sem.at[t]
         )
 
-    def deliver(h, c):
-        target = (far_ref, near_ref)[h]
-        return pltpu.make_async_copy(
-            ready_ref.at[h, c], target.at[pl.ds(c * part, part)], out_sem.at[h, c]
-        )
-
-    for h, c in chunks:
-        fetch(h, c).start()
-    for h, c in chunks:
-        fetch(h, c).wait()
-        upper = jnp.logical_not(odd) if h == 1 else odd
-        ready_ref[h, c] = merged(held_ref[h, c, 0], held_ref[h, c, 1], upper)
-        deliver(h, c).start()
-    for h, c in chunks:
-        deliver(h, c).wait()
+    for t in order:
+        fetch(t).start()
+    for t in order[:2]:
+        fetch(t).wait()
+    low, high = slice(0, LANES), slice((tiles - 1) * LANES, tiles * LANES)
+    for y in range(far_ref.shape[0]):
+        down = merged(held_ref[0, y, :, :, low], held_ref[1, y, :, :, low], False)
+        up = merged(held_ref[0, y, :, :, high], held_ref[1, y, :, :, high], True)
+        far_ref[y] = jnp.where(odd, up, down)
+        near_ref[y] = jnp.where(odd, down, up)
+    for t in order[2:]:
+        fetch(t).wait()
 
 
 def pack_faces(state):
@@ -82,15 +75,10 @@
     message = jax.ShapeDtypeStruct((count_y, fields, count_z, LANES), jnp.float32)
     return pl.pallas_call(
         pack_kernel,
-        out_shape=(message, message),
+        out_shape=(jax.ShapeDtypeStruct(state.shape, jnp.float32), message, message),
         in_specs=[pl.BlockSpec(memory_space=pl.ANY)],
-        out_specs=(pl.BlockSpec(memory_space=pl.ANY),) * 2,
-        scratch_shapes=[
-            pltpu.VMEM((2, 2, 2, count_y // 2, fields, count_z, LANES), jnp.float32),
-            pltpu.VMEM((2, 2, count_y // 2, fields, count_z, LANES), jnp.float32),
-            pltpu.SemaphoreType.DMA((2, 2)),
-            pltpu.SemaphoreType.DMA((2, 2)),
-        ],
+        out_specs=(pl.BlockSpec(memory_space=pltpu.VMEM),) * 3,
+        scratch_shapes=[pltpu.SemaphoreType.DMA((nodes // LANES,))],
         compiler_params=pltpu.CompilerParams(vmem_limit_bytes=PACK_LIMIT),
         cost_estimate=pl.CostEstimate(flops=10**6, bytes_accessed=2 * 10**6, transcendentals=0),
         name="pack_faces",
@@ -467,18 +455,16 @@
     flags_view = jnp.transpose(flags[0], (2, 0, 1))
     nx, ny, nz = (lax.axis_size(a) for a in ("gx", "gy", "gz"))
     table = jnp.asarray(trace_table(), jnp.bfloat16)
-    far, near = pack_faces(view)
-    far, near, table, state = lax.optimization_barrier((far, near, table, state))
-    view = jnp.transpose(state[:, 0], (0, 1, 3, 2, 4))
+    view, far, near = pack_faces(view)
     far_in = lax.ppermute(far, "gx", swaps(nx, 1, True))
     near_in = lax.ppermute(near, "gx", swaps(nx, 0, True))
     traces, y_two, y_one, z_two, z_one = extract_traces(view, table)
     y_one = lax.ppermute(y_one, "gy", swaps(ny, 0, False))
-    y_two = lax.ppermute(y_two, "gy", swaps(ny, 1, False))
+    y_two = lax.ppermute(y_two, "gy", swaps(ny, 1, True))
     z_one = lax.ppermute(z_one, "gz", swaps(nz, 0, False))
     medium = material[:, 0]
     z_two, medium, y_one = lax.optimization_barrier((z_two, medium, y_one))
-    z_two = lax.ppermute(z_two, "gz", swaps(nz, 1, False))
+    z_two = lax.ppermute(z_two, "gz", swaps(nz, 1, True))
     part, coef, source, edge = volume(view, deriv, medium, orient_view, flags_view)
     advanced, kernel = finish(
         view, traces, far_in, near_in, y_two, y_one, z_two, z_one, coef, source, edge, part,

time: 26.1 us -> 22.3 us (0.85)
  the two profiles are of different devices: /device:TPU:42 before, /device:TPU:1 now
where the time goes in v4:
time: 22.3 us; the launch traced here: 22.2 us
  starting transfers between devices  11.8 us (53%)
  Pallas kernels  9.48 us (43%)
  between operations  0.75 us (3%)
    ppermute x1, starting transfers between devices, local(): far_in = lax.ppermute(far, 'gx', swaps(nx, 1, True))  6.1 us
    pallas_call x1, Pallas kernels, finish(): pl.pallas_call(final_kernel, out_shape=outs, in_specs=[pl.BlockSpec(memor...  4.11 us
    ppermute x1, starting transfers between devices, local(): z_two = lax.ppermute(z_two, 'gz', swaps(nz, 1, True))  2.75 us
    pallas_call x1, Pallas kernels, volume(): pl.pallas_call(volume_kernel, out_shape=outs, in_specs=[pl.BlockSpec(memo...  2.5 us
    pallas_call x1, Pallas kernels, pack_faces(): pl.pallas_call(pack_kernel, out_shape=(jax.ShapeDtypeStruct(state.shape,...  1.79 us
    ppermute x1, starting transfers between devices, local(): z_one = lax.ppermute(z_one, 'gz', swaps(nz, 0, False))  1.65 us
    pallas_call x1, Pallas kernels, extract_traces(): pl.pallas_call(trace_kernel, out_shape=(jax.ShapeDtypeStruct((2, count_y,...  1.08 us
    ppermute x1, starting transfers between devices, local(): y_one = lax.ppermute(y_one, 'gy', swaps(ny, 0, False))  1.04 us
  transfers between devices with their start and end apart: 6, of which 1 were waited for; matrix products, arithmetic and copies ran while one was open for 0% of the time, Pallas kernels for 16%

profile of v4, /device:TPU:1, one launch (start us, length us, event | category | flops | bytes accessed | tf_op | source)
XLA Modules:
  0.0 22.2 jit_solution(3690256798028036915)
XLA Ops:
  0.6 0.0 copy-start.3
  0.6 0.0 copy-start
  0.7 0.0 copy-start.4
  0.7 0.0 copy-start.5
  0.7 0.0 copy-start.6
  0.7 1.8 %pack_faces.1 = (f32[2,4,9,16,512]{4,3,2,1,0:T(8,128)S(1)}, f32[4,9,16,128]{3,2,1,0:T(8,128)S(1)}, f32[4,9,16,128]{3,2,1,0:T(8,128)S(1)}) custom-call(f32[2,4,9,16,512]{4,3,2,1,0:T(8,128)} %bitcast.25), custom_call_target="tpu_custom_call" | custom-call | flops 1000000 | bytes 2000000 | tf_op jit(solution)/shard_map/pack_faces/pallas_call | solution.py:76
  2.5 6.1 %collective-permute-start = (f32[4,9,16,128]{3,2,1,0:T(8,128)S(1)}, f32[4,9,16,128]{3,2,1,0:T(8,128)S(1)}, u32[]{:S(2)}, u32[]{:S(2)}) collective-permute-start(f32[4,9,16,128]{3,2,1,0:T(8,128)S(1)} %get-tuple-element.21), channel_id=1, source_target_pairs={{16,32},{32,16},{48,64},{64,48},{80,96},{96,80},{112,0},{0,112},{1... | collective-permute-start | bytes 884744 | tf_op jit(solution)/shard_map/ppermute | solution.py:459
  8.6 0.0 collective-permute-start.1
  8.6 0.0 copy-done.3
  8.6 1.1 %extract_traces.1 = (f32[2,4,9,16,256]{4,3,2,1,0:T(8,128)S(1)}, f32[9,16,128]{2,1,0:T(8,128)S(1)}, f32[9,16,128]{2,1,0:T(8,128)S(1)}, f32[4,9,128]{2,1,0:T(8,128)S(1)}, f32[4,9,128]{2,1,0:T(8,128)S(1)}) custom-call(f32[2,4,9,16,512]{4,3,2,1,0:T(8,128)S(1)} %get-tuple-element.19.state_ref, bf16[512,256]{1,0:T(8,128)(2,1)S(1)} %copy-done.3), custom_call_target="tpu_custom_call" | custom-call | flops 600000000 | bytes 4000000 | tf_op jit(solution)/shard_map/extract_traces/pallas_call | solution.py:123
  9.7 0.0 copy-start.1
  9.7 0.0 copy-start.2
  9.7 1.0 %collective-permute-start.3 = (f32[9,16,128]{2,1,0:T(8,128)S(1)}, f32[9,16,128]{2,1,0:T(8,128)S(1)}, u32[]{:S(2)}, u32[]{:S(2)}) collective-permute-start(f32[9,16,128]{2,1,0:T(8,128)S(1)} %get-tuple-element.25), channel_id=1, source_target_pairs={{0,4},{4,0},{8,12},{12,8},{1,5},{5,1},{9,13},{13,9},{2,6},{6,2},{1... | collective-permute-start | bytes 221192 | tf_op jit(solution)/shard_map/ppermute | solution.py:462
  10.7 0.3 %collective-permute-start.2 = (f32[9,16,128]{2,1,0:T(8,128)S(1)}, f32[9,16,128]{2,1,0:T(8,128)S(1)}, u32[]{:S(2)}, u32[]{:S(2)}) collective-permute-start(f32[9,16,128]{2,1,0:T(8,128)S(1)} %get-tuple-element.23), channel_id=1, source_target_pairs={{4,8},{8,4},{12,0},{0,12},{5,9},{9,5},{13,1},{1,13},{6,10},{10,6},... | collective-permute-start | bytes 221192 | tf_op jit(solution)/shard_map/ppermute | solution.py:463
  11.0 1.6 %collective-permute-start.5 = (f32[4,9,128]{2,1,0:T(8,128)S(1)}, f32[4,9,128]{2,1,0:T(8,128)S(1)}, u32[]{:S(2)}, u32[]{:S(2)}) collective-permute-start(f32[4,9,128]{2,1,0:T(8,128)S(1)} %get-tuple-element.28), channel_id=1, source_target_pairs={{0,1},{1,0},{2,3},{3,2},{4,5},{5,4},{6,7},{7,6},{8,9},{9,8},{10,11... | collective-permute-start | bytes 55304 | tf_op jit(solution)/shard_map/ppermute | solution.py:464
  12.7 0.0 collective-permute-done.3.y_one
  12.7 2.7 %collective-permute-start.4 = (f32[4,9,128]{2,1,0:T(8,128)S(1)}, f32[4,9,128]{2,1,0:T(8,128)S(1)}, u32[]{:S(2)}, u32[]{:S(2)}) collective-permute-start(f32[4,9,128]{2,1,0:T(8,128)S(1)} %get-tuple-element.27), channel_id=1, source_target_pairs={{1,2},{2,1},{3,0},{0,3},{5,6},{6,5},{7,4},{4,7},{9,10},{10,9},{11,... | collective-permute-start | bytes 55304 | tf_op jit(solution)/shard_map/ppermute | solution.py:467
  15.4 0.0 copy-done
  15.4 0.0 copy-done.4
  15.4 0.0 copy-done.5
  15.4 0.0 copy-done.6
  15.4 2.5 %volume.1 = (f32[2,4,9,16,512]{4,3,2,1,0:T(8,128)S(1)}, f32[4,4,16,128]{3,2,1,0:T(8,128)S(1)}, s32[3,4,16,128]{3,2,1,0:T(8,128)S(1)}, f32[2,2,4,16,128]{4,3,2,1,0:T(8,128)S(1)}) custom-call(f32[2,4,9,16,512]{4,3,2,1,0:T(8,128)S(1)} %get-tuple-element.19.state_ref, bf16[512,1536]{1,0:T(8,128)(2,1)S(1)} %copy-done, f32[3,4,16]{2,1,0:T(4,128)S(1)} %bitcast.24, ...), custom_call_target="tpu_custom_call" | custom-call | flops 1000000 | bytes 100000 | tf_op jit(solution)/shard_map/volume/pallas_call | solution.py:285
  17.9 0.0 collective-permute-done.5.z_one
  18.0 0.1 collective-permute-done.2.y_two
  18.0 0.0 collective-permute-done.4.z_two
  18.0 0.0 collective-permute-done.far_ref
  18.0 0.0 collective-permute-done.1.near_ref
  18.0 0.0 copy-done.1
  18.1 0.0 copy-done.2
  18.1 4.1 %finish.1 = (f32[2,4,9,16,512]{4,3,2,1,0:T(8,128)}, f32[9,4,16]{2,1,0:T(4,128)}) custom-call(f32[2,4,9,16,512]{4,3,2,1,0:T(8,128)S(1)} %get-tuple-element.19.state_ref, f32[2,4,9,16,256]{4,3,2,1,0:T(8,128)S(1)} %get-tuple-element.20.trace_ref, f32[4,9,16,128]{3,2,1,0:T(8,128)S(1)} %collective-permute-done.far_ref, ...), custom_call_target="tpu_custom_call" | custom-call | flops 900000000 | bytes 10000000 | tf_op jit(solution)/shard_map/finish/pallas_call | solution.py:426
Async XLA Ops:
  0.6 8.0 %copy-start.3 = (bf16[512,256]{1,0:T(8,128)(2,1)S(1)}, bf16[512,256]{1,0:T(8,128)(2,1)}, u32[]{:S(2)}) copy-start(bf16[512,256]{1,0:T(8,128)(2,1)} %constant.2.clone.table_ref) | copy-start | bytes 786436
  0.6 14.8 %copy-start = (bf16[512,1536]{1,0:T(8,128)(2,1)S(1)}, bf16[512,1536]{1,0:T(8,128)(2,1)}, u32[]{:S(2)}) copy-start(bf16[512,1536]{1,0:T(8,128)(2,1)} %deriv_ref.1) | copy-start | bytes 4718596
  0.7 14.8 %copy-start.4 = (s32[1,4,16,6]{2,1,3,0:T(4,128)S(1)}, s32[1,4,16,6]{2,1,3,0:T(4,128)}, u32[]{:S(2)}) copy-start(s32[1,4,16,6]{2,1,3,0:T(4,128)} %param.13) | copy-start | bytes 4612
  0.7 14.8 %copy-start.5 = (s32[1,4,16,6]{2,1,3,0:T(4,128)S(1)}, s32[1,4,16,6]{2,1,3,0:T(4,128)}, u32[]{:S(2)}) copy-start(s32[1,4,16,6]{2,1,3,0:T(4,128)} %param.14) | copy-start | bytes 4612
  0.7 14.8 %copy-start.6 = (f32[3,1,4,16]{3,2,1,0:T(4,128)S(1)}, f32[3,1,4,16]{3,2,1,0:T(4,128)}, u32[]{:S(2)}) copy-start(f32[3,1,4,16]{3,2,1,0:T(4,128)} %param.11) | copy-start | bytes 2308
  2.5 15.6 %collective-permute-start = (f32[4,9,16,128]{3,2,1,0:T(8,128)S(1)}, f32[4,9,16,128]{3,2,1,0:T(8,128)S(1)}, u32[]{:S(2)}, u32[]{:S(2)}) collective-permute-start(f32[4,9,16,128]{3,2,1,0:T(8,128)S(1)} %get-tuple-element.21), channel_id=1, source_target_pairs={{16,32},{32,16},{48,64},{64,48},{80,96},{96,80},{112,0},{0,112},{1... | collective-permute-start | bytes 884744 | tf_op jit(solution)/shard_map/ppermute | solution.py:459
  8.6 9.5 %collective-permute-start.1 = (f32[4,9,16,128]{3,2,1,0:T(8,128)S(1)}, f32[4,9,16,128]{3,2,1,0:T(8,128)S(1)}, u32[]{:S(2)}, u32[]{:S(2)}) collective-permute-start(f32[4,9,16,128]{3,2,1,0:T(8,128)S(1)} %get-tuple-element.22), channel_id=1, source_target_pairs={{0,16},{16,0},{32,48},{48,32},{64,80},{80,64},{96,112},{112,96},{1... | collective-permute-start | bytes 884744 | tf_op jit(solution)/shard_map/ppermute | solution.py:460
  9.7 8.4 %copy-start.1 = (f32[1,4,16,9,384]{4,2,3,1,0:T(8,128)S(1)}, f32[1,4,16,9,384]{4,2,3,1,0:T(8,128)}, u32[]{:S(2)}) copy-start(f32[1,4,16,9,384]{4,2,3,1,0:T(8,128)} %param.12) | copy-start | bytes 2654212
  9.7 8.4 %copy-start.2 = (bf16[384,512]{1,0:T(8,128)(2,1)S(1)}, bf16[384,512]{1,0:T(8,128)(2,1)}, u32[]{:S(2)}) copy-start(bf16[384,512]{1,0:T(8,128)(2,1)} %lift_ref.1) | copy-start | bytes 1179652
  9.7 3.0 %collective-permute-start.3 = (f32[9,16,128]{2,1,0:T(8,128)S(1)}, f32[9,16,128]{2,1,0:T(8,128)S(1)}, u32[]{:S(2)}, u32[]{:S(2)}) collective-permute-start(f32[9,16,128]{2,1,0:T(8,128)S(1)} %get-tuple-element.25), channel_id=1, source_target_pairs={{0,4},{4,0},{8,12},{12,8},{1,5},{5,1},{9,13},{13,9},{2,6},{6,2},{1... | collective-permute-start | bytes 221192 | tf_op jit(solution)/shard_map/ppermute | solution.py:462
  10.7 7.3 %collective-permute-start.2 = (f32[9,16,128]{2,1,0:T(8,128)S(1)}, f32[9,16,128]{2,1,0:T(8,128)S(1)}, u32[]{:S(2)}, u32[]{:S(2)}) collective-permute-start(f32[9,16,128]{2,1,0:T(8,128)S(1)} %get-tuple-element.23), channel_id=1, source_target_pairs={{4,8},{8,4},{12,0},{0,12},{5,9},{9,5},{13,1},{1,13},{6,10},{10,6},... | collective-permute-start | bytes 221192 | tf_op jit(solution)/shard_map/ppermute | solution.py:463
  11.0 6.9 %collective-permute-start.5 = (f32[4,9,128]{2,1,0:T(8,128)S(1)}, f32[4,9,128]{2,1,0:T(8,128)S(1)}, u32[]{:S(2)}, u32[]{:S(2)}) collective-permute-start(f32[4,9,128]{2,1,0:T(8,128)S(1)} %get-tuple-element.28), channel_id=1, source_target_pairs={{0,1},{1,0},{2,3},{3,2},{4,5},{5,4},{6,7},{7,6},{8,9},{9,8},{10,11... | collective-permute-start | bytes 55304 | tf_op jit(solution)/shard_map/ppermute | solution.py:464
  12.7 5.4 %collective-permute-start.4 = (f32[4,9,128]{2,1,0:T(8,128)S(1)}, f32[4,9,128]{2,1,0:T(8,128)S(1)}, u32[]{:S(2)}, u32[]{:S(2)}) collective-permute-start(f32[4,9,128]{2,1,0:T(8,128)S(1)} %get-tuple-element.27), channel_id=1, source_target_pairs={{1,2},{2,1},{3,0},{0,3},{5,6},{6,5},{7,4},{4,7},{9,10},{10,9},{11,... | collective-permute-start | bytes 55304 | tf_op jit(solution)/shard_map/ppermute | solution.py:467

commit v5 on v4

--- a/solution.py
+++ b/solution.py
@@ -301,122 +301,165 @@
     )(state, deriv, material, orient, flags)
 
 
-def final_kernel(
-    state_ref, trace_ref, far_ref, near_ref, y_two, y_one, z_two, z_one,
-    coef_ref, source_ref, edge_ref, partial_ref, stored_ref, lift_ref,
-    advanced_ref, kernel_ref,
-    flux_ref, sum_ref, out_ref, out_sem,
+def face_flux(jumps, d, coefs):
+    lam, mu, inv, speed = coefs
+    flux = [speed * jump for jump in jumps]
+    for i in range(3):
+        flux[i] = flux[i] + inv * jumps[stress_slot[i][d]]
+    common = lam * jumps[d]
+    for i in range(3):
+        flux[3 + i] = flux[3 + i] + common
+    for i, j, f in ((0, 0, 3), (1, 1, 4), (2, 2, 5), (1, 2, 6), (0, 2, 7), (0, 1, 8)):
+        if j == d:
+            flux[f] = flux[f] + mu * jumps[i]
+        if i == d:
+            flux[f] = flux[f] + mu * jumps[j]
+    return [term.astype(jnp.bfloat16) for term in flux]
+
+
+def side_kernel(
+    trace_ref, y_two, y_one, z_two, z_one, coef_ref, source_ref, edge_ref, stored_ref,
+    flux_ref, sum_ref,
 ):
-    count_y, fields, count_z, nodes = state_ref.shape[1:]
+    _, count_y, fields, count_z, _ = trace_ref.shape
     last_y = count_y - 1
-    odd_x = odd_position("gx")
     odd_y = odd_position("gy")
     odd_z = odd_position("gz")
     lane = lane_index((count_z, LANES))
     upper = lane >= FACE
     z_pos = lax.broadcasted_iota(jnp.int32, lane.shape, 0)
-    take_near = upper == odd_x
-
-    def write(y):
-        return pltpu.make_async_copy(out_ref.at[:, y], advanced_ref.at[:, y], out_sem.at[y])
 
     def row(y, carry):
         below = jnp.maximum(y - 1, 0)
         above = jnp.minimum(y + 1, last_y)
-        lam, mu, inv, speed = [coef_ref[k, y] for k in range(4)]
+        coefs = [coef_ref[k, y] for k in range(4)]
         for s in range(2):
-            for d in range(3):
+            for d in (1, 2):
                 source = source_ref[d, y]
-                if d == 0 and s == 1:
-                    source = (source + FACE) % LANES
-                if d > 0:
-                    rim = edge_ref[d - 1, 0, y] > 0.0
-                    free = edge_ref[d - 1, 1, y]
-                    keep_velocity = free - 1.0
-                    keep_stress = -free - 1.0
+                rim = edge_ref[d - 1, 0, y] > 0.0
+                free = edge_ref[d - 1, 1, y]
+                keep_velocity = free - 1.0
+                keep_stress = -free - 1.0
+                half = slice((d - 1) * LANES, d * LANES)
                 jumps = []
                 for f in range(fields):
-                    if d == 0:
-                        inside = jnp.where(
-                            upper, state_ref[s, y, f, :, nodes - LANES :], state_ref[s, y, f, :, :LANES]
-                        )
-                        near, far = (near_ref[y, f], far_ref[y, f])
-                        if s == 1:
-                            near, far = (far, near)
-                        mixed = jnp.where(take_near, near, far)
-                    elif d == 1:
-                        inside = trace_ref[s, y, f, :, :LANES]
+                    inside = trace_ref[s, y, f, :, half]
+                    if d == 1:
                         two, one = (y_two[f], y_one[f])
-                        from_below = jnp.where(odd_y, one, two)
-                        from_above = jnp.where(odd_y, two, one)
-                        if s == 1:
-                            from_below = pltpu.roll(from_below, FACE, 1)
-                            from_above = pltpu.roll(from_above, FACE, 1)
-                        lower = jnp.where(y == 0, from_below, trace_ref[s, below, f, :, :LANES])
-                        higher = jnp.where(y == last_y, from_above, trace_ref[s, above, f, :, :LANES])
-                        mixed = jnp.where(upper, lower, higher)
+                        odd = odd_y
                     else:
-                        inside = trace_ref[s, y, f, :, LANES:]
                         two = jnp.broadcast_to(z_two[y, f : f + 1, :], lane.shape)
                         one = jnp.broadcast_to(z_one[y, f : f + 1, :], lane.shape)
-                        from_below = jnp.where(odd_z, one, two)
-                        from_above = jnp.where(odd_z, two, one)
-                        if s == 1:
-                            from_below = pltpu.roll(from_below, FACE, 1)
-                            from_above = pltpu.roll(from_above, FACE, 1)
+                        odd = odd_z
+                    from_below = jnp.where(odd, one, two)
+                    from_above = jnp.where(odd, two, one)
+                    if s == 1:
+                        from_below = pltpu.roll(from_below, FACE, 1)
+                        from_above = pltpu.roll(from_above, FACE, 1)
+                    if d == 1:
+                        lower = jnp.where(y == 0, from_below, trace_ref[s, below, f, :, half])
+                        higher = jnp.where(y == last_y, from_above, trace_ref[s, above, f, :, half])
+                    else:
                         lower = jnp.where(z_pos == 0, from_below, pltpu.roll(inside, 1, 0))
                         higher = jnp.where(
                             z_pos == count_z - 1, from_above, pltpu.roll(inside, count_z - 1, 0)
                         )
-                        mixed = jnp.where(upper, lower, higher)
-                    turned = jnp.take_along_axis(mixed, source, axis=1)
-                    jump = turned - inside
-                    if d > 0:
-                        keep = keep_velocity if f < 3 else keep_stress
-                        jump = jnp.where(rim, inside * keep, jump)
+                    mixed = jnp.where(upper, lower, higher)
+                    jump = jnp.take_along_axis(mixed, source, axis=1) - inside
+                    keep = keep_velocity if f < 3 else keep_stress
+                    jump = jnp.where(rim, inside * keep, jump)
                     jumps.append(jump)
                     if s == 1:
                         term = stored_ref[y, f, :, d * LANES : (d + 1) * LANES] * jump
-                        if d == 0:
-                            sum_ref[f] = term
+                        if d == 1:
+                            sum_ref[y, f] = term
                         else:
-                            sum_ref[f] += term
-                flux = [speed * jump for jump in jumps]
-                for i in range(3):
-                    flux[i] = flux[i] + inv * jumps[stress_slot[i][d]]
-                common = lam * jumps[d]
-                for i in range(3):
-                    flux[3 + i] = flux[3 + i] + common
-                for i, j, f in ((0, 0, 3), (1, 1, 4), (2, 2, 5), (1, 2, 6), (0, 2, 7), (0, 1, 8)):
-                    if j == d:
-                        flux[f] = flux[f] + mu * jumps[i]
-                    if i == d:
-                        flux[f] = flux[f] + mu * jumps[j]
-                for f in range(fields):
-                    flux_ref[s, f, :, d * LANES : (d + 1) * LANES] = flux[f].astype(jnp.bfloat16)
+                            sum_ref[y, f] += term
+                for f, term in enumerate(face_flux(jumps, d, coefs)):
+                    flux_ref[y, s, f, :, half] = term
+        return carry
+
+    lax.fori_loop(0, count_y, row, 0)
+
+
+def side_faces(traces, y_two, y_one, z_two, z_one, coef, source, edge, stored):
+    _, count_y, fields, count_z, _ = traces.shape
+    return pl.pallas_call(
+        side_kernel,
+        out_shape=(
+            jax.ShapeDtypeStruct((count_y, 2, fields, count_z, 2 * LANES), jnp.bfloat16),
+            jax.ShapeDtypeStruct((count_y, fields, count_z, LANES), jnp.float32),
+        ),
+        in_specs=[pl.BlockSpec(memory_space=pltpu.VMEM)] * 9,
+        out_specs=(pl.BlockSpec(memory_space=pltpu.VMEM),) * 2,
+        compiler_params=pltpu.CompilerParams(vmem_limit_bytes=LIMIT),
+        cost_estimate=pl.CostEstimate(flops=10**6, bytes_accessed=10**5, transcendentals=0),
+        name="side_faces",
+    )(traces, y_two, y_one, z_two, z_one, coef, source, edge, stored)
+
+
+def final_kernel(
+    state_ref, far_ref, near_ref, coef_ref, source_ref, side_ref, side_sum_ref, partial_ref,
+    stored_ref, lift_ref,
+    advanced_ref, kernel_ref,
+    flux_ref, out_ref, out_sem,
+):
+    _, count_y, fields, count_z, nodes = state_ref.shape
+    lane = lane_index((count_z, LANES))
+    upper = lane >= FACE
+    z_pos = lax.broadcasted_iota(jnp.int32, lane.shape, 0)
+    take_near = upper == odd_position("gx")
+
+    def write(s, y):
+        return pltpu.make_async_copy(out_ref.at[s, y], advanced_ref.at[s, y], out_sem.at[s, y])
+
+    def row(y, carry):
+        coefs = [coef_ref[k, y] for k in range(4)]
+        for s in range(2):
+            source = source_ref[0, y]
+            if s == 1:
+                source = (source + FACE) % LANES
+            jumps = []
+            for f in range(fields):
+                inside = jnp.where(
+                    upper, state_ref[s, y, f, :, nodes - LANES :], state_ref[s, y, f, :, :LANES]
+                )
+                near, far = (near_ref[y, f], far_ref[y, f])
+                if s == 1:
+                    near, far = (far, near)
+                mixed = jnp.where(take_near, near, far)
+                jump = jnp.take_along_axis(mixed, source, axis=1) - inside
+                jumps.append(jump)
+                if s == 1:
+                    terms = side_sum_ref[y, f] + stored_ref[y, f, :, :LANES] * jump
+                    sums = jnp.sum(terms, axis=1, keepdims=True) * (1.0 / FACE)
+                    across = jnp.sum(jnp.where(z_pos == lane, sums, 0.0), axis=0, keepdims=True)
+                    kernel_ref[f, pl.ds(y, 1), :] = across[:, :count_z]
+            for f, term in enumerate(face_flux(jumps, 0, coefs)):
+                flux_ref[s, f] = term
         lifted = jnp.dot(
-            flux_ref[...].reshape(2 * fields * count_z, 3 * LANES),
-            lift_ref[...],
+            side_ref[y].reshape(2 * fields * count_z, 2 * LANES),
+            lift_ref[LANES:],
             preferred_element_type=jnp.float32,
-        ).reshape(2, fields, count_z, nodes)
+        ) + jnp.dot(
+            flux_ref[...].reshape(2 * fields * count_z, LANES),
+            lift_ref[:LANES],
+            preferred_element_type=jnp.float32,
+        )
+        lifted = lifted.reshape(2, fields, count_z, nodes)
         for s in range(2):
             scale = step_size if s == 0 else -step_size
             out_ref[s, y] = partial_ref[s, y] + scale * lifted[s]
-        write(y).start()
-        for f in range(fields):
-            sums = jnp.sum(sum_ref[f], axis=1, keepdims=True) * (1.0 / FACE)
-            across = jnp.sum(jnp.where(z_pos == lane, sums, 0.0), axis=0, keepdims=True)
-            kernel_ref[f, pl.ds(y, 1), :] = across[:, :count_z]
+            write(s, y).start()
         return carry
 
     lax.fori_loop(0, count_y, row, 0)
     for y in range(count_y):
-        write(y).wait()
-
-
-def finish(
-    state, traces, far, near, y_two, y_one, z_two, z_one, coef, source, edge, part, stored, lift
-):
+        for s in range(2):
+            write(s, y).wait()
+
+
+def finish(state, far, near, coef, source, side, side_sum, part, stored, lift):
     _, count_y, fields, count_z, nodes = state.shape
     f32 = jnp.float32
     outs = (
@@ -426,18 +469,17 @@
     return pl.pallas_call(
         final_kernel,
         out_shape=outs,
-        in_specs=[pl.BlockSpec(memory_space=pltpu.VMEM)] * 14,
+        in_specs=[pl.BlockSpec(memory_space=pltpu.VMEM)] * 10,
         out_specs=(pl.BlockSpec(memory_space=pl.ANY), pl.BlockSpec(memory_space=pltpu.VMEM)),
         scratch_shapes=[
-            pltpu.VMEM((2, fields, count_z, 3 * LANES), jnp.bfloat16),
-            pltpu.VMEM((fields, count_z, LANES), f32),
+            pltpu.VMEM((2, fields, count_z, LANES), jnp.bfloat16),
             pltpu.VMEM(state.shape, f32),
-            pltpu.SemaphoreType.DMA((count_y,)),
+            pltpu.SemaphoreType.DMA((2, count_y)),
         ],
         compiler_params=pltpu.CompilerParams(vmem_limit_bytes=LIMIT),
         cost_estimate=pl.CostEstimate(flops=9 * 10**8, bytes_accessed=10**7, transcendentals=0),
         name="finish",
-    )(state, traces, far, near, y_two, y_one, z_two, z_one, coef, source, edge, part, stored, lift)
+    )(state, far, near, coef, source, side, side_sum, part, stored, lift)
 
 
 def swaps(count, start, wrap):
@@ -445,6 +487,18 @@
     for i in range(start, count if wrap else count - 1, 2):
         j = (i + 1) % count
         pairs += [(i, j), (j, i)]
+    return pairs
+
+
+def inner_swaps(count_y, count_z):
+    pairs = []
+    for y in range(count_y):
+        for z in range(count_z):
+            if z in (0, count_z - 1):
+                target = (y ^ 1, z)
+            else:
+                target = (y, z + 1 if z % 2 == 1 else z - 1)
+            pairs.append((y * count_z + z, target[0] * count_z + target[1]))
     return pairs
 
 
@@ -464,11 +518,13 @@
     z_one = lax.ppermute(z_one, "gz", swaps(nz, 0, False))
     medium = material[:, 0]
     z_two, medium, y_one = lax.optimization_barrier((z_two, medium, y_one))
-    z_two = lax.ppermute(z_two, "gz", swaps(nz, 1, True))
+    z_two = lax.ppermute(z_two, ("gy", "gz"), inner_swaps(ny, nz))
     part, coef, source, edge = volume(view, deriv, medium, orient_view, flags_view)
+    side, side_sum = side_faces(
+        traces, y_two, y_one, z_two, z_one, coef, source, edge, stored_view
+    )
     advanced, kernel = finish(
-        view, traces, far_in, near_in, y_two, y_one, z_two, z_one, coef, source, edge, part,
-        stored_view, lift,
+        view, far_in, near_in, coef, source, side, side_sum, part, stored_view, lift
     )
     return (
         jnp.transpose(advanced, (0, 1, 3, 2, 4))[:, None],

time: 22.3 us -> 23.2 us (1.040)
  starting transfers between devices: 11.8 us -> 9.79 us
  waiting for transfers between devices: 0.1 us -> 1.84 us
  Pallas kernels: 9.48 us -> 10.7 us
    pallas_call x0 -> x1, Pallas kernels: none -> 2.33 us  [side_faces(): pl.pallas_call(side_kernel, out_shape=(jax.ShapeDtypeStruct((count_y, 2,...]
    ppermute x1, starting transfers between devices: 2.75 us -> 0.71 us  [local(): z_two = lax.ppermute(z_two, ('gy', 'gz'), inner_swaps(ny, nz))]
    ppermute x1, waiting for transfers between devices: 0.08 us -> 1.83 us  [local(): y_two = lax.ppermute(y_two, 'gy', swaps(ny, 1, True))]
    pallas_call x1, Pallas kernels: 4.11 us -> 2.99 us  [finish(): pl.pallas_call(final_kernel, out_shape=outs, in_specs=[pl.BlockSpec(memor...]
  transfers between devices with their start and end apart: 6 -> 6, of which waited for: 1 -> 1; matrix products, arithmetic and copies ran while one was open for 0% -> 0% of each run, Pallas kernels for 16% -> 26%
where the time goes in v5:
time: 23.2 us; the launch traced here: 23.1 us
  Pallas kernels  10.7 us (46%)
  starting transfers between devices  9.79 us (42%)
  waiting for transfers between devices  1.84 us (8%)
  between operations  0.76 us (3%)
    ppermute x1, starting transfers between devices, local(): far_in = lax.ppermute(far, 'gx', swaps(nx, 1, True))  6.1 us
    pallas_call x1, Pallas kernels, finish(): pl.pallas_call(final_kernel, out_shape=outs, in_specs=[pl.BlockSpec(memor...  2.99 us
    pallas_call x1, Pallas kernels, volume(): pl.pallas_call(volume_kernel, out_shape=outs, in_specs=[pl.BlockSpec(memo...  2.5 us
    pallas_call x1, Pallas kernels, side_faces(): pl.pallas_call(side_kernel, out_shape=(jax.ShapeDtypeStruct((count_y, 2,...  2.33 us
    ppermute x1, waiting for transfers between devices, local(): y_two = lax.ppermute(y_two, 'gy', swaps(ny, 1, True))  1.83 us
    pallas_call x1, Pallas kernels, pack_faces(): pl.pallas_call(pack_kernel, out_shape=(jax.ShapeDtypeStruct(state.shape,...  1.79 us
    ppermute x1, starting transfers between devices, local(): z_one = lax.ppermute(z_one, 'gz', swaps(nz, 0, False))  1.65 us
    pallas_call x1, Pallas kernels, extract_traces(): pl.pallas_call(trace_kernel, out_shape=(jax.ShapeDtypeStruct((2, count_y,...  1.08 us
  transfers between devices with their start and end apart: 6, of which 1 were waited for; matrix products, arithmetic and copies ran while one was open for 0% of the time, Pallas kernels for 26%

profile of v5, /device:TPU:1, one launch (start us, length us, event | category | flops | bytes accessed | tf_op | source)
XLA Modules:
  0.0 23.1 jit_solution(16035675536302531453)
XLA Ops:
  0.6 0.0 copy-start.3
  0.6 0.0 copy-start.1
  0.7 0.0 copy-start.4
  0.7 0.0 copy-start.5
  0.7 0.0 copy-start.6
  0.7 1.8 %pack_faces.1 = (f32[2,4,9,16,512]{4,3,2,1,0:T(8,128)S(1)}, f32[4,9,16,128]{3,2,1,0:T(8,128)S(1)}, f32[4,9,16,128]{3,2,1,0:T(8,128)S(1)}) custom-call(f32[2,4,9,16,512]{4,3,2,1,0:T(8,128)} %bitcast.26), custom_call_target="tpu_custom_call" | custom-call | flops 1000000 | bytes 2000000 | tf_op jit(solution)/shard_map/pack_faces/pallas_call | solution.py:76
  2.5 6.1 %collective-permute-start = (f32[4,9,16,128]{3,2,1,0:T(8,128)S(1)}, f32[4,9,16,128]{3,2,1,0:T(8,128)S(1)}, u32[]{:S(2)}, u32[]{:S(2)}) collective-permute-start(f32[4,9,16,128]{3,2,1,0:T(8,128)S(1)} %get-tuple-element.22), channel_id=1, source_target_pairs={{16,32},{32,16},{48,64},{64,48},{80,96},{96,80},{112,0},{0,112},{1... | collective-permute-start | bytes 884744 | tf_op jit(solution)/shard_map/ppermute | solution.py:513
  8.6 0.0 collective-permute-start.1
  8.6 0.0 copy-done.3
  8.6 1.1 %extract_traces.1 = (f32[2,4,9,16,256]{4,3,2,1,0:T(8,128)S(1)}, f32[9,16,128]{2,1,0:T(8,128)S(1)}, f32[9,16,128]{2,1,0:T(8,128)S(1)}, f32[4,9,128]{2,1,0:T(8,128)S(1)}, f32[4,9,128]{2,1,0:T(8,128)S(1)}) custom-call(f32[2,4,9,16,512]{4,3,2,1,0:T(8,128)S(1)} %get-tuple-element.21.state_ref, bf16[512,256]{1,0:T(8,128)(2,1)S(1)} %copy-done.3), custom_call_target="tpu_custom_call" | custom-call | flops 600000000 | bytes 4000000 | tf_op jit(solution)/shard_map/extract_traces/pallas_call | solution.py:123
  9.7 0.0 copy-start
  9.7 1.0 %collective-permute-start.2 = (f32[9,16,128]{2,1,0:T(8,128)S(1)}, f32[9,16,128]{2,1,0:T(8,128)S(1)}, u32[]{:S(2)}, u32[]{:S(2)}) collective-permute-start(f32[9,16,128]{2,1,0:T(8,128)S(1)} %get-tuple-element.25), channel_id=1, source_target_pairs={{0,4},{4,0},{8,12},{12,8},{1,5},{5,1},{9,13},{13,9},{2,6},{6,2},{1... | collective-permute-start | bytes 221192 | tf_op jit(solution)/shard_map/ppermute | solution.py:516
  10.7 0.3 %collective-permute-start.3 = (f32[9,16,128]{2,1,0:T(8,128)S(1)}, f32[9,16,128]{2,1,0:T(8,128)S(1)}, u32[]{:S(2)}, u32[]{:S(2)}) collective-permute-start(f32[9,16,128]{2,1,0:T(8,128)S(1)} %get-tuple-element.30), channel_id=1, source_target_pairs={{4,8},{8,4},{12,0},{0,12},{5,9},{9,5},{13,1},{1,13},{6,10},{10,6},... | collective-permute-start | bytes 221192 | tf_op jit(solution)/shard_map/ppermute | solution.py:517
  11.0 1.6 %collective-permute-start.5 = (f32[4,9,128]{2,1,0:T(8,128)S(1)}, f32[4,9,128]{2,1,0:T(8,128)S(1)}, u32[]{:S(2)}, u32[]{:S(2)}) collective-permute-start(f32[4,9,128]{2,1,0:T(8,128)S(1)} %get-tuple-element.33), channel_id=1, source_target_pairs={{0,1},{1,0},{2,3},{3,2},{4,5},{5,4},{6,7},{7,6},{8,9},{9,8},{10,11... | collective-permute-start | bytes 55304 | tf_op jit(solution)/shard_map/ppermute | solution.py:518
  12.7 0.0 collective-permute-done.2.y_one
  12.7 0.7 %collective-permute-start.4 = (f32[4,9,128]{2,1,0:T(8,128)S(1)}, f32[4,9,128]{2,1,0:T(8,128)S(1)}, u32[]{:S(2)}, u32[]{:S(2)}) collective-permute-start(f32[4,9,128]{2,1,0:T(8,128)S(1)} %get-tuple-element.32), channel_id=1, source_target_pairs={{0,4},{1,2},{2,1},{3,7},{4,0},{5,6},{6,5},{7,3},{8,12},{9,10},{10,... | collective-permute-start | bytes 55304 | tf_op jit(solution)/shard_map/ppermute | solution.py:521
  13.4 0.0 copy-done.1
  13.4 0.0 copy-done.4
  13.4 0.0 copy-done.5
  13.4 0.0 copy-done.6
  13.4 0.0 copy-start.2
  13.4 2.5 %volume.1 = (f32[2,4,9,16,512]{4,3,2,1,0:T(8,128)S(1)}, f32[4,4,16,128]{3,2,1,0:T(8,128)S(1)}, s32[3,4,16,128]{3,2,1,0:T(8,128)S(1)}, f32[2,2,4,16,128]{4,3,2,1,0:T(8,128)S(1)}) custom-call(f32[2,4,9,16,512]{4,3,2,1,0:T(8,128)S(1)} %get-tuple-element.21.state_ref, bf16[512,1536]{1,0:T(8,128)(2,1)S(1)} %copy-done.1, f32[3,4,16]{2,1,0:T(4,128)S(1)} %bitcast.25, ...), custom_call_target="tpu_custom_call" | custom-call | flops 1000000 | bytes 100000 | tf_op jit(solution)/shard_map/volume/pallas_call | solution.py:285
  15.9 0.0 collective-permute-done.5.z_one
  15.9 1.8 %collective-permute-done.3.y_two = f32[9,16,128]{2,1,0:T(8,128)S(1)} collective-permute-done((f32[9,16,128]{2,1,0:T(8,128)S(1)}, f32[9,16,128]{2,1,0:T(8,128)S(1)}, u32[]{:S(2)}, u32[]{:S(2)}) %collective-permute-start.3) | collective-permute-done | bytes 73760 | tf_op jit(solution)/shard_map/ppermute | solution.py:517
  17.7 0.0 collective-permute-done.4.z_two
  17.7 0.0 copy-done
  17.7 2.3 %side_faces.1 = (bf16[4,2,9,16,256]{4,3,2,1,0:T(8,128)(2,1)S(1)}, f32[4,9,16,128]{3,2,1,0:T(8,128)S(1)}) custom-call(f32[2,4,9,16,256]{4,3,2,1,0:T(8,128)S(1)} %get-tuple-element.29.trace_ref, f32[9,16,128]{2,1,0:T(8,128)S(1)} %collective-permute-done.3.y_two, f32[9,16,128]{2,1,0:T(8,128)S(1)} %collective-permute-done.2.y_one, ...), custom_call_target="tpu_custom_call" | custom-call | flops 1000000 | bytes 100000 | tf_op jit(solution)/shard_map/side_faces/pallas_call | solution.py:387
  20.1 0.0 collective-permute-done.far_ref
  20.1 0.0 collective-permute-done.1.near_ref
  20.1 0.0 copy-done.2
  20.1 3.0 %finish.1 = (f32[2,4,9,16,512]{4,3,2,1,0:T(8,128)}, f32[9,4,16]{2,1,0:T(4,128)}) custom-call(f32[2,4,9,16,512]{4,3,2,1,0:T(8,128)S(1)} %get-tuple-element.21.state_ref, f32[4,9,16,128]{3,2,1,0:T(8,128)S(1)} %collective-permute-done.far_ref, f32[4,9,16,128]{3,2,1,0:T(8,128)S(1)} %collective-permute-done.1.near_ref, ...), custom_call_target="tpu_custom_call" | custom-call | flops 900000000 | bytes 10000000 | tf_op jit(solution)/shard_map/finish/pallas_call | solution.py:469
Async XLA Ops:
  0.6 8.0 %copy-start.3 = (bf16[512,256]{1,0:T(8,128)(2,1)S(1)}, bf16[512,256]{1,0:T(8,128)(2,1)}, u32[]{:S(2)}) copy-start(bf16[512,256]{1,0:T(8,128)(2,1)} %constant.2.clone.table_ref) | copy-start | bytes 786436
  0.6 12.7 %copy-start.1 = (bf16[512,1536]{1,0:T(8,128)(2,1)S(1)}, bf16[512,1536]{1,0:T(8,128)(2,1)}, u32[]{:S(2)}) copy-start(bf16[512,1536]{1,0:T(8,128)(2,1)} %deriv_ref.1) | copy-start | bytes 4718596
  0.7 12.7 %copy-start.4 = (s32[1,4,16,6]{2,1,3,0:T(4,128)S(1)}, s32[1,4,16,6]{2,1,3,0:T(4,128)}, u32[]{:S(2)}) copy-start(s32[1,4,16,6]{2,1,3,0:T(4,128)} %param.13) | copy-start | bytes 4612
  0.7 12.7 %copy-start.5 = (s32[1,4,16,6]{2,1,3,0:T(4,128)S(1)}, s32[1,4,16,6]{2,1,3,0:T(4,128)}, u32[]{:S(2)}) copy-start(s32[1,4,16,6]{2,1,3,0:T(4,128)} %param.14) | copy-start | bytes 4612
  0.7 12.7 %copy-start.6 = (f32[3,1,4,16]{3,2,1,0:T(4,128)S(1)}, f32[3,1,4,16]{3,2,1,0:T(4,128)}, u32[]{:S(2)}) copy-start(f32[3,1,4,16]{3,2,1,0:T(4,128)} %param.11) | copy-start | bytes 2308
  2.5 17.6 %collective-permute-start = (f32[4,9,16,128]{3,2,1,0:T(8,128)S(1)}, f32[4,9,16,128]{3,2,1,0:T(8,128)S(1)}, u32[]{:S(2)}, u32[]{:S(2)}) collective-permute-start(f32[4,9,16,128]{3,2,1,0:T(8,128)S(1)} %get-tuple-element.22), channel_id=1, source_target_pairs={{16,32},{32,16},{48,64},{64,48},{80,96},{96,80},{112,0},{0,112},{1... | collective-permute-start | bytes 884744 | tf_op jit(solution)/shard_map/ppermute | solution.py:513
  8.6 11.5 %collective-permute-start.1 = (f32[4,9,16,128]{3,2,1,0:T(8,128)S(1)}, f32[4,9,16,128]{3,2,1,0:T(8,128)S(1)}, u32[]{:S(2)}, u32[]{:S(2)}) collective-permute-start(f32[4,9,16,128]{3,2,1,0:T(8,128)S(1)} %get-tuple-element.23), channel_id=1, source_target_pairs={{0,16},{16,0},{32,48},{48,32},{64,80},{80,64},{96,112},{112,96},{1... | collective-permute-start | bytes 884744 | tf_op jit(solution)/shard_map/ppermute | solution.py:514
  9.7 8.1 %copy-start = (f32[1,4,16,9,384]{4,2,3,1,0:T(8,128)S(1)}, f32[1,4,16,9,384]{4,2,3,1,0:T(8,128)}, u32[]{:S(2)}) copy-start(f32[1,4,16,9,384]{4,2,3,1,0:T(8,128)} %param.12) | copy-start | bytes 2654212
  9.7 3.0 %collective-permute-start.2 = (f32[9,16,128]{2,1,0:T(8,128)S(1)}, f32[9,16,128]{2,1,0:T(8,128)S(1)}, u32[]{:S(2)}, u32[]{:S(2)}) collective-permute-start(f32[9,16,128]{2,1,0:T(8,128)S(1)} %get-tuple-element.25), channel_id=1, source_target_pairs={{0,4},{4,0},{8,12},{12,8},{1,5},{5,1},{9,13},{13,9},{2,6},{6,2},{1... | collective-permute-start | bytes 221192 | tf_op jit(solution)/shard_map/ppermute | solution.py:516
  10.7 7.0 %collective-permute-start.3 = (f32[9,16,128]{2,1,0:T(8,128)S(1)}, f32[9,16,128]{2,1,0:T(8,128)S(1)}, u32[]{:S(2)}, u32[]{:S(2)}) collective-permute-start(f32[9,16,128]{2,1,0:T(8,128)S(1)} %get-tuple-element.30), channel_id=1, source_target_pairs={{4,8},{8,4},{12,0},{0,12},{5,9},{9,5},{13,1},{1,13},{6,10},{10,6},... | collective-permute-start | bytes 221192 | tf_op jit(solution)/shard_map/ppermute | solution.py:517
  11.0 4.9 %collective-permute-start.5 = (f32[4,9,128]{2,1,0:T(8,128)S(1)}, f32[4,9,128]{2,1,0:T(8,128)S(1)}, u32[]{:S(2)}, u32[]{:S(2)}) collective-permute-start(f32[4,9,128]{2,1,0:T(8,128)S(1)} %get-tuple-element.33), channel_id=1, source_target_pairs={{0,1},{1,0},{2,3},{3,2},{4,5},{5,4},{6,7},{7,6},{8,9},{9,8},{10,11... | collective-permute-start | bytes 55304 | tf_op jit(solution)/shard_map/ppermute | solution.py:518
  12.7 5.1 %collective-permute-start.4 = (f32[4,9,128]{2,1,0:T(8,128)S(1)}, f32[4,9,128]{2,1,0:T(8,128)S(1)}, u32[]{:S(2)}, u32[]{:S(2)}) collective-permute-start(f32[4,9,128]{2,1,0:T(8,128)S(1)} %get-tuple-element.32), channel_id=1, source_target_pairs={{0,4},{1,2},{2,1},{3,7},{4,0},{5,6},{6,5},{7,3},{8,12},{9,10},{10,... | collective-permute-start | bytes 55304 | tf_op jit(solution)/shard_map/ppermute | solution.py:521
  13.4 6.7 %copy-start.2 = (bf16[384,512]{1,0:T(8,128)(2,1)S(1)}, bf16[384,512]{1,0:T(8,128)(2,1)}, u32[]{:S(2)}) copy-start(bf16[384,512]{1,0:T(8,128)(2,1)} %lift_ref.1) | copy-start | bytes 1179652

commit v6 on v5

--- a/solution.py
+++ b/solution.py
@@ -106,20 +106,19 @@
     up = merged(trace_ref[0, end, :, :, :LANES], trace_ref[1, end, :, :, :LANES], True)
     y_two[...] = jnp.where(odd_y, up, down)
     y_one[...] = jnp.where(odd_y, down, up)
-    for y in range(count_y):
-        first = merged(trace_ref[0, y, :, 0, LANES:], trace_ref[1, y, :, 0, LANES:], False)
-        last = merged(
-            trace_ref[0, y, :, count_z - 1, LANES:], trace_ref[1, y, :, count_z - 1, LANES:], True
-        )
-        z_two[y] = jnp.where(odd_z, last, first)
-        z_one[y] = jnp.where(odd_z, first, last)
+    for s in range(2):
+        for y in range(count_y):
+            first = trace_ref[s, y, :, 0, LANES:]
+            last = trace_ref[s, y, :, count_z - 1, LANES:]
+            z_two[s, y] = jnp.where(odd_z, last, first)
+            z_one[s, y] = jnp.where(odd_z, first, last)
 
 
 def extract_traces(state, table):
     _, count_y, fields, count_z, nodes = state.shape
     f32 = jnp.float32
     y_message = jax.ShapeDtypeStruct((fields, count_z, LANES), f32)
-    z_message = jax.ShapeDtypeStruct((count_y, fields, LANES), f32)
+    z_message = jax.ShapeDtypeStruct((2, count_y, fields, LANES), f32)
     return pl.pallas_call(
         trace_kernel,
         out_shape=(
@@ -317,72 +316,69 @@
     return [term.astype(jnp.bfloat16) for term in flux]
 
 
+def rim_jump(turned, inside, edge, f):
+    rim, free = edge
+    keep = free - 1.0 if f < 3 else -free - 1.0
+    return jnp.where(rim > 0.0, inside * keep, turned - inside)
+
+
 def side_kernel(
-    trace_ref, y_two, y_one, z_two, z_one, coef_ref, source_ref, edge_ref, stored_ref,
-    flux_ref, sum_ref,
+    trace_ref, z_two, z_one, coef_ref, source_ref, edge_ref, stored_ref, flux_ref, sum_ref
 ):
     _, count_y, fields, count_z, _ = trace_ref.shape
     last_y = count_y - 1
-    odd_y = odd_position("gy")
     odd_z = odd_position("gz")
     lane = lane_index((count_z, LANES))
     upper = lane >= FACE
     z_pos = lax.broadcasted_iota(jnp.int32, lane.shape, 0)
+    at_low = jnp.logical_and(z_pos == 0, upper)
+    at_high = jnp.logical_and(z_pos == count_z - 1, jnp.logical_not(upper))
 
     def row(y, carry):
-        below = jnp.maximum(y - 1, 0)
-        above = jnp.minimum(y + 1, last_y)
         coefs = [coef_ref[k, y] for k in range(4)]
+        edge = (edge_ref[1, 0, y], edge_ref[1, 1, y])
+        source = source_ref[2, y]
         for s in range(2):
-            for d in (1, 2):
-                source = source_ref[d, y]
-                rim = edge_ref[d - 1, 0, y] > 0.0
-                free = edge_ref[d - 1, 1, y]
-                keep_velocity = free - 1.0
-                keep_stress = -free - 1.0
-                half = slice((d - 1) * LANES, d * LANES)
+            jumps = []
+            for f in range(fields):
+                inside = trace_ref[s, y, f, :, LANES:]
+                two = z_two[s, y, f : f + 1, :]
+                one = z_one[s, y, f : f + 1, :]
+                from_below = jnp.where(odd_z, one, two)
+                from_above = jnp.where(odd_z, two, one)
+                mixed = jnp.where(upper, pltpu.roll(inside, 1, 0), pltpu.roll(inside, count_z - 1, 0))
+                mixed = jnp.where(at_low, from_below, jnp.where(at_high, from_above, mixed))
+                turned = jnp.take_along_axis(mixed, source, axis=1)
+                jump = rim_jump(turned, inside, edge, f)
+                jumps.append(jump)
+                if s == 1:
+                    sum_ref[y, f] = stored_ref[y, f, :, 2 * LANES :] * jump
+            for f, term in enumerate(face_flux(jumps, 2, coefs)):
+                flux_ref[y, s, f, :, LANES:] = term
+
+        @pl.when(jnp.logical_and(y > 0, y < last_y))
+        def _():
+            turn = source_ref[1, y]
+            for s in range(2):
                 jumps = []
                 for f in range(fields):
-                    inside = trace_ref[s, y, f, :, half]
-                    if d == 1:
-                        two, one = (y_two[f], y_one[f])
-                        odd = odd_y
-                    else:
-                        two = jnp.broadcast_to(z_two[y, f : f + 1, :], lane.shape)
-                        one = jnp.broadcast_to(z_one[y, f : f + 1, :], lane.shape)
-                        odd = odd_z
-                    from_below = jnp.where(odd, one, two)
-                    from_above = jnp.where(odd, two, one)
-                    if s == 1:
-                        from_below = pltpu.roll(from_below, FACE, 1)
-                        from_above = pltpu.roll(from_above, FACE, 1)
-                    if d == 1:
-                        lower = jnp.where(y == 0, from_below, trace_ref[s, below, f, :, half])
-                        higher = jnp.where(y == last_y, from_above, trace_ref[s, above, f, :, half])
-                    else:
-                        lower = jnp.where(z_pos == 0, from_below, pltpu.roll(inside, 1, 0))
-                        higher = jnp.where(
-                            z_pos == count_z - 1, from_above, pltpu.roll(inside, count_z - 1, 0)
-                        )
-                    mixed = jnp.where(upper, lower, higher)
-                    jump = jnp.take_along_axis(mixed, source, axis=1) - inside
-                    keep = keep_velocity if f < 3 else keep_stress
-                    jump = jnp.where(rim, inside * keep, jump)
+                    inside = trace_ref[s, y, f, :, :LANES]
+                    mixed = jnp.where(
+                        upper, trace_ref[s, y - 1, f, :, :LANES], trace_ref[s, y + 1, f, :, :LANES]
+                    )
+                    jump = jnp.take_along_axis(mixed, turn, axis=1) - inside
                     jumps.append(jump)
                     if s == 1:
-                        term = stored_ref[y, f, :, d * LANES : (d + 1) * LANES] * jump
-                        if d == 1:
-                            sum_ref[y, f] = term
-                        else:
-                            sum_ref[y, f] += term
-                for f, term in enumerate(face_flux(jumps, d, coefs)):
-                    flux_ref[y, s, f, :, half] = term
+                        sum_ref[y, f] += stored_ref[y, f, :, LANES : 2 * LANES] * jump
+                for f, term in enumerate(face_flux(jumps, 1, coefs)):
+                    flux_ref[y, s, f, :, :LANES] = term
+
         return carry
 
     lax.fori_loop(0, count_y, row, 0)
 
 
-def side_faces(traces, y_two, y_one, z_two, z_one, coef, source, edge, stored):
+def side_faces(traces, z_two, z_one, coef, source, edge, stored):
     _, count_y, fields, count_z, _ = traces.shape
     return pl.pallas_call(
         side_kernel,
@@ -390,25 +386,27 @@
             jax.ShapeDtypeStruct((count_y, 2, fields, count_z, 2 * LANES), jnp.bfloat16),
             jax.ShapeDtypeStruct((count_y, fields, count_z, LANES), jnp.float32),
         ),
-        in_specs=[pl.BlockSpec(memory_space=pltpu.VMEM)] * 9,
+        in_specs=[pl.BlockSpec(memory_space=pltpu.VMEM)] * 7,
         out_specs=(pl.BlockSpec(memory_space=pltpu.VMEM),) * 2,
         compiler_params=pltpu.CompilerParams(vmem_limit_bytes=LIMIT),
         cost_estimate=pl.CostEstimate(flops=10**6, bytes_accessed=10**5, transcendentals=0),
         name="side_faces",
-    )(traces, y_two, y_one, z_two, z_one, coef, source, edge, stored)
+    )(traces, z_two, z_one, coef, source, edge, stored)
 
 
 def final_kernel(
-    state_ref, far_ref, near_ref, coef_ref, source_ref, side_ref, side_sum_ref, partial_ref,
-    stored_ref, lift_ref,
+    state_ref, trace_ref, far_ref, near_ref, y_two, y_one, coef_ref, source_ref, edge_ref,
+    side_ref, side_sum_ref, partial_ref, stored_ref, lift_ref,
     advanced_ref, kernel_ref,
-    flux_ref, out_ref, out_sem,
+    flux_ref, sum_ref, out_ref, out_sem,
 ):
     _, count_y, fields, count_z, nodes = state_ref.shape
+    last_y = count_y - 1
     lane = lane_index((count_z, LANES))
     upper = lane >= FACE
     z_pos = lax.broadcasted_iota(jnp.int32, lane.shape, 0)
     take_near = upper == odd_position("gx")
+    odd_y = odd_position("gy")
 
     def write(s, y):
         return pltpu.make_async_copy(out_ref.at[s, y], advanced_ref.at[s, y], out_sem.at[s, y])
@@ -431,19 +429,46 @@
                 jump = jnp.take_along_axis(mixed, source, axis=1) - inside
                 jumps.append(jump)
                 if s == 1:
-                    terms = side_sum_ref[y, f] + stored_ref[y, f, :, :LANES] * jump
-                    sums = jnp.sum(terms, axis=1, keepdims=True) * (1.0 / FACE)
-                    across = jnp.sum(jnp.where(z_pos == lane, sums, 0.0), axis=0, keepdims=True)
-                    kernel_ref[f, pl.ds(y, 1), :] = across[:, :count_z]
+                    sum_ref[f] = side_sum_ref[y, f] + stored_ref[y, f, :, :LANES] * jump
             for f, term in enumerate(face_flux(jumps, 0, coefs)):
-                flux_ref[s, f] = term
+                flux_ref[s, f, :, :LANES] = term
+        at_rim = jnp.logical_or(y == 0, y == last_y)
+
+        @pl.when(jnp.logical_not(at_rim))
+        def _():
+            flux_ref[:, :, :, LANES:] = side_ref[y, :, :, :, :LANES]
+
+        @pl.when(at_rim)
+        def _():
+            edge = (edge_ref[0, 0, y], edge_ref[0, 1, y])
+            turn = source_ref[1, y]
+            first = y == 0
+            take_two = jnp.logical_xor(first, odd_y)
+            outer = upper == first
+            inner_row = jnp.where(first, jnp.minimum(1, last_y), last_y - 1)
+            for s in range(2):
+                jumps = []
+                for f in range(fields):
+                    received = jnp.where(take_two, y_two[f], y_one[f])
+                    if s == 1:
+                        received = pltpu.roll(received, FACE, 1)
+                    inside = trace_ref[s, y, f, :, :LANES]
+                    mixed = jnp.where(outer, received, trace_ref[s, inner_row, f, :, :LANES])
+                    turned = jnp.take_along_axis(mixed, turn, axis=1)
+                    jump = rim_jump(turned, inside, edge, f)
+                    jumps.append(jump)
+                    if s == 1:
+                        sum_ref[f] += stored_ref[y, f, :, LANES : 2 * LANES] * jump
+                for f, term in enumerate(face_flux(jumps, 1, coefs)):
+                    flux_ref[s, f, :, LANES:] = term
+
         lifted = jnp.dot(
-            side_ref[y].reshape(2 * fields * count_z, 2 * LANES),
-            lift_ref[LANES:],
+            flux_ref[...].reshape(2 * fields * count_z, 2 * LANES),
+            lift_ref[: 2 * LANES],
             preferred_element_type=jnp.float32,
         ) + jnp.dot(
-            flux_ref[...].reshape(2 * fields * count_z, LANES),
-            lift_ref[:LANES],
+            side_ref[y, :, :, :, LANES:].reshape(2 * fields * count_z, LANES),
+            lift_ref[2 * LANES :],
             preferred_element_type=jnp.float32,
         )
         lifted = lifted.reshape(2, fields, count_z, nodes)
@@ -451,6 +476,10 @@
             scale = step_size if s == 0 else -step_size
             out_ref[s, y] = partial_ref[s, y] + scale * lifted[s]
             write(s, y).start()
+        for f in range(fields):
+            sums = jnp.sum(sum_ref[f], axis=1, keepdims=True) * (1.0 / FACE)
+            across = jnp.sum(jnp.where(z_pos == lane, sums, 0.0), axis=0, keepdims=True)
+            kernel_ref[f, pl.ds(y, 1), :] = across[:, :count_z]
         return carry
 
     lax.fori_loop(0, count_y, row, 0)
@@ -459,7 +488,9 @@
             write(s, y).wait()
 
 
-def finish(state, far, near, coef, source, side, side_sum, part, stored, lift):
+def finish(
+    state, traces, far, near, y_two, y_one, coef, source, edge, side, side_sum, part, stored, lift
+):
     _, count_y, fields, count_z, nodes = state.shape
     f32 = jnp.float32
     outs = (
@@ -469,17 +500,18 @@
     return pl.pallas_call(
         final_kernel,
         out_shape=outs,
-        in_specs=[pl.BlockSpec(memory_space=pltpu.VMEM)] * 10,
+        in_specs=[pl.BlockSpec(memory_space=pltpu.VMEM)] * 14,
         out_specs=(pl.BlockSpec(memory_space=pl.ANY), pl.BlockSpec(memory_space=pltpu.VMEM)),
         scratch_shapes=[
-            pltpu.VMEM((2, fields, count_z, LANES), jnp.bfloat16),
+            pltpu.VMEM((2, fields, count_z, 2 * LANES), jnp.bfloat16),
+            pltpu.VMEM((fields, count_z, LANES), f32),
             pltpu.VMEM(state.shape, f32),
             pltpu.SemaphoreType.DMA((2, count_y)),
         ],
         compiler_params=pltpu.CompilerParams(vmem_limit_bytes=LIMIT),
         cost_estimate=pl.CostEstimate(flops=9 * 10**8, bytes_accessed=10**7, transcendentals=0),
         name="finish",
-    )(state, far, near, coef, source, side, side_sum, part, stored, lift)
+    )(state, traces, far, near, y_two, y_one, coef, source, edge, side, side_sum, part, stored, lift)
 
 
 def swaps(count, start, wrap):
@@ -490,15 +522,14 @@
     return pairs
 
 
-def inner_swaps(count_y, count_z):
+def inner_swaps(count, other):
     pairs = []
-    for y in range(count_y):
-        for z in range(count_z):
-            if z in (0, count_z - 1):
-                target = (y ^ 1, z)
+    for i in range(count):
+        for k in range(other):
+            if i in (0, count - 1):
+                pairs.append((i, k, i, k ^ 1))
             else:
-                target = (y, z + 1 if z % 2 == 1 else z - 1)
-            pairs.append((y * count_z + z, target[0] * count_z + target[1]))
+                pairs.append((i, k, i + 1 if i % 2 == 1 else i - 1, k))
     return pairs
 
 
@@ -514,17 +545,18 @@
     near_in = lax.ppermute(near, "gx", swaps(nx, 0, True))
     traces, y_two, y_one, z_two, z_one = extract_traces(view, table)
     y_one = lax.ppermute(y_one, "gy", swaps(ny, 0, False))
-    y_two = lax.ppermute(y_two, "gy", swaps(ny, 1, True))
+    pairs = [(y * nz + z, b * nz + a) for y, z, b, a in inner_swaps(ny, nz)]
+    y_two = lax.ppermute(y_two, ("gy", "gz"), pairs)
     z_one = lax.ppermute(z_one, "gz", swaps(nz, 0, False))
     medium = material[:, 0]
     z_two, medium, y_one = lax.optimization_barrier((z_two, medium, y_one))
-    z_two = lax.ppermute(z_two, ("gy", "gz"), inner_swaps(ny, nz))
+    pairs = [(y * nz + z, b * nz + a) for z, y, a, b in inner_swaps(nz, ny)]
+    z_two = lax.ppermute(z_two, ("gy", "gz"), pairs)
     part, coef, source, edge = volume(view, deriv, medium, orient_view, flags_view)
-    side, side_sum = side_faces(
-        traces, y_two, y_one, z_two, z_one, coef, source, edge, stored_view
-    )
+    side, side_sum = side_faces(traces, z_two, z_one, coef, source, edge, stored_view)
     advanced, kernel = finish(
-        view, far_in, near_in, coef, source, side, side_sum, part, stored_view, lift
+        view, traces, far_in, near_in, y_two, y_one, coef, source, edge, side, side_sum, part,
+        stored_view, lift,
     )
     return (
         jnp.transpose(advanced, (0, 1, 3, 2, 4))[:, None],

time: 23.2 us -> 21 us (0.905)
  Pallas kernels: 10.7 us -> 9.78 us
  waiting for transfers between devices: 1.84 us -> 1.01 us
  starting transfers between devices: 9.79 us -> 9.27 us
    pallas_call x1, Pallas kernels: 2.33 us -> 0.83 us  [side_faces(): pl.pallas_call(side_kernel, out_shape=(jax.ShapeDtypeStruct((count_y, 2,...]
    ppermute x2, waiting for transfers between devices: 1.83 us -> 1 us  [the longest x1 1 us: local(): y_two = lax.ppermute(y_two, ('gy', 'gz'), pairs)]
    pallas_call x1, Pallas kernels: 2.99 us -> 3.59 us  [finish(): pl.pallas_call(final_kernel, out_shape=outs, in_specs=[pl.BlockSpec(memor...]
    ppermute x2, starting transfers between devices: 1 us -> 0.47 us  [the longest x1 0.29 us: local(): y_two = lax.ppermute(y_two, ('gy', 'gz'), pairs)]
  transfers between devices with their start and end apart: 6 -> 6, of which waited for: 1 -> 1; matrix products, arithmetic and copies ran while one was open for 0% -> 0% of each run, Pallas kernels for 26% -> 21%
where the time goes in v6:
time: 21 us; the launch traced here: 20.8 us
  Pallas kernels  9.78 us (47%)
  starting transfers between devices  9.27 us (44%)
  waiting for transfers between devices  1.01 us (5%)
  between operations  0.76 us (4%)
    ppermute x1, starting transfers between devices, local(): far_in = lax.ppermute(far, 'gx', swaps(nx, 1, True))  6.1 us
    pallas_call x1, Pallas kernels, finish(): pl.pallas_call(final_kernel, out_shape=outs, in_specs=[pl.BlockSpec(memor...  3.59 us
    pallas_call x1, Pallas kernels, volume(): pl.pallas_call(volume_kernel, out_shape=outs, in_specs=[pl.BlockSpec(memo...  2.51 us
    pallas_call x1, Pallas kernels, pack_faces(): pl.pallas_call(pack_kernel, out_shape=(jax.ShapeDtypeStruct(state.shape,...  1.79 us
    ppermute x1, starting transfers between devices, local(): z_one = lax.ppermute(z_one, 'gz', swaps(nz, 0, False))  1.64 us
    pallas_call x1, Pallas kernels, extract_traces(): pl.pallas_call(trace_kernel, out_shape=(jax.ShapeDtypeStruct((2, count_y,...  1.06 us
    ppermute x1, starting transfers between devices, local(): y_one = lax.ppermute(y_one, 'gy', swaps(ny, 0, False))  1.04 us
    ppermute x1, waiting for transfers between devices, local(): y_two = lax.ppermute(y_two, ('gy', 'gz'), pairs)  1 us
  transfers between devices with their start and end apart: 6, of which 1 were waited for; matrix products, arithmetic and copies ran while one was open for 0% of the time, Pallas kernels for 21%

profile of v6, /device:TPU:1, one launch (start us, length us, event | category | flops | bytes accessed | tf_op | source)
XLA Modules:
  0.0 20.8 jit_solution(11378637329035315020)
XLA Ops:
  0.6 0.0 copy-start.3
  0.6 0.0 copy-start.1
  0.7 0.0 copy-start.4
  0.7 0.0 copy-start.5
  0.7 0.0 copy-start.6
  0.7 1.8 %pack_faces.1 = (f32[2,4,9,16,512]{4,3,2,1,0:T(8,128)S(1)}, f32[4,9,16,128]{3,2,1,0:T(8,128)S(1)}, f32[4,9,16,128]{3,2,1,0:T(8,128)S(1)}) custom-call(f32[2,4,9,16,512]{4,3,2,1,0:T(8,128)} %bitcast.26), custom_call_target="tpu_custom_call" | custom-call | flops 1000000 | bytes 2000000 | tf_op jit(solution)/shard_map/pack_faces/pallas_call | solution.py:76
  2.5 6.1 %collective-permute-start = (f32[4,9,16,128]{3,2,1,0:T(8,128)S(1)}, f32[4,9,16,128]{3,2,1,0:T(8,128)S(1)}, u32[]{:S(2)}, u32[]{:S(2)}) collective-permute-start(f32[4,9,16,128]{3,2,1,0:T(8,128)S(1)} %get-tuple-element.23), channel_id=1, source_target_pairs={{16,32},{32,16},{48,64},{64,48},{80,96},{96,80},{112,0},{0,112},{1... | collective-permute-start | bytes 884744 | tf_op jit(solution)/shard_map/ppermute | solution.py:544
  8.6 0.0 collective-permute-start.1
  8.6 0.0 copy-done.3
  8.6 1.1 %extract_traces.1 = (f32[2,4,9,16,256]{4,3,2,1,0:T(8,128)S(1)}, f32[9,16,128]{2,1,0:T(8,128)S(1)}, f32[9,16,128]{2,1,0:T(8,128)S(1)}, f32[2,4,9,128]{3,2,1,0:T(8,128)S(1)}, f32[2,4,9,128]{3,2,1,0:T(8,128)S(1)}) custom-call(f32[2,4,9,16,512]{4,3,2,1,0:T(8,128)S(1)} %get-tuple-element.21.state_ref, bf16[512,256]{1,0:T(8,128)(2,1)S(1)} %copy-done.3), custom_call_target="tpu_custom_call" | custom-call | flops 600000000 | bytes 4000000 | tf_op jit(solution)/shard_map/extract_traces/pallas_call | solution.py:122
  9.7 0.0 copy-start
  9.7 1.0 %collective-permute-start.3 = (f32[9,16,128]{2,1,0:T(8,128)S(1)}, f32[9,16,128]{2,1,0:T(8,128)S(1)}, u32[]{:S(2)}, u32[]{:S(2)}) collective-permute-start(f32[9,16,128]{2,1,0:T(8,128)S(1)} %get-tuple-element.27), channel_id=1, source_target_pairs={{0,4},{4,0},{8,12},{12,8},{1,5},{5,1},{9,13},{13,9},{2,6},{6,2},{1... | collective-permute-start | bytes 221192 | tf_op jit(solution)/shard_map/ppermute | solution.py:547
  10.7 0.3 %collective-permute-start.2 = (f32[9,16,128]{2,1,0:T(8,128)S(1)}, f32[9,16,128]{2,1,0:T(8,128)S(1)}, u32[]{:S(2)}, u32[]{:S(2)}) collective-permute-start(f32[9,16,128]{2,1,0:T(8,128)S(1)} %get-tuple-element.25), channel_id=1, source_target_pairs={{0,1},{1,0},{2,3},{3,2},{4,8},{5,9},{6,10},{7,11},{8,4},{9,5},{10,... | collective-permute-start | bytes 221192 | tf_op jit(solution)/shard_map/ppermute | solution.py:549
  11.0 1.6 %collective-permute-start.5 = (f32[2,4,9,128]{3,2,1,0:T(8,128)S(1)}, f32[2,4,9,128]{3,2,1,0:T(8,128)S(1)}, u32[]{:S(2)}, u32[]{:S(2)}) collective-permute-start(f32[2,4,9,128]{3,2,1,0:T(8,128)S(1)} %get-tuple-element.34), channel_id=1, source_target_pairs={{0,1},{1,0},{2,3},{3,2},{4,5},{5,4},{6,7},{7,6},{8,9},{9,8},{10,11... | collective-permute-start | bytes 110600 | tf_op jit(solution)/shard_map/ppermute | solution.py:550
  12.6 0.0 collective-permute-done.3.y_one
  12.6 0.2 collective-permute-start.4
  12.8 0.0 copy-done.1
  12.8 0.0 copy-done.4
  12.8 0.0 copy-done.5
  12.8 0.0 copy-done.6
  12.8 0.0 copy-start.2
  12.9 2.5 %volume.1 = (f32[2,4,9,16,512]{4,3,2,1,0:T(8,128)S(1)}, f32[4,4,16,128]{3,2,1,0:T(8,128)S(1)}, s32[3,4,16,128]{3,2,1,0:T(8,128)S(1)}, f32[2,2,4,16,128]{4,3,2,1,0:T(8,128)S(1)}) custom-call(f32[2,4,9,16,512]{4,3,2,1,0:T(8,128)S(1)} %get-tuple-element.21.state_ref, bf16[512,1536]{1,0:T(8,128)(2,1)S(1)} %copy-done.1, f32[3,4,16]{2,1,0:T(4,128)S(1)} %bitcast.25, ...), custom_call_target="tpu_custom_call" | custom-call | flops 1000000 | bytes 100000 | tf_op jit(solution)/shard_map/volume/pallas_call | solution.py:284
  15.4 0.0 collective-permute-done.5.z_one
  15.4 0.0 collective-permute-done.4.z_two
  15.4 0.0 copy-done
  15.4 0.8 %side_faces.1 = (bf16[4,2,9,16,256]{4,3,2,1,0:T(8,128)(2,1)S(1)}, f32[4,9,16,128]{3,2,1,0:T(8,128)S(1)}) custom-call(f32[2,4,9,16,256]{4,3,2,1,0:T(8,128)S(1)} %get-tuple-element.22.trace_ref, f32[2,4,9,128]{3,2,1,0:T(8,128)S(1)} %collective-permute-done.4.z_two, f32[2,4,9,128]{3,2,1,0:T(8,128)S(1)} %collective-permute-done.5.z_one, ...), custom_call_target="tpu_custom_call" | custom-call | flops 1000000 | bytes 100000 | tf_op jit(solution)/shard_map/side_faces/pallas_call | solution.py:383
  16.2 1.0 %collective-permute-done.2.y_two = f32[9,16,128]{2,1,0:T(8,128)S(1)} collective-permute-done((f32[9,16,128]{2,1,0:T(8,128)S(1)}, f32[9,16,128]{2,1,0:T(8,128)S(1)}, u32[]{:S(2)}, u32[]{:S(2)}) %collective-permute-start.2) | collective-permute-done | bytes 73760 | tf_op jit(solution)/shard_map/ppermute | solution.py:549
  17.2 0.0 collective-permute-done.far_ref
  17.2 0.0 collective-permute-done.1.near_ref
  17.3 0.0 copy-done.2
  17.3 3.6 %finish.1 = (f32[2,4,9,16,512]{4,3,2,1,0:T(8,128)}, f32[9,4,16]{2,1,0:T(4,128)}) custom-call(f32[2,4,9,16,512]{4,3,2,1,0:T(8,128)S(1)} %get-tuple-element.21.state_ref, f32[2,4,9,16,256]{4,3,2,1,0:T(8,128)S(1)} %get-tuple-element.22.trace_ref, f32[4,9,16,128]{3,2,1,0:T(8,128)S(1)} %collective-permute-done.far_ref, ...), custom_call_target="tpu_custom_call" | custom-call | flops 900000000 | bytes 10000000 | tf_op jit(solution)/shard_map/finish/pallas_call | solution.py:500
Async XLA Ops:
  0.6 8.0 %copy-start.3 = (bf16[512,256]{1,0:T(8,128)(2,1)S(1)}, bf16[512,256]{1,0:T(8,128)(2,1)}, u32[]{:S(2)}) copy-start(bf16[512,256]{1,0:T(8,128)(2,1)} %constant.2.clone.table_ref) | copy-start | bytes 786436
  0.6 12.2 %copy-start.1 = (bf16[512,1536]{1,0:T(8,128)(2,1)S(1)}, bf16[512,1536]{1,0:T(8,128)(2,1)}, u32[]{:S(2)}) copy-start(bf16[512,1536]{1,0:T(8,128)(2,1)} %deriv_ref.1) | copy-start | bytes 4718596
  0.7 12.2 %copy-start.4 = (s32[1,4,16,6]{2,1,3,0:T(4,128)S(1)}, s32[1,4,16,6]{2,1,3,0:T(4,128)}, u32[]{:S(2)}) copy-start(s32[1,4,16,6]{2,1,3,0:T(4,128)} %param.13) | copy-start | bytes 4612
  0.7 12.2 %copy-start.5 = (s32[1,4,16,6]{2,1,3,0:T(4,128)S(1)}, s32[1,4,16,6]{2,1,3,0:T(4,128)}, u32[]{:S(2)}) copy-start(s32[1,4,16,6]{2,1,3,0:T(4,128)} %param.14) | copy-start | bytes 4612
  0.7 12.2 %copy-start.6 = (f32[3,1,4,16]{3,2,1,0:T(4,128)S(1)}, f32[3,1,4,16]{3,2,1,0:T(4,128)}, u32[]{:S(2)}) copy-start(f32[3,1,4,16]{3,2,1,0:T(4,128)} %param.11) | copy-start | bytes 2308
  2.5 14.8 %collective-permute-start = (f32[4,9,16,128]{3,2,1,0:T(8,128)S(1)}, f32[4,9,16,128]{3,2,1,0:T(8,128)S(1)}, u32[]{:S(2)}, u32[]{:S(2)}) collective-permute-start(f32[4,9,16,128]{3,2,1,0:T(8,128)S(1)} %get-tuple-element.23), channel_id=1, source_target_pairs={{16,32},{32,16},{48,64},{64,48},{80,96},{96,80},{112,0},{0,112},{1... | collective-permute-start | bytes 884744 | tf_op jit(solution)/shard_map/ppermute | solution.py:544
  8.6 8.7 %collective-permute-start.1 = (f32[4,9,16,128]{3,2,1,0:T(8,128)S(1)}, f32[4,9,16,128]{3,2,1,0:T(8,128)S(1)}, u32[]{:S(2)}, u32[]{:S(2)}) collective-permute-start(f32[4,9,16,128]{3,2,1,0:T(8,128)S(1)} %get-tuple-element.24), channel_id=1, source_target_pairs={{0,16},{16,0},{32,48},{48,32},{64,80},{80,64},{96,112},{112,96},{1... | collective-permute-start | bytes 884744 | tf_op jit(solution)/shard_map/ppermute | solution.py:545
  9.7 5.7 %copy-start = (f32[1,4,16,9,384]{4,2,3,1,0:T(8,128)S(1)}, f32[1,4,16,9,384]{4,2,3,1,0:T(8,128)}, u32[]{:S(2)}) copy-start(f32[1,4,16,9,384]{4,2,3,1,0:T(8,128)} %param.12) | copy-start | bytes 2654212
  9.7 3.0 %collective-permute-start.3 = (f32[9,16,128]{2,1,0:T(8,128)S(1)}, f32[9,16,128]{2,1,0:T(8,128)S(1)}, u32[]{:S(2)}, u32[]{:S(2)}) collective-permute-start(f32[9,16,128]{2,1,0:T(8,128)S(1)} %get-tuple-element.27), channel_id=1, source_target_pairs={{0,4},{4,0},{8,12},{12,8},{1,5},{5,1},{9,13},{13,9},{2,6},{6,2},{1... | collective-permute-start | bytes 221192 | tf_op jit(solution)/shard_map/ppermute | solution.py:547
  10.7 6.5 %collective-permute-start.2 = (f32[9,16,128]{2,1,0:T(8,128)S(1)}, f32[9,16,128]{2,1,0:T(8,128)S(1)}, u32[]{:S(2)}, u32[]{:S(2)}) collective-permute-start(f32[9,16,128]{2,1,0:T(8,128)S(1)} %get-tuple-element.25), channel_id=1, source_target_pairs={{0,1},{1,0},{2,3},{3,2},{4,8},{5,9},{6,10},{7,11},{8,4},{9,5},{10,... | collective-permute-start | bytes 221192 | tf_op jit(solution)/shard_map/ppermute | solution.py:549
  11.0 4.4 %collective-permute-start.5 = (f32[2,4,9,128]{3,2,1,0:T(8,128)S(1)}, f32[2,4,9,128]{3,2,1,0:T(8,128)S(1)}, u32[]{:S(2)}, u32[]{:S(2)}) collective-permute-start(f32[2,4,9,128]{3,2,1,0:T(8,128)S(1)} %get-tuple-element.34), channel_id=1, source_target_pairs={{0,1},{1,0},{2,3},{3,2},{4,5},{5,4},{6,7},{7,6},{8,9},{9,8},{10,11... | collective-permute-start | bytes 110600 | tf_op jit(solution)/shard_map/ppermute | solution.py:550
  12.6 2.7 %collective-permute-start.4 = (f32[2,4,9,128]{3,2,1,0:T(8,128)S(1)}, f32[2,4,9,128]{3,2,1,0:T(8,128)S(1)}, u32[]{:S(2)}, u32[]{:S(2)}) collective-permute-start(f32[2,4,9,128]{3,2,1,0:T(8,128)S(1)} %get-tuple-element.33), channel_id=1, source_target_pairs={{0,4},{4,0},{8,12},{12,8},{1,2},{5,6},{9,10},{13,14},{2,1},{6,5},{... | collective-permute-start | bytes 110600 | tf_op jit(solution)/shard_map/ppermute | solution.py:554
  12.8 4.4 %copy-start.2 = (bf16[384,512]{1,0:T(8,128)(2,1)S(1)}, bf16[384,512]{1,0:T(8,128)(2,1)}, u32[]{:S(2)}) copy-start(bf16[384,512]{1,0:T(8,128)(2,1)} %lift_ref.1) | copy-start | bytes 1179652

commit v7 on v6

--- a/solution.py
+++ b/solution.py
@@ -411,7 +411,10 @@
     def write(s, y):
         return pltpu.make_async_copy(out_ref.at[s, y], advanced_ref.at[s, y], out_sem.at[s, y])
 
-    def row(y, carry):
+    order = list(range(1, last_y)) + [0, last_y]
+
+    def fluxes(y):
+        slot = order.index(y) % 2
         coefs = [coef_ref[k, y] for k in range(4)]
         for s in range(2):
             source = source_ref[0, y]
@@ -429,60 +432,58 @@
                 jump = jnp.take_along_axis(mixed, source, axis=1) - inside
                 jumps.append(jump)
                 if s == 1:
-                    sum_ref[f] = side_sum_ref[y, f] + stored_ref[y, f, :, :LANES] * jump
+                    sum_ref[slot, f] = side_sum_ref[y, f] + stored_ref[y, f, :, :LANES] * jump
             for f, term in enumerate(face_flux(jumps, 0, coefs)):
-                flux_ref[s, f, :, :LANES] = term
-        at_rim = jnp.logical_or(y == 0, y == last_y)
-
-        @pl.when(jnp.logical_not(at_rim))
-        def _():
-            flux_ref[:, :, :, LANES:] = side_ref[y, :, :, :, :LANES]
-
-        @pl.when(at_rim)
-        def _():
-            edge = (edge_ref[0, 0, y], edge_ref[0, 1, y])
-            turn = source_ref[1, y]
-            first = y == 0
-            take_two = jnp.logical_xor(first, odd_y)
-            outer = upper == first
-            inner_row = jnp.where(first, jnp.minimum(1, last_y), last_y - 1)
-            for s in range(2):
-                jumps = []
-                for f in range(fields):
-                    received = jnp.where(take_two, y_two[f], y_one[f])
-                    if s == 1:
-                        received = pltpu.roll(received, FACE, 1)
-                    inside = trace_ref[s, y, f, :, :LANES]
-                    mixed = jnp.where(outer, received, trace_ref[s, inner_row, f, :, :LANES])
-                    turned = jnp.take_along_axis(mixed, turn, axis=1)
-                    jump = rim_jump(turned, inside, edge, f)
-                    jumps.append(jump)
-                    if s == 1:
-                        sum_ref[f] += stored_ref[y, f, :, LANES : 2 * LANES] * jump
-                for f, term in enumerate(face_flux(jumps, 1, coefs)):
-                    flux_ref[s, f, :, LANES:] = term
-
-        lifted = jnp.dot(
-            flux_ref[...].reshape(2 * fields * count_z, 2 * LANES),
-            lift_ref[: 2 * LANES],
-            preferred_element_type=jnp.float32,
-        ) + jnp.dot(
-            side_ref[y, :, :, :, LANES:].reshape(2 * fields * count_z, LANES),
-            lift_ref[2 * LANES :],
-            preferred_element_type=jnp.float32,
-        )
-        lifted = lifted.reshape(2, fields, count_z, nodes)
+                flux_ref[slot, s, f, :, :LANES] = term
+        if 0 < y < last_y:
+            flux_ref[slot, :, :, :, LANES:] = side_ref[y, :, :, :, :LANES]
+            return
+        edge = (edge_ref[0, 0, y], edge_ref[0, 1, y])
+        turn = source_ref[1, y]
+        take_two = jnp.logical_not(odd_y) if y == 0 else odd_y
+        outer = upper if y == 0 else jnp.logical_not(upper)
+        inner_row = 1 if y == 0 else last_y - 1
         for s in range(2):
+            jumps = []
+            for f in range(fields):
+                received = jnp.where(take_two, y_two[f], y_one[f])
+                if s == 1:
+                    received = pltpu.roll(received, FACE, 1)
+                inside = trace_ref[s, y, f, :, :LANES]
+                mixed = jnp.where(outer, received, trace_ref[s, inner_row, f, :, :LANES])
+                turned = jnp.take_along_axis(mixed, turn, axis=1)
+                jump = rim_jump(turned, inside, edge, f)
+                jumps.append(jump)
+                if s == 1:
+                    sum_ref[slot, f] += stored_ref[y, f, :, LANES : 2 * LANES] * jump
+            for f, term in enumerate(face_flux(jumps, 1, coefs)):
+                flux_ref[slot, s, f, :, LANES:] = term
+
+    def results(y):
+        slot = order.index(y) % 2
+        for s in range(2):
+            lifted = jnp.dot(
+                flux_ref[slot, s].reshape(fields * count_z, 2 * LANES),
+                lift_ref[: 2 * LANES],
+                preferred_element_type=jnp.float32,
+            ) + jnp.dot(
+                side_ref[y, s, :, :, LANES:].reshape(fields * count_z, LANES),
+                lift_ref[2 * LANES :],
+                preferred_element_type=jnp.float32,
+            )
             scale = step_size if s == 0 else -step_size
-            out_ref[s, y] = partial_ref[s, y] + scale * lifted[s]
+            out_ref[s, y] = partial_ref[s, y] + scale * lifted.reshape(fields, count_z, nodes)
             write(s, y).start()
         for f in range(fields):
-            sums = jnp.sum(sum_ref[f], axis=1, keepdims=True) * (1.0 / FACE)
+            sums = jnp.sum(sum_ref[slot, f], axis=1, keepdims=True) * (1.0 / FACE)
             across = jnp.sum(jnp.where(z_pos == lane, sums, 0.0), axis=0, keepdims=True)
             kernel_ref[f, pl.ds(y, 1), :] = across[:, :count_z]
-        return carry
-
-    lax.fori_loop(0, count_y, row, 0)
+
+    fluxes(order[0])
+    for k, y in enumerate(order):
+        if k + 1 < count_y:
+            fluxes(order[k + 1])
+        results(y)
     for y in range(count_y):
         for s in range(2):
             write(s, y).wait()
@@ -503,8 +504,8 @@
         in_specs=[pl.BlockSpec(memory_space=pltpu.VMEM)] * 14,
         out_specs=(pl.BlockSpec(memory_space=pl.ANY), pl.BlockSpec(memory_space=pltpu.VMEM)),
         scratch_shapes=[
-            pltpu.VMEM((2, fields, count_z, 2 * LANES), jnp.bfloat16),
-            pltpu.VMEM((fields, count_z, LANES), f32),
+            pltpu.VMEM((2, 2, fields, count_z, 2 * LANES), jnp.bfloat16),
+            pltpu.VMEM((2, fields, count_z, LANES), f32),
             pltpu.VMEM(state.shape, f32),
             pltpu.SemaphoreType.DMA((2, count_y)),
         ],

time: 21 us -> 19.9 us (0.948)
  Pallas kernels: 9.78 us -> 8.66 us
    pallas_call x1, Pallas kernels: 3.59 us -> 2.48 us  [finish(): pl.pallas_call(final_kernel, out_shape=outs, in_specs=[pl.BlockSpec(memor...]
  transfers between devices with their start and end apart: 6 -> 6, of which waited for: 1 -> 1; matrix products, arithmetic and copies ran while one was open for 0% -> 0% of each run, Pallas kernels for 21% -> 22%
where the time goes in v7:
time: 19.9 us; the launch traced here: 19.7 us
  starting transfers between devices  9.27 us (47%)
  Pallas kernels  8.66 us (44%)
  waiting for transfers between devices  1.01 us (5%)
  between operations  0.76 us (4%)
    ppermute x1, starting transfers between devices, local(): far_in = lax.ppermute(far, 'gx', swaps(nx, 1, True))  6.1 us
    pallas_call x1, Pallas kernels, volume(): pl.pallas_call(volume_kernel, out_shape=outs, in_specs=[pl.BlockSpec(memo...  2.51 us
    pallas_call x1, Pallas kernels, finish(): pl.pallas_call(final_kernel, out_shape=outs, in_specs=[pl.BlockSpec(memor...  2.48 us
    pallas_call x1, Pallas kernels, pack_faces(): pl.pallas_call(pack_kernel, out_shape=(jax.ShapeDtypeStruct(state.shape,...  1.79 us
    ppermute x1, starting transfers between devices, local(): z_one = lax.ppermute(z_one, 'gz', swaps(nz, 0, False))  1.64 us
    pallas_call x1, Pallas kernels, extract_traces(): pl.pallas_call(trace_kernel, out_shape=(jax.ShapeDtypeStruct((2, count_y,...  1.06 us
    ppermute x1, starting transfers between devices, local(): y_one = lax.ppermute(y_one, 'gy', swaps(ny, 0, False))  1.04 us
    ppermute x1, waiting for transfers between devices, local(): y_two = lax.ppermute(y_two, ('gy', 'gz'), pairs)  1 us
  transfers between devices with their start and end apart: 6, of which 1 were waited for; matrix products, arithmetic and copies ran while one was open for 0% of the time, Pallas kernels for 22%

profile of v7, /device:TPU:1, one launch (start us, length us, event | category | flops | bytes accessed | tf_op | source)
XLA Modules:
  0.0 19.7 jit_solution(15509325659884427385)
XLA Ops:
  0.6 0.0 copy-start.3
  0.6 0.0 copy-start.1
  0.7 0.0 copy-start.4
  0.7 0.0 copy-start.5
  0.7 0.0 copy-start.6
  0.7 1.8 %pack_faces.1 = (f32[2,4,9,16,512]{4,3,2,1,0:T(8,128)S(1)}, f32[4,9,16,128]{3,2,1,0:T(8,128)S(1)}, f32[4,9,16,128]{3,2,1,0:T(8,128)S(1)}) custom-call(f32[2,4,9,16,512]{4,3,2,1,0:T(8,128)} %bitcast.26), custom_call_target="tpu_custom_call" | custom-call | flops 1000000 | bytes 2000000 | tf_op jit(solution)/shard_map/pack_faces/pallas_call | solution.py:76
  2.5 6.1 %collective-permute-start = (f32[4,9,16,128]{3,2,1,0:T(8,128)S(1)}, f32[4,9,16,128]{3,2,1,0:T(8,128)S(1)}, u32[]{:S(2)}, u32[]{:S(2)}) collective-permute-start(f32[4,9,16,128]{3,2,1,0:T(8,128)S(1)} %get-tuple-element.23), channel_id=1, source_target_pairs={{16,32},{32,16},{48,64},{64,48},{80,96},{96,80},{112,0},{0,112},{1... | collective-permute-start | bytes 884744 | tf_op jit(solution)/shard_map/ppermute | solution.py:545
  8.6 0.0 collective-permute-start.1
  8.6 0.0 copy-done.3
  8.6 1.1 %extract_traces.1 = (f32[2,4,9,16,256]{4,3,2,1,0:T(8,128)S(1)}, f32[9,16,128]{2,1,0:T(8,128)S(1)}, f32[9,16,128]{2,1,0:T(8,128)S(1)}, f32[2,4,9,128]{3,2,1,0:T(8,128)S(1)}, f32[2,4,9,128]{3,2,1,0:T(8,128)S(1)}) custom-call(f32[2,4,9,16,512]{4,3,2,1,0:T(8,128)S(1)} %get-tuple-element.21.state_ref, bf16[512,256]{1,0:T(8,128)(2,1)S(1)} %copy-done.3), custom_call_target="tpu_custom_call" | custom-call | flops 600000000 | bytes 4000000 | tf_op jit(solution)/shard_map/extract_traces/pallas_call | solution.py:122
  9.7 0.0 copy-start
  9.7 1.0 %collective-permute-start.3 = (f32[9,16,128]{2,1,0:T(8,128)S(1)}, f32[9,16,128]{2,1,0:T(8,128)S(1)}, u32[]{:S(2)}, u32[]{:S(2)}) collective-permute-start(f32[9,16,128]{2,1,0:T(8,128)S(1)} %get-tuple-element.27), channel_id=1, source_target_pairs={{0,4},{4,0},{8,12},{12,8},{1,5},{5,1},{9,13},{13,9},{2,6},{6,2},{1... | collective-permute-start | bytes 221192 | tf_op jit(solution)/shard_map/ppermute | solution.py:548
  10.7 0.3 %collective-permute-start.2 = (f32[9,16,128]{2,1,0:T(8,128)S(1)}, f32[9,16,128]{2,1,0:T(8,128)S(1)}, u32[]{:S(2)}, u32[]{:S(2)}) collective-permute-start(f32[9,16,128]{2,1,0:T(8,128)S(1)} %get-tuple-element.25), channel_id=1, source_target_pairs={{0,1},{1,0},{2,3},{3,2},{4,8},{5,9},{6,10},{7,11},{8,4},{9,5},{10,... | collective-permute-start | bytes 221192 | tf_op jit(solution)/shard_map/ppermute | solution.py:550
  11.0 1.6 %collective-permute-start.5 = (f32[2,4,9,128]{3,2,1,0:T(8,128)S(1)}, f32[2,4,9,128]{3,2,1,0:T(8,128)S(1)}, u32[]{:S(2)}, u32[]{:S(2)}) collective-permute-start(f32[2,4,9,128]{3,2,1,0:T(8,128)S(1)} %get-tuple-element.34), channel_id=1, source_target_pairs={{0,1},{1,0},{2,3},{3,2},{4,5},{5,4},{6,7},{7,6},{8,9},{9,8},{10,11... | collective-permute-start | bytes 110600 | tf_op jit(solution)/shard_map/ppermute | solution.py:551
  12.6 0.0 collective-permute-done.3.y_one
  12.6 0.2 collective-permute-start.4
  12.8 0.0 copy-done.1
  12.8 0.0 copy-done.4
  12.8 0.0 copy-done.5
  12.8 0.0 copy-done.6
  12.8 0.0 copy-start.2
  12.9 2.5 %volume.1 = (f32[2,4,9,16,512]{4,3,2,1,0:T(8,128)S(1)}, f32[4,4,16,128]{3,2,1,0:T(8,128)S(1)}, s32[3,4,16,128]{3,2,1,0:T(8,128)S(1)}, f32[2,2,4,16,128]{4,3,2,1,0:T(8,128)S(1)}) custom-call(f32[2,4,9,16,512]{4,3,2,1,0:T(8,128)S(1)} %get-tuple-element.21.state_ref, bf16[512,1536]{1,0:T(8,128)(2,1)S(1)} %copy-done.1, f32[3,4,16]{2,1,0:T(4,128)S(1)} %bitcast.25, ...), custom_call_target="tpu_custom_call" | custom-call | flops 1000000 | bytes 100000 | tf_op jit(solution)/shard_map/volume/pallas_call | solution.py:284
  15.4 0.0 collective-permute-done.5.z_one
  15.4 0.0 collective-permute-done.4.z_two
  15.4 0.0 copy-done
  15.4 0.8 %side_faces.1 = (bf16[4,2,9,16,256]{4,3,2,1,0:T(8,128)(2,1)S(1)}, f32[4,9,16,128]{3,2,1,0:T(8,128)S(1)}) custom-call(f32[2,4,9,16,256]{4,3,2,1,0:T(8,128)S(1)} %get-tuple-element.22.trace_ref, f32[2,4,9,128]{3,2,1,0:T(8,128)S(1)} %collective-permute-done.4.z_two, f32[2,4,9,128]{3,2,1,0:T(8,128)S(1)} %collective-permute-done.5.z_one, ...), custom_call_target="tpu_custom_call" | custom-call | flops 1000000 | bytes 100000 | tf_op jit(solution)/shard_map/side_faces/pallas_call | solution.py:383
  16.2 1.0 %collective-permute-done.2.y_two = f32[9,16,128]{2,1,0:T(8,128)S(1)} collective-permute-done((f32[9,16,128]{2,1,0:T(8,128)S(1)}, f32[9,16,128]{2,1,0:T(8,128)S(1)}, u32[]{:S(2)}, u32[]{:S(2)}) %collective-permute-start.2) | collective-permute-done | bytes 73760 | tf_op jit(solution)/shard_map/ppermute | solution.py:550
  17.2 0.0 collective-permute-done.far_ref
  17.2 0.0 collective-permute-done.1.near_ref
  17.3 0.0 copy-done.2
  17.3 2.5 %finish.1 = (f32[2,4,9,16,512]{4,3,2,1,0:T(8,128)}, f32[9,4,16]{2,1,0:T(4,128)}) custom-call(f32[2,4,9,16,512]{4,3,2,1,0:T(8,128)S(1)} %get-tuple-element.21.state_ref, f32[2,4,9,16,256]{4,3,2,1,0:T(8,128)S(1)} %get-tuple-element.22.trace_ref, f32[4,9,16,128]{3,2,1,0:T(8,128)S(1)} %collective-permute-done.far_ref, ...), custom_call_target="tpu_custom_call" | custom-call | flops 900000000 | bytes 10000000 | tf_op jit(solution)/shard_map/finish/pallas_call | solution.py:501
Async XLA Ops:
  0.6 8.0 %copy-start.3 = (bf16[512,256]{1,0:T(8,128)(2,1)S(1)}, bf16[512,256]{1,0:T(8,128)(2,1)}, u32[]{:S(2)}) copy-start(bf16[512,256]{1,0:T(8,128)(2,1)} %constant.2.clone.table_ref) | copy-start | bytes 786436
  0.6 12.2 %copy-start.1 = (bf16[512,1536]{1,0:T(8,128)(2,1)S(1)}, bf16[512,1536]{1,0:T(8,128)(2,1)}, u32[]{:S(2)}) copy-start(bf16[512,1536]{1,0:T(8,128)(2,1)} %deriv_ref.1) | copy-start | bytes 4718596
  0.7 12.2 %copy-start.4 = (s32[1,4,16,6]{2,1,3,0:T(4,128)S(1)}, s32[1,4,16,6]{2,1,3,0:T(4,128)}, u32[]{:S(2)}) copy-start(s32[1,4,16,6]{2,1,3,0:T(4,128)} %param.13) | copy-start | bytes 4612
  0.7 12.2 %copy-start.5 = (s32[1,4,16,6]{2,1,3,0:T(4,128)S(1)}, s32[1,4,16,6]{2,1,3,0:T(4,128)}, u32[]{:S(2)}) copy-start(s32[1,4,16,6]{2,1,3,0:T(4,128)} %param.14) | copy-start | bytes 4612
  0.7 12.2 %copy-start.6 = (f32[3,1,4,16]{3,2,1,0:T(4,128)S(1)}, f32[3,1,4,16]{3,2,1,0:T(4,128)}, u32[]{:S(2)}) copy-start(f32[3,1,4,16]{3,2,1,0:T(4,128)} %param.11) | copy-start | bytes 2308
  2.5 14.8 %collective-permute-start = (f32[4,9,16,128]{3,2,1,0:T(8,128)S(1)}, f32[4,9,16,128]{3,2,1,0:T(8,128)S(1)}, u32[]{:S(2)}, u32[]{:S(2)}) collective-permute-start(f32[4,9,16,128]{3,2,1,0:T(8,128)S(1)} %get-tuple-element.23), channel_id=1, source_target_pairs={{16,32},{32,16},{48,64},{64,48},{80,96},{96,80},{112,0},{0,112},{1... | collective-permute-start | bytes 884744 | tf_op jit(solution)/shard_map/ppermute | solution.py:545
  8.6 8.7 %collective-permute-start.1 = (f32[4,9,16,128]{3,2,1,0:T(8,128)S(1)}, f32[4,9,16,128]{3,2,1,0:T(8,128)S(1)}, u32[]{:S(2)}, u32[]{:S(2)}) collective-permute-start(f32[4,9,16,128]{3,2,1,0:T(8,128)S(1)} %get-tuple-element.24), channel_id=1, source_target_pairs={{0,16},{16,0},{32,48},{48,32},{64,80},{80,64},{96,112},{112,96},{1... | collective-permute-start | bytes 884744 | tf_op jit(solution)/shard_map/ppermute | solution.py:546
  9.7 5.7 %copy-start = (f32[1,4,16,9,384]{4,2,3,1,0:T(8,128)S(1)}, f32[1,4,16,9,384]{4,2,3,1,0:T(8,128)}, u32[]{:S(2)}) copy-start(f32[1,4,16,9,384]{4,2,3,1,0:T(8,128)} %param.12) | copy-start | bytes 2654212
  9.7 3.0 %collective-permute-start.3 = (f32[9,16,128]{2,1,0:T(8,128)S(1)}, f32[9,16,128]{2,1,0:T(8,128)S(1)}, u32[]{:S(2)}, u32[]{:S(2)}) collective-permute-start(f32[9,16,128]{2,1,0:T(8,128)S(1)} %get-tuple-element.27), channel_id=1, source_target_pairs={{0,4},{4,0},{8,12},{12,8},{1,5},{5,1},{9,13},{13,9},{2,6},{6,2},{1... | collective-permute-start | bytes 221192 | tf_op jit(solution)/shard_map/ppermute | solution.py:548
  10.7 6.5 %collective-permute-start.2 = (f32[9,16,128]{2,1,0:T(8,128)S(1)}, f32[9,16,128]{2,1,0:T(8,128)S(1)}, u32[]{:S(2)}, u32[]{:S(2)}) collective-permute-start(f32[9,16,128]{2,1,0:T(8,128)S(1)} %get-tuple-element.25), channel_id=1, source_target_pairs={{0,1},{1,0},{2,3},{3,2},{4,8},{5,9},{6,10},{7,11},{8,4},{9,5},{10,... | collective-permute-start | bytes 221192 | tf_op jit(solution)/shard_map/ppermute | solution.py:550
  11.0 4.4 %collective-permute-start.5 = (f32[2,4,9,128]{3,2,1,0:T(8,128)S(1)}, f32[2,4,9,128]{3,2,1,0:T(8,128)S(1)}, u32[]{:S(2)}, u32[]{:S(2)}) collective-permute-start(f32[2,4,9,128]{3,2,1,0:T(8,128)S(1)} %get-tuple-element.34), channel_id=1, source_target_pairs={{0,1},{1,0},{2,3},{3,2},{4,5},{5,4},{6,7},{7,6},{8,9},{9,8},{10,11... | collective-permute-start | bytes 110600 | tf_op jit(solution)/shard_map/ppermute | solution.py:551
  12.6 2.7 %collective-permute-start.4 = (f32[2,4,9,128]{3,2,1,0:T(8,128)S(1)}, f32[2,4,9,128]{3,2,1,0:T(8,128)S(1)}, u32[]{:S(2)}, u32[]{:S(2)}) collective-permute-start(f32[2,4,9,128]{3,2,1,0:T(8,128)S(1)} %get-tuple-element.33), channel_id=1, source_target_pairs={{0,4},{4,0},{8,12},{12,8},{1,2},{5,6},{9,10},{13,14},{2,1},{6,5},{... | collective-permute-start | bytes 110600 | tf_op jit(solution)/shard_map/ppermute | solution.py:555
  12.8 4.4 %copy-start.2 = (bf16[384,512]{1,0:T(8,128)(2,1)S(1)}, bf16[384,512]{1,0:T(8,128)(2,1)}, u32[]{:S(2)}) copy-start(bf16[384,512]{1,0:T(8,128)(2,1)} %lift_ref.1) | copy-start | bytes 1179652

commit v8 on v7

--- a/solution.py
+++ b/solution.py
@@ -88,7 +88,7 @@
 def trace_kernel(state_ref, table_ref, trace_ref, y_two, y_one, z_two, z_one):
     _, count_y, fields, count_z, _ = state_ref.shape
 
-    def one_state(s, carry):
+    def one_state(s):
         values = state_ref[s].reshape(count_y * fields * count_z, -1)
         high = values.astype(jnp.bfloat16)
         low = (values - high.astype(jnp.float32)).astype(jnp.bfloat16)
@@ -96,9 +96,9 @@
         picked = jnp.dot(high, table, preferred_element_type=jnp.float32)
         picked = picked + jnp.dot(low, table, preferred_element_type=jnp.float32)
         trace_ref[s] = picked.reshape(count_y, fields, count_z, 2 * LANES)
-        return carry
-
-    lax.fori_loop(0, 2, one_state, 0)
+
+    for s in range(2):
+        one_state(s)
     odd_y = odd_position("gy")
     odd_z = odd_position("gz")
     end = count_y - 1
@@ -225,11 +225,11 @@
                 edge_ref[d - 1, 0, y] = rim
                 edge_ref[d - 1, 1, y] = free
 
-    def columns_part(n, carry):
+    def columns_part(n):
         base = n * width
 
         def operator(d):
-            return deriv_ref[:, pl.ds(pl.multiple_of(d * nodes + base, LANES), width)]
+            return deriv_ref[:, d * nodes + base : d * nodes + base + width]
 
         velocity = low_ref[0:3].reshape(3 * rows, nodes)
         for d in range(3):
@@ -249,7 +249,7 @@
                 inv = scale * wide_ref[2, y]
                 for tile in range(width // LANES):
                     columns = slice(tile * LANES, (tile + 1) * LANES)
-                    where = pl.ds(pl.multiple_of(base + tile * LANES, LANES), LANES)
+                    where = slice(base + tile * LANES, base + (tile + 1) * LANES)
 
                     def g(d, i):
                         return grad_ref[d, i * rows + at : i * rows + at + count_z, columns]
@@ -265,9 +265,9 @@
                         put(3 + i, common + (mu + mu) * diag[i])
                     for f, i, j in shear_pairs:
                         put(f, mu * (g(j, i) + g(i, j)))
-        return carry
-
-    lax.fori_loop(0, nodes // width, columns_part, 0)
+
+    for n in range(nodes // width):
+        columns_part(n)
 
 
 def volume(state, deriv, material, orient, flags):
@@ -334,7 +334,7 @@
     at_low = jnp.logical_and(z_pos == 0, upper)
     at_high = jnp.logical_and(z_pos == count_z - 1, jnp.logical_not(upper))
 
-    def row(y, carry):
+    def row(y):
         coefs = [coef_ref[k, y] for k in range(4)]
         edge = (edge_ref[1, 0, y], edge_ref[1, 1, y])
         source = source_ref[2, y]
@@ -356,8 +356,7 @@
             for f, term in enumerate(face_flux(jumps, 2, coefs)):
                 flux_ref[y, s, f, :, LANES:] = term
 
-        @pl.when(jnp.logical_and(y > 0, y < last_y))
-        def _():
+        if 0 < y < last_y:
             turn = source_ref[1, y]
             for s in range(2):
                 jumps = []
@@ -373,9 +372,8 @@
                 for f, term in enumerate(face_flux(jumps, 1, coefs)):
                     flux_ref[y, s, f, :, :LANES] = term
 
-        return carry
-
-    lax.fori_loop(0, count_y, row, 0)
+    for y in range(count_y):
+        row(y)
 
 
 def side_faces(traces, z_two, z_one, coef, source, edge, stored):

time: 19.9 us -> 19.9 us (level)
  waiting for transfers between devices: 1.01 us -> 2.09 us
  Pallas kernels: 8.66 us -> 7.62 us
    ppermute x1, waiting for transfers between devices: 1 us -> 1.71 us  [local(): y_two = lax.ppermute(y_two, ('gy', 'gz'), pairs)]
    pallas_call x1, Pallas kernels: 2.51 us -> 1.95 us  [volume(): pl.pallas_call(volume_kernel, out_shape=outs, in_specs=[pl.BlockSpec(memo...]
    ppermute x1, waiting for transfers between devices: 0.01 us -> 0.37 us  [local(): z_one = lax.ppermute(z_one, 'gz', swaps(nz, 0, False))]
    pallas_call x1, Pallas kernels: 0.83 us -> 0.51 us  [side_faces(): pl.pallas_call(side_kernel, out_shape=(jax.ShapeDtypeStruct((count_y, 2,...]
  transfers between devices with their start and end apart: 6 -> 6, of which waited for: 1 -> 2; matrix products, arithmetic and copies ran while one was open for 0% -> 0% of each run, Pallas kernels for 22% -> 17%
where the time goes in v8:
time: 19.9 us; the launch traced here: 19.7 us
  starting transfers between devices  9.27 us (47%)
  Pallas kernels  7.62 us (38%)
  waiting for transfers between devices  2.09 us (11%)
  between operations  0.73 us (4%)
    ppermute x1, starting transfers between devices, local(): far_in = lax.ppermute(far, 'gx', swaps(nx, 1, True))  6.1 us
    pallas_call x1, Pallas kernels, finish(): pl.pallas_call(final_kernel, out_shape=outs, in_specs=[pl.BlockSpec(memor...  2.48 us
    pallas_call x1, Pallas kernels, volume(): pl.pallas_call(volume_kernel, out_shape=outs, in_specs=[pl.BlockSpec(memo...  1.95 us
    pallas_call x1, Pallas kernels, pack_faces(): pl.pallas_call(pack_kernel, out_shape=(jax.ShapeDtypeStruct(state.shape,...  1.79 us
    ppermute x1, waiting for transfers between devices, local(): y_two = lax.ppermute(y_two, ('gy', 'gz'), pairs)  1.71 us
    ppermute x1, starting transfers between devices, local(): z_one = lax.ppermute(z_one, 'gz', swaps(nz, 0, False))  1.64 us
    ppermute x1, starting transfers between devices, local(): y_one = lax.ppermute(y_one, 'gy', swaps(ny, 0, False))  1.04 us
    pallas_call x1, Pallas kernels, extract_traces(): pl.pallas_call(trace_kernel, out_shape=(jax.ShapeDtypeStruct((2, count_y,...  0.9 us
  transfers between devices with their start and end apart: 6, of which 2 were waited for; matrix products, arithmetic and copies ran while one was open for 0% of the time, Pallas kernels for 17%

profile of v8, /device:TPU:1, one launch (start us, length us, event | category | flops | bytes accessed | tf_op | source)
XLA Modules:
  0.0 19.7 jit_solution(1987699377960626759)
XLA Ops:
  0.6 0.0 copy-start.3
  0.6 0.0 copy-start.1
  0.7 0.0 copy-start.4
  0.7 0.0 copy-start.5
  0.7 0.0 copy-start.6
  0.7 1.8 %pack_faces.1 = (f32[2,4,9,16,512]{4,3,2,1,0:T(8,128)S(1)}, f32[4,9,16,128]{3,2,1,0:T(8,128)S(1)}, f32[4,9,16,128]{3,2,1,0:T(8,128)S(1)}) custom-call(f32[2,4,9,16,512]{4,3,2,1,0:T(8,128)} %bitcast.26), custom_call_target="tpu_custom_call" | custom-call | flops 1000000 | bytes 2000000 | tf_op jit(solution)/shard_map/pack_faces/pallas_call | solution.py:76
  2.5 6.1 %collective-permute-start = (f32[4,9,16,128]{3,2,1,0:T(8,128)S(1)}, f32[4,9,16,128]{3,2,1,0:T(8,128)S(1)}, u32[]{:S(2)}, u32[]{:S(2)}) collective-permute-start(f32[4,9,16,128]{3,2,1,0:T(8,128)S(1)} %get-tuple-element.23), channel_id=1, source_target_pairs={{16,32},{32,16},{48,64},{64,48},{80,96},{96,80},{112,0},{0,112},{1... | collective-permute-start | bytes 884744 | tf_op jit(solution)/shard_map/ppermute | solution.py:543
  8.6 0.0 collective-permute-start.1
  8.6 0.0 copy-done.3
  8.6 0.9 %extract_traces.1 = (f32[2,4,9,16,256]{4,3,2,1,0:T(8,128)S(1)}, f32[9,16,128]{2,1,0:T(8,128)S(1)}, f32[9,16,128]{2,1,0:T(8,128)S(1)}, f32[2,4,9,128]{3,2,1,0:T(8,128)S(1)}, f32[2,4,9,128]{3,2,1,0:T(8,128)S(1)}) custom-call(f32[2,4,9,16,512]{4,3,2,1,0:T(8,128)S(1)} %get-tuple-element.21.state_ref, bf16[512,256]{1,0:T(8,128)(2,1)S(1)} %copy-done.3), custom_call_target="tpu_custom_call" | custom-call | flops 600000000 | bytes 4000000 | tf_op jit(solution)/shard_map/extract_traces/pallas_call | solution.py:122
  9.5 0.0 copy-start
  9.5 1.0 %collective-permute-start.3 = (f32[9,16,128]{2,1,0:T(8,128)S(1)}, f32[9,16,128]{2,1,0:T(8,128)S(1)}, u32[]{:S(2)}, u32[]{:S(2)}) collective-permute-start(f32[9,16,128]{2,1,0:T(8,128)S(1)} %get-tuple-element.27), channel_id=1, source_target_pairs={{0,4},{4,0},{8,12},{12,8},{1,5},{5,1},{9,13},{13,9},{2,6},{6,2},{1... | collective-permute-start | bytes 221192 | tf_op jit(solution)/shard_map/ppermute | solution.py:546
  10.5 0.3 %collective-permute-start.2 = (f32[9,16,128]{2,1,0:T(8,128)S(1)}, f32[9,16,128]{2,1,0:T(8,128)S(1)}, u32[]{:S(2)}, u32[]{:S(2)}) collective-permute-start(f32[9,16,128]{2,1,0:T(8,128)S(1)} %get-tuple-element.25), channel_id=1, source_target_pairs={{0,1},{1,0},{2,3},{3,2},{4,8},{5,9},{6,10},{7,11},{8,4},{9,5},{10,... | collective-permute-start | bytes 221192 | tf_op jit(solution)/shard_map/ppermute | solution.py:548
  10.8 1.6 %collective-permute-start.5 = (f32[2,4,9,128]{3,2,1,0:T(8,128)S(1)}, f32[2,4,9,128]{3,2,1,0:T(8,128)S(1)}, u32[]{:S(2)}, u32[]{:S(2)}) collective-permute-start(f32[2,4,9,128]{3,2,1,0:T(8,128)S(1)} %get-tuple-element.34), channel_id=1, source_target_pairs={{0,1},{1,0},{2,3},{3,2},{4,5},{5,4},{6,7},{7,6},{8,9},{9,8},{10,11... | collective-permute-start | bytes 110600 | tf_op jit(solution)/shard_map/ppermute | solution.py:549
  12.5 0.0 collective-permute-done.3.y_one
  12.5 0.2 collective-permute-start.4
  12.7 0.0 copy-done.1
  12.7 0.0 copy-done.4
  12.7 0.0 copy-done.5
  12.7 0.0 copy-done.6
  12.7 0.0 copy-start.2
  12.7 2.0 %volume.1 = (f32[2,4,9,16,512]{4,3,2,1,0:T(8,128)S(1)}, f32[4,4,16,128]{3,2,1,0:T(8,128)S(1)}, s32[3,4,16,128]{3,2,1,0:T(8,128)S(1)}, f32[2,2,4,16,128]{4,3,2,1,0:T(8,128)S(1)}) custom-call(f32[2,4,9,16,512]{4,3,2,1,0:T(8,128)S(1)} %get-tuple-element.21.state_ref, bf16[512,1536]{1,0:T(8,128)(2,1)S(1)} %copy-done.1, f32[3,4,16]{2,1,0:T(4,128)S(1)} %bitcast.25, ...), custom_call_target="tpu_custom_call" | custom-call | flops 1000000 | bytes 100000 | tf_op jit(solution)/shard_map/volume/pallas_call | solution.py:284
  14.7 0.4 %collective-permute-done.5.z_one = f32[2,4,9,128]{3,2,1,0:T(8,128)S(1)} collective-permute-done((f32[2,4,9,128]{3,2,1,0:T(8,128)S(1)}, f32[2,4,9,128]{3,2,1,0:T(8,128)S(1)}, u32[]{:S(2)}, u32[]{:S(2)}) %collective-permute-start.5) | collective-permute-done | bytes 36896 | tf_op jit(solution)/shard_map/ppermute | solution.py:549
  15.0 0.0 collective-permute-done.4.z_two
  15.0 0.0 copy-done
  15.0 0.5 %side_faces.1 = (bf16[4,2,9,16,256]{4,3,2,1,0:T(8,128)(2,1)S(1)}, f32[4,9,16,128]{3,2,1,0:T(8,128)S(1)}) custom-call(f32[2,4,9,16,256]{4,3,2,1,0:T(8,128)S(1)} %get-tuple-element.22.trace_ref, f32[2,4,9,128]{3,2,1,0:T(8,128)S(1)} %collective-permute-done.4.z_two, f32[2,4,9,128]{3,2,1,0:T(8,128)S(1)} %collective-permute-done.5.z_one, ...), custom_call_target="tpu_custom_call" | custom-call | flops 1000000 | bytes 100000 | tf_op jit(solution)/shard_map/side_faces/pallas_call | solution.py:381
  15.5 1.7 %collective-permute-done.2.y_two = f32[9,16,128]{2,1,0:T(8,128)S(1)} collective-permute-done((f32[9,16,128]{2,1,0:T(8,128)S(1)}, f32[9,16,128]{2,1,0:T(8,128)S(1)}, u32[]{:S(2)}, u32[]{:S(2)}) %collective-permute-start.2) | collective-permute-done | bytes 73760 | tf_op jit(solution)/shard_map/ppermute | solution.py:548
  17.2 0.0 collective-permute-done.far_ref
  17.2 0.0 collective-permute-done.1.near_ref
  17.3 0.0 copy-done.2
  17.3 2.5 %finish.1 = (f32[2,4,9,16,512]{4,3,2,1,0:T(8,128)}, f32[9,4,16]{2,1,0:T(4,128)}) custom-call(f32[2,4,9,16,512]{4,3,2,1,0:T(8,128)S(1)} %get-tuple-element.21.state_ref, f32[2,4,9,16,256]{4,3,2,1,0:T(8,128)S(1)} %get-tuple-element.22.trace_ref, f32[4,9,16,128]{3,2,1,0:T(8,128)S(1)} %collective-permute-done.far_ref, ...), custom_call_target="tpu_custom_call" | custom-call | flops 900000000 | bytes 10000000 | tf_op jit(solution)/shard_map/finish/pallas_call | solution.py:499
Async XLA Ops:
  0.6 8.0 %copy-start.3 = (bf16[512,256]{1,0:T(8,128)(2,1)S(1)}, bf16[512,256]{1,0:T(8,128)(2,1)}, u32[]{:S(2)}) copy-start(bf16[512,256]{1,0:T(8,128)(2,1)} %constant.2.clone.table_ref) | copy-start | bytes 786436
  0.6 12.0 %copy-start.1 = (bf16[512,1536]{1,0:T(8,128)(2,1)S(1)}, bf16[512,1536]{1,0:T(8,128)(2,1)}, u32[]{:S(2)}) copy-start(bf16[512,1536]{1,0:T(8,128)(2,1)} %deriv_ref.1) | copy-start | bytes 4718596
  0.7 12.0 %copy-start.4 = (s32[1,4,16,6]{2,1,3,0:T(4,128)S(1)}, s32[1,4,16,6]{2,1,3,0:T(4,128)}, u32[]{:S(2)}) copy-start(s32[1,4,16,6]{2,1,3,0:T(4,128)} %param.13) | copy-start | bytes 4612
  0.7 12.0 %copy-start.5 = (s32[1,4,16,6]{2,1,3,0:T(4,128)S(1)}, s32[1,4,16,6]{2,1,3,0:T(4,128)}, u32[]{:S(2)}) copy-start(s32[1,4,16,6]{2,1,3,0:T(4,128)} %param.14) | copy-start | bytes 4612
  0.7 12.0 %copy-start.6 = (f32[3,1,4,16]{3,2,1,0:T(4,128)S(1)}, f32[3,1,4,16]{3,2,1,0:T(4,128)}, u32[]{:S(2)}) copy-start(f32[3,1,4,16]{3,2,1,0:T(4,128)} %param.11) | copy-start | bytes 2308
  2.5 14.8 %collective-permute-start = (f32[4,9,16,128]{3,2,1,0:T(8,128)S(1)}, f32[4,9,16,128]{3,2,1,0:T(8,128)S(1)}, u32[]{:S(2)}, u32[]{:S(2)}) collective-permute-start(f32[4,9,16,128]{3,2,1,0:T(8,128)S(1)} %get-tuple-element.23), channel_id=1, source_target_pairs={{16,32},{32,16},{48,64},{64,48},{80,96},{96,80},{112,0},{0,112},{1... | collective-permute-start | bytes 884744 | tf_op jit(solution)/shard_map/ppermute | solution.py:543
  8.6 8.7 %collective-permute-start.1 = (f32[4,9,16,128]{3,2,1,0:T(8,128)S(1)}, f32[4,9,16,128]{3,2,1,0:T(8,128)S(1)}, u32[]{:S(2)}, u32[]{:S(2)}) collective-permute-start(f32[4,9,16,128]{3,2,1,0:T(8,128)S(1)} %get-tuple-element.24), channel_id=1, source_target_pairs={{0,16},{16,0},{32,48},{48,32},{64,80},{80,64},{96,112},{112,96},{1... | collective-permute-start | bytes 884744 | tf_op jit(solution)/shard_map/ppermute | solution.py:544
  9.5 5.5 %copy-start = (f32[1,4,16,9,384]{4,2,3,1,0:T(8,128)S(1)}, f32[1,4,16,9,384]{4,2,3,1,0:T(8,128)}, u32[]{:S(2)}) copy-start(f32[1,4,16,9,384]{4,2,3,1,0:T(8,128)} %param.12) | copy-start | bytes 2654212
  9.5 3.0 %collective-permute-start.3 = (f32[9,16,128]{2,1,0:T(8,128)S(1)}, f32[9,16,128]{2,1,0:T(8,128)S(1)}, u32[]{:S(2)}, u32[]{:S(2)}) collective-permute-start(f32[9,16,128]{2,1,0:T(8,128)S(1)} %get-tuple-element.27), channel_id=1, source_target_pairs={{0,4},{4,0},{8,12},{12,8},{1,5},{5,1},{9,13},{13,9},{2,6},{6,2},{1... | collective-permute-start | bytes 221192 | tf_op jit(solution)/shard_map/ppermute | solution.py:546
  10.5 6.7 %collective-permute-start.2 = (f32[9,16,128]{2,1,0:T(8,128)S(1)}, f32[9,16,128]{2,1,0:T(8,128)S(1)}, u32[]{:S(2)}, u32[]{:S(2)}) collective-permute-start(f32[9,16,128]{2,1,0:T(8,128)S(1)} %get-tuple-element.25), channel_id=1, source_target_pairs={{0,1},{1,0},{2,3},{3,2},{4,8},{5,9},{6,10},{7,11},{8,4},{9,5},{10,... | collective-permute-start | bytes 221192 | tf_op jit(solution)/shard_map/ppermute | solution.py:548
  10.8 4.2 %collective-permute-start.5 = (f32[2,4,9,128]{3,2,1,0:T(8,128)S(1)}, f32[2,4,9,128]{3,2,1,0:T(8,128)S(1)}, u32[]{:S(2)}, u32[]{:S(2)}) collective-permute-start(f32[2,4,9,128]{3,2,1,0:T(8,128)S(1)} %get-tuple-element.34), channel_id=1, source_target_pairs={{0,1},{1,0},{2,3},{3,2},{4,5},{5,4},{6,7},{7,6},{8,9},{9,8},{10,11... | collective-permute-start | bytes 110600 | tf_op jit(solution)/shard_map/ppermute | solution.py:549
  12.5 2.6 %collective-permute-start.4 = (f32[2,4,9,128]{3,2,1,0:T(8,128)S(1)}, f32[2,4,9,128]{3,2,1,0:T(8,128)S(1)}, u32[]{:S(2)}, u32[]{:S(2)}) collective-permute-start(f32[2,4,9,128]{3,2,1,0:T(8,128)S(1)} %get-tuple-element.33), channel_id=1, source_target_pairs={{0,4},{4,0},{8,12},{12,8},{1,2},{5,6},{9,10},{13,14},{2,1},{6,5},{... | collective-permute-start | bytes 110600 | tf_op jit(solution)/shard_map/ppermute | solution.py:553
  12.7 4.6 %copy-start.2 = (bf16[384,512]{1,0:T(8,128)(2,1)S(1)}, bf16[384,512]{1,0:T(8,128)(2,1)}, u32[]{:S(2)}) copy-start(bf16[384,512]{1,0:T(8,128)(2,1)} %lift_ref.1) | copy-start | bytes 1179652

commit v9 on v8

--- a/solution.py
+++ b/solution.py
@@ -58,14 +58,28 @@
 
     for t in order:
         fetch(t).start()
-    for t in order[:2]:
+    low, high = slice(0, LANES), slice((tiles - 1) * LANES, tiles * LANES)
+
+    def put(message, upper):
+        def faces(columns):
+            for y in range(message.shape[0]):
+                message[y] = merged(
+                    held_ref[0, y, :, :, columns], held_ref[1, y, :, :, columns], upper
+                )
+
+        faces(high if upper else low)
+
+    for t, upper in ((order[0], False), (order[1], True)):
         fetch(t).wait()
-    low, high = slice(0, LANES), slice((tiles - 1) * LANES, tiles * LANES)
-    for y in range(far_ref.shape[0]):
-        down = merged(held_ref[0, y, :, :, low], held_ref[1, y, :, :, low], False)
-        up = merged(held_ref[0, y, :, :, high], held_ref[1, y, :, :, high], True)
-        far_ref[y] = jnp.where(odd, up, down)
-        near_ref[y] = jnp.where(odd, down, up)
+
+        @pl.when(odd == upper)
+        def _():
+            put(far_ref, upper)
+
+        @pl.when(odd != upper)
+        def _():
+            put(near_ref, upper)
+
     for t in order[2:]:
         fetch(t).wait()
 

time: 19.9 us -> 19.9 us (level)
  no operation moved by 1% of the time
where the time goes in v9:
time: 19.9 us; the launch traced here: 19.7 us
  starting transfers between devices  9.27 us (47%)
  Pallas kernels  7.62 us (38%)
  waiting for transfers between devices  2.09 us (11%)
  between operations  0.73 us (4%)
    ppermute x1, starting transfers between devices, local(): far_in = lax.ppermute(far, 'gx', swaps(nx, 1, True))  6.1 us
    pallas_call x1, Pallas kernels, finish(): pl.pallas_call(final_kernel, out_shape=outs, in_specs=[pl.BlockSpec(memor...  2.48 us
    pallas_call x1, Pallas kernels, volume(): pl.pallas_call(volume_kernel, out_shape=outs, in_specs=[pl.BlockSpec(memo...  1.95 us
    pallas_call x1, Pallas kernels, pack_faces(): pl.pallas_call(pack_kernel, out_shape=(jax.ShapeDtypeStruct(state.shape,...  1.79 us
    ppermute x1, waiting for transfers between devices, local(): y_two = lax.ppermute(y_two, ('gy', 'gz'), pairs)  1.71 us
    ppermute x1, starting transfers between devices, local(): z_one = lax.ppermute(z_one, 'gz', swaps(nz, 0, False))  1.64 us
    ppermute x1, starting transfers between devices, local(): y_one = lax.ppermute(y_one, 'gy', swaps(ny, 0, False))  1.04 us
    pallas_call x1, Pallas kernels, extract_traces(): pl.pallas_call(trace_kernel, out_shape=(jax.ShapeDtypeStruct((2, count_y,...  0.9 us
  transfers between devices with their start and end apart: 6, of which 2 were waited for; matrix products, arithmetic and copies ran while one was open for 0% of the time, Pallas kernels for 17%

profile of v9, /device:TPU:1, one launch (start us, length us, event | category | flops | bytes accessed | tf_op | source)
XLA Modules:
  0.0 19.7 jit_solution(13682324332451948916)
XLA Ops:
  0.6 0.0 copy-start.3
  0.6 0.0 copy-start.1
  0.7 0.0 copy-start.4
  0.7 0.0 copy-start.5
  0.7 0.0 copy-start.6
  0.7 1.8 %pack_faces.1 = (f32[2,4,9,16,512]{4,3,2,1,0:T(8,128)S(1)}, f32[4,9,16,128]{3,2,1,0:T(8,128)S(1)}, f32[4,9,16,128]{3,2,1,0:T(8,128)S(1)}) custom-call(f32[2,4,9,16,512]{4,3,2,1,0:T(8,128)} %bitcast.26), custom_call_target="tpu_custom_call" | custom-call | flops 1000000 | bytes 2000000 | tf_op jit(solution)/shard_map/pack_faces/pallas_call | solution.py:90
  2.5 6.1 %collective-permute-start = (f32[4,9,16,128]{3,2,1,0:T(8,128)S(1)}, f32[4,9,16,128]{3,2,1,0:T(8,128)S(1)}, u32[]{:S(2)}, u32[]{:S(2)}) collective-permute-start(f32[4,9,16,128]{3,2,1,0:T(8,128)S(1)} %get-tuple-element.23), channel_id=1, source_target_pairs={{16,32},{32,16},{48,64},{64,48},{80,96},{96,80},{112,0},{0,112},{1... | collective-permute-start | bytes 884744 | tf_op jit(solution)/shard_map/ppermute | solution.py:557
  8.6 0.0 collective-permute-start.1
  8.6 0.0 copy-done.3
  8.6 0.9 %extract_traces.1 = (f32[2,4,9,16,256]{4,3,2,1,0:T(8,128)S(1)}, f32[9,16,128]{2,1,0:T(8,128)S(1)}, f32[9,16,128]{2,1,0:T(8,128)S(1)}, f32[2,4,9,128]{3,2,1,0:T(8,128)S(1)}, f32[2,4,9,128]{3,2,1,0:T(8,128)S(1)}) custom-call(f32[2,4,9,16,512]{4,3,2,1,0:T(8,128)S(1)} %get-tuple-element.21.state_ref, bf16[512,256]{1,0:T(8,128)(2,1)S(1)} %copy-done.3), custom_call_target="tpu_custom_call" | custom-call | flops 600000000 | bytes 4000000 | tf_op jit(solution)/shard_map/extract_traces/pallas_call | solution.py:136
  9.5 0.0 copy-start
  9.5 1.0 %collective-permute-start.3 = (f32[9,16,128]{2,1,0:T(8,128)S(1)}, f32[9,16,128]{2,1,0:T(8,128)S(1)}, u32[]{:S(2)}, u32[]{:S(2)}) collective-permute-start(f32[9,16,128]{2,1,0:T(8,128)S(1)} %get-tuple-element.27), channel_id=1, source_target_pairs={{0,4},{4,0},{8,12},{12,8},{1,5},{5,1},{9,13},{13,9},{2,6},{6,2},{1... | collective-permute-start | bytes 221192 | tf_op jit(solution)/shard_map/ppermute | solution.py:560
  10.5 0.3 %collective-permute-start.2 = (f32[9,16,128]{2,1,0:T(8,128)S(1)}, f32[9,16,128]{2,1,0:T(8,128)S(1)}, u32[]{:S(2)}, u32[]{:S(2)}) collective-permute-start(f32[9,16,128]{2,1,0:T(8,128)S(1)} %get-tuple-element.25), channel_id=1, source_target_pairs={{0,1},{1,0},{2,3},{3,2},{4,8},{5,9},{6,10},{7,11},{8,4},{9,5},{10,... | collective-permute-start | bytes 221192 | tf_op jit(solution)/shard_map/ppermute | solution.py:562
  10.8 1.6 %collective-permute-start.5 = (f32[2,4,9,128]{3,2,1,0:T(8,128)S(1)}, f32[2,4,9,128]{3,2,1,0:T(8,128)S(1)}, u32[]{:S(2)}, u32[]{:S(2)}) collective-permute-start(f32[2,4,9,128]{3,2,1,0:T(8,128)S(1)} %get-tuple-element.34), channel_id=1, source_target_pairs={{0,1},{1,0},{2,3},{3,2},{4,5},{5,4},{6,7},{7,6},{8,9},{9,8},{10,11... | collective-permute-start | bytes 110600 | tf_op jit(solution)/shard_map/ppermute | solution.py:563
  12.5 0.0 collective-permute-done.3.y_one
  12.5 0.2 collective-permute-start.4
  12.7 0.0 copy-done.1
  12.7 0.0 copy-done.4
  12.7 0.0 copy-done.5
  12.7 0.0 copy-done.6
  12.7 0.0 copy-start.2
  12.7 2.0 %volume.1 = (f32[2,4,9,16,512]{4,3,2,1,0:T(8,128)S(1)}, f32[4,4,16,128]{3,2,1,0:T(8,128)S(1)}, s32[3,4,16,128]{3,2,1,0:T(8,128)S(1)}, f32[2,2,4,16,128]{4,3,2,1,0:T(8,128)S(1)}) custom-call(f32[2,4,9,16,512]{4,3,2,1,0:T(8,128)S(1)} %get-tuple-element.21.state_ref, bf16[512,1536]{1,0:T(8,128)(2,1)S(1)} %copy-done.1, f32[3,4,16]{2,1,0:T(4,128)S(1)} %bitcast.25, ...), custom_call_target="tpu_custom_call" | custom-call | flops 1000000 | bytes 100000 | tf_op jit(solution)/shard_map/volume/pallas_call | solution.py:298
  14.7 0.4 %collective-permute-done.5.z_one = f32[2,4,9,128]{3,2,1,0:T(8,128)S(1)} collective-permute-done((f32[2,4,9,128]{3,2,1,0:T(8,128)S(1)}, f32[2,4,9,128]{3,2,1,0:T(8,128)S(1)}, u32[]{:S(2)}, u32[]{:S(2)}) %collective-permute-start.5) | collective-permute-done | bytes 36896 | tf_op jit(solution)/shard_map/ppermute | solution.py:563
  15.0 0.0 collective-permute-done.4.z_two
  15.0 0.0 copy-done
  15.0 0.5 %side_faces.1 = (bf16[4,2,9,16,256]{4,3,2,1,0:T(8,128)(2,1)S(1)}, f32[4,9,16,128]{3,2,1,0:T(8,128)S(1)}) custom-call(f32[2,4,9,16,256]{4,3,2,1,0:T(8,128)S(1)} %get-tuple-element.22.trace_ref, f32[2,4,9,128]{3,2,1,0:T(8,128)S(1)} %collective-permute-done.4.z_two, f32[2,4,9,128]{3,2,1,0:T(8,128)S(1)} %collective-permute-done.5.z_one, ...), custom_call_target="tpu_custom_call" | custom-call | flops 1000000 | bytes 100000 | tf_op jit(solution)/shard_map/side_faces/pallas_call | solution.py:395
  15.5 1.7 %collective-permute-done.2.y_two = f32[9,16,128]{2,1,0:T(8,128)S(1)} collective-permute-done((f32[9,16,128]{2,1,0:T(8,128)S(1)}, f32[9,16,128]{2,1,0:T(8,128)S(1)}, u32[]{:S(2)}, u32[]{:S(2)}) %collective-permute-start.2) | collective-permute-done | bytes 73760 | tf_op jit(solution)/shard_map/ppermute | solution.py:562
  17.2 0.0 collective-permute-done.far_ref
  17.2 0.0 collective-permute-done.1.near_ref
  17.3 0.0 copy-done.2
  17.3 2.5 %finish.1 = (f32[2,4,9,16,512]{4,3,2,1,0:T(8,128)}, f32[9,4,16]{2,1,0:T(4,128)}) custom-call(f32[2,4,9,16,512]{4,3,2,1,0:T(8,128)S(1)} %get-tuple-element.21.state_ref, f32[2,4,9,16,256]{4,3,2,1,0:T(8,128)S(1)} %get-tuple-element.22.trace_ref, f32[4,9,16,128]{3,2,1,0:T(8,128)S(1)} %collective-permute-done.far_ref, ...), custom_call_target="tpu_custom_call" | custom-call | flops 900000000 | bytes 10000000 | tf_op jit(solution)/shard_map/finish/pallas_call | solution.py:513
Async XLA Ops:
  0.6 8.0 %copy-start.3 = (bf16[512,256]{1,0:T(8,128)(2,1)S(1)}, bf16[512,256]{1,0:T(8,128)(2,1)}, u32[]{:S(2)}) copy-start(bf16[512,256]{1,0:T(8,128)(2,1)} %constant.2.clone.table_ref) | copy-start | bytes 786436
  0.6 12.0 %copy-start.1 = (bf16[512,1536]{1,0:T(8,128)(2,1)S(1)}, bf16[512,1536]{1,0:T(8,128)(2,1)}, u32[]{:S(2)}) copy-start(bf16[512,1536]{1,0:T(8,128)(2,1)} %deriv_ref.1) | copy-start | bytes 4718596
  0.7 12.0 %copy-start.4 = (s32[1,4,16,6]{2,1,3,0:T(4,128)S(1)}, s32[1,4,16,6]{2,1,3,0:T(4,128)}, u32[]{:S(2)}) copy-start(s32[1,4,16,6]{2,1,3,0:T(4,128)} %param.13) | copy-start | bytes 4612
  0.7 12.0 %copy-start.5 = (s32[1,4,16,6]{2,1,3,0:T(4,128)S(1)}, s32[1,4,16,6]{2,1,3,0:T(4,128)}, u32[]{:S(2)}) copy-start(s32[1,4,16,6]{2,1,3,0:T(4,128)} %param.14) | copy-start | bytes 4612
  0.7 12.0 %copy-start.6 = (f32[3,1,4,16]{3,2,1,0:T(4,128)S(1)}, f32[3,1,4,16]{3,2,1,0:T(4,128)}, u32[]{:S(2)}) copy-start(f32[3,1,4,16]{3,2,1,0:T(4,128)} %param.11) | copy-start | bytes 2308
  2.5 14.8 %collective-permute-start = (f32[4,9,16,128]{3,2,1,0:T(8,128)S(1)}, f32[4,9,16,128]{3,2,1,0:T(8,128)S(1)}, u32[]{:S(2)}, u32[]{:S(2)}) collective-permute-start(f32[4,9,16,128]{3,2,1,0:T(8,128)S(1)} %get-tuple-element.23), channel_id=1, source_target_pairs={{16,32},{32,16},{48,64},{64,48},{80,96},{96,80},{112,0},{0,112},{1... | collective-permute-start | bytes 884744 | tf_op jit(solution)/shard_map/ppermute | solution.py:557
  8.6 8.7 %collective-permute-start.1 = (f32[4,9,16,128]{3,2,1,0:T(8,128)S(1)}, f32[4,9,16,128]{3,2,1,0:T(8,128)S(1)}, u32[]{:S(2)}, u32[]{:S(2)}) collective-permute-start(f32[4,9,16,128]{3,2,1,0:T(8,128)S(1)} %get-tuple-element.24), channel_id=1, source_target_pairs={{0,16},{16,0},{32,48},{48,32},{64,80},{80,64},{96,112},{112,96},{1... | collective-permute-start | bytes 884744 | tf_op jit(solution)/shard_map/ppermute | solution.py:558
  9.5 5.5 %copy-start = (f32[1,4,16,9,384]{4,2,3,1,0:T(8,128)S(1)}, f32[1,4,16,9,384]{4,2,3,1,0:T(8,128)}, u32[]{:S(2)}) copy-start(f32[1,4,16,9,384]{4,2,3,1,0:T(8,128)} %param.12) | copy-start | bytes 2654212
  9.5 3.0 %collective-permute-start.3 = (f32[9,16,128]{2,1,0:T(8,128)S(1)}, f32[9,16,128]{2,1,0:T(8,128)S(1)}, u32[]{:S(2)}, u32[]{:S(2)}) collective-permute-start(f32[9,16,128]{2,1,0:T(8,128)S(1)} %get-tuple-element.27), channel_id=1, source_target_pairs={{0,4},{4,0},{8,12},{12,8},{1,5},{5,1},{9,13},{13,9},{2,6},{6,2},{1... | collective-permute-start | bytes 221192 | tf_op jit(solution)/shard_map/ppermute | solution.py:560
  10.5 6.7 %collective-permute-start.2 = (f32[9,16,128]{2,1,0:T(8,128)S(1)}, f32[9,16,128]{2,1,0:T(8,128)S(1)}, u32[]{:S(2)}, u32[]{:S(2)}) collective-permute-start(f32[9,16,128]{2,1,0:T(8,128)S(1)} %get-tuple-element.25), channel_id=1, source_target_pairs={{0,1},{1,0},{2,3},{3,2},{4,8},{5,9},{6,10},{7,11},{8,4},{9,5},{10,... | collective-permute-start | bytes 221192 | tf_op jit(solution)/shard_map/ppermute | solution.py:562
  10.8 4.2 %collective-permute-start.5 = (f32[2,4,9,128]{3,2,1,0:T(8,128)S(1)}, f32[2,4,9,128]{3,2,1,0:T(8,128)S(1)}, u32[]{:S(2)}, u32[]{:S(2)}) collective-permute-start(f32[2,4,9,128]{3,2,1,0:T(8,128)S(1)} %get-tuple-element.34), channel_id=1, source_target_pairs={{0,1},{1,0},{2,3},{3,2},{4,5},{5,4},{6,7},{7,6},{8,9},{9,8},{10,11... | collective-permute-start | bytes 110600 | tf_op jit(solution)/shard_map/ppermute | solution.py:563
  12.5 2.6 %collective-permute-start.4 = (f32[2,4,9,128]{3,2,1,0:T(8,128)S(1)}, f32[2,4,9,128]{3,2,1,0:T(8,128)S(1)}, u32[]{:S(2)}, u32[]{:S(2)}) collective-permute-start(f32[2,4,9,128]{3,2,1,0:T(8,128)S(1)} %get-tuple-element.33), channel_id=1, source_target_pairs={{0,4},{4,0},{8,12},{12,8},{1,2},{5,6},{9,10},{13,14},{2,1},{6,5},{... | collective-permute-start | bytes 110600 | tf_op jit(solution)/shard_map/ppermute | solution.py:567
  12.7 4.6 %copy-start.2 = (bf16[384,512]{1,0:T(8,128)(2,1)S(1)}, bf16[384,512]{1,0:T(8,128)(2,1)}, u32[]{:S(2)}) copy-start(bf16[384,512]{1,0:T(8,128)(2,1)} %lift_ref.1) | copy-start | bytes 1179652
